TPU v7x, 256 devices: a whole 4x4x8 slice. The times are simulated.
256 devices in a mesh: seq: 32 (over x, z), dp: 8 (over y, core).
Axes of the slice: x: 4, y: 4, z: 8, core: 2. Of those that a mesh axis runs over, the one named last changes fastest.
Arguments:
- layer_input: bfloat16 [8, 4096, 4096], P('dp', 'seq'), may hold values from -6 to 6
- projection: bfloat16 [4096, 256], replicated, may hold values from -0.09375 to 0.09375
- ssm_input: bfloat16 [8, 4096, 4096], P('dp', 'seq'), may hold values from -6 to 6
- step_logit: float32 [8, 4096, 64], P('dp', 'seq'), may hold values from -4 to 4
- decay_rate: float32 [64], replicated, may hold values from 0.00012207031 to 0.1
- output_grad: bfloat16 [8, 4096, 4096], P('dp', 'seq'), may hold values from -6 to 6
Outputs:
- input_grad: bfloat16 [8, 4096, 4096], P('dp', 'seq')
- step_grad: float32 [8, 4096, 64], P('dp', 'seq')
- rate_grad: float32 [64], replicated
- projection_grad: float32 [4096, 256], P('seq')
All inputs are finite; a program needn't handle non-finite values.
Results may differ from a plain program's by a relative error of at most 0.011.
Values sent between devices are 32-bit elements; how exact they have to be, the bound alone decides.
No kernel may reach another device: no remote copies, remote signals or barrier semaphores. Data moves between devices by JAX's collectives and lax.ppermute only.
A program may use at most 320 MiB of HBM per device.

v0:
```python
import jax
import jax.numpy as jnp
from jax import lax
from jax.sharding import PartitionSpec as P


def carried_in(value, axis, join, neutral, backward):
    count, mine = (lax.axis_size(axis), lax.axis_index(axis))
    pieces = jax.tree.map(lambda part: lax.all_gather(part, axis), value)
    if backward:
        pieces = jax.tree.map(lambda part: part[::-1], pieces)
        mine = count - 1 - mine
    subtotal = jax.tree.map(
        lambda part, zero: jnp.full_like(part, 0) + jnp.asarray(zero, part.dtype), value, neutral
    )

    def lap(position, subtotal):
        longer = join(subtotal, jax.tree.map(lambda part: part[position], pieces))
        return jax.tree.map(lambda new, old: jnp.where(position < mine, new, old), longer, subtotal)

    return lax.fori_loop(0, count - 1, lap, subtotal)


def span_forward(ssm_block, b_block, c_block, logit_block, decay_rate, carry_in):
    row_count = ssm_block.shape[0]
    head_count = logit_block.shape[1]
    values = ssm_block.astype(jnp.float32).reshape(row_count, head_count, -1)
    b_vals = b_block.astype(jnp.float32)
    c_vals = c_block.astype(jnp.float32)
    dt_soft = jax.nn.softplus(logit_block)
    log_decay = jnp.cumsum(-decay_rate[None, :] * dt_soft, axis=0)
    causal = (
        lax.broadcasted_iota(jnp.int32, (row_count, row_count), 0)
        >= lax.broadcasted_iota(jnp.int32, (row_count, row_count), 1)
    )[None, :, :]
    decay_heads = log_decay.T
    gap_log = decay_heads[:, :, None] - decay_heads[:, None, :]
    decays = jnp.exp(jnp.where(causal, gap_log, -jnp.inf))
    scores = jnp.einsum("tn,sn->ts", c_vals, b_vals, precision=lax.Precision.HIGHEST)
    weights = decays * scores[None, :, :] * dt_soft.T[:, None, :]
    inner = jnp.einsum("hts,shp->thp", weights, values, precision=lax.Precision.HIGHEST)
    outer = jnp.exp(log_decay)[:, :, None] * jnp.einsum(
        "tn,hpn->thp", c_vals, carry_in, precision=lax.Precision.HIGHEST
    )
    to_end = jnp.exp(log_decay[-1][None, :] - log_decay) * dt_soft
    carry_out = jnp.exp(log_decay[-1])[:, None, None] * carry_in + jnp.einsum(
        "sh,shp,sn->hpn", to_end, values, b_vals, precision=lax.Precision.HIGHEST
    )
    return (inner + outer, carry_out)


def affine_combine(earlier, later):
    return (earlier[0] * later[0], later[0][:, None, None] * earlier[1] + later[1])


def shards(layer_input, projection, ssm_input, step_logit, decay_rate, output_grad):
    tokens = layer_input[0]
    x_rows = ssm_input[0]
    logit_rows = step_logit[0]
    grad_rows = output_grad[0]
    row_count = x_rows.shape[0]
    head_count = logit_rows.shape[1]
    head_size = x_rows.shape[1] // head_count
    state_size = projection.shape[1] // 2
    projected = jnp.dot(tokens, projection, preferred_element_type=jnp.float32).astype(jnp.bfloat16)
    b_rows = projected[:, :state_size]
    c_rows = projected[:, state_size:]
    values = x_rows.astype(jnp.float32).reshape(row_count, head_count, head_size)
    dt_soft = jax.nn.softplus(logit_rows)
    log_decay = jnp.cumsum(-decay_rate[None, :] * dt_soft, axis=0)
    span_decay = jnp.exp(log_decay[-1])
    to_end = jnp.exp(log_decay[-1][None, :] - log_decay) * dt_soft
    local_state = jnp.einsum(
        "sh,shp,sn->hpn",
        to_end,
        values,
        b_rows.astype(jnp.float32),
        precision=lax.Precision.HIGHEST,
    )
    identity = (
        jnp.ones((head_count,), jnp.float32),
        jnp.zeros((head_count, head_size, state_size), jnp.float32),
    )
    entering = carried_in((span_decay, local_state), "seq", affine_combine, identity, False)[1]
    grad_vals = grad_rows.astype(jnp.float32).reshape(row_count, head_count, head_size)
    local_adjoint = jnp.einsum(
        "th,thp,tn->hpn",
        jnp.exp(log_decay),
        grad_vals,
        c_rows.astype(jnp.float32),
        precision=lax.Precision.HIGHEST,
    )
    leaving = carried_in((span_decay, local_adjoint), "seq", affine_combine, identity, True)[1]

    def forward_at(x_arg, b_arg, c_arg, logit_arg, rate_arg):
        return span_forward(x_arg, b_arg, c_arg, logit_arg, rate_arg, entering)

    unused, pullback = jax.vjp(forward_at, x_rows, b_rows, c_rows, logit_rows, decay_rate)
    grad_x, grad_b, grad_c, grad_logit, grad_rate = pullback((grad_vals, leaving))
    grad_bc = jnp.concatenate([grad_b, grad_c], axis=1)
    block_rows = projection.shape[0] // lax.axis_size("seq")
    grad_w = lax.dot_general(
        tokens, grad_bc, (((0,), (0,)), ((), ())), preferred_element_type=jnp.float32
    )
    summed, rate_sum = lax.psum((grad_w, grad_rate), ("seq", "dp"))
    weight_rows = lax.dynamic_slice_in_dim(
        summed, lax.axis_index("seq") * block_rows, block_rows, 0
    )
    return (grad_x[None], grad_logit[None], rate_sum, weight_rows)


def solution(mesh):
    placed = (
        P("dp", "seq", None),
        P(),
        P("dp", "seq", None),
        P("dp", "seq", None),
        P(),
        P("dp", "seq", None),
    )
    return jax.shard_map(
        shards,
        mesh=mesh,
        in_specs=placed,
        out_specs=(P("dp", "seq", None), P("dp", "seq", None), P(), P("seq", None)),
        check_vma=False,
    )
```

profile of v0, /device:TPU:1, one launch (start us, length us, event | category | flops | bytes accessed | tf_op | source)
XLA Modules:
  0.0 1467.6 jit_solution(1567927609858886739)
XLA Ops:
  15.3 36.1 %all-gather.2 = f32[32,1,64]{2,1,0:T(1,128)S(1)} all-gather(f32[1,1,64]{2,1,0:T(1,128)S(1)} %bitcast.129), channel_id=1, replica_groups=mesh['seq'=32,'dp'=8] {'seq'}, dimensions={0}, use_global_device_ids=true | all-gather | bytes 8448 | tf_op jit(solution)/shard_map/all_gather | solution.py:9
  53.8 396.3 %all-gather.6.cloned.1.call-done = f32[2048,64,128]{2,1,0:T(8,128)} async-done(((f32[64,64,128]{2,1,0:T(8,128)}), f32[2048,64,128]{2,1,0:T(8,128)}) %all-gather.6.cloned.1.call-update) | async-done | bytes 67108880 | tf_op jit(solution)/shard_map/all_gather | solution.py:9
  450.0 43.5 %rev.7 = f32[32,64,64,128]{3,2,1,0:T(8,128)} reverse(f32[32,64,64,128]{3,2,1,0:T(8,128)} %bitcast.6), dimensions={0} | reverse | bytes 134217728 | tf_op jit(solution)/shard_map/rev | solution.py:11
  493.6 120.6 %while.28 = (s32[]{:T(128)}, f32[64,64,128]{2,1,0:T(8,128)}, s32[]{:T(128)}, f32[32,64]{1,0:T(8,128)S(1)}, f32[32,64,64,128]{3,2,1,0:T(8,128)}, /*index=5*/s32[]{:T(128)}, s32[]{:T(128)}) while((s32[]{:T(128)}, f32[64,64,128]{2,1,0:T(8,128)}, s32[]{:T(128)}, f32[32,64]{1,0:T(8,128)S(1)}, f32[32,64,64,128]{3,2,1,0:T(8,128)}, ...), condition=%wide.region_2.3_spmd.clone, body=%wide.region_1.2_spmd.clone.sunk | while | flops 2097156 | bytes 6292329 | solution.py:21
  496.9 3.9 fusion.78
  500.8 3.9 fusion.78
  504.7 3.9 fusion.78
  508.6 3.9 fusion.78
  512.5 3.9 fusion.78
  520.3 3.9 fusion.78
  539.9 3.9 fusion.78
  551.6 3.9 fusion.78
  571.1 3.9 fusion.78
  582.9 3.9 fusion.78
  594.6 3.9 fusion.78
  614.1 4.4 fusion.13
  622.7 5.5 fusion.23
  628.3 4.8 fusion.11
  633.3 417.1 %all-gather.8.cloned.1.call-done = f32[2048,64,128]{2,1,0:T(8,128)} async-done(((f32[64,64,128]{2,1,0:T(8,128)}), f32[2048,64,128]{2,1,0:T(8,128)}) %all-gather.8.cloned.1.call-update) | async-done | bytes 67108880 | tf_op jit(solution)/shard_map/all_gather | solution.py:9
  1050.4 136.0 %while.29 = (s32[]{:T(128)}, f32[64,64,128]{2,1,0:T(8,128)}, s32[]{:T(128)}, f32[32,64]{1,0:T(8,128)S(1)}, f32[32,64,64,128]{3,2,1,0:T(8,128)}, /*index=5*/s32[]{:T(128)}, s32[]{:T(128)}) while((s32[]{:T(128)}, f32[64,64,128]{2,1,0:T(8,128)}, s32[]{:T(128)}, f32[32,64]{1,0:T(8,128)S(1)}, f32[32,64,64,128]{3,2,1,0:T(8,128)}, ...), condition=%wide.region_5.6_spmd.clone, body=%wide.region_4.5_spmd.clone.sunk | while | flops 2097156 | bytes 6292329 | solution.py:21
  1186.4 5.2 fusion.24
  1195.4 5.6 fusion.14
  1211.3 75.5 %psum.14 = f32[64]{0:T(128)} all-reduce(f32[64]{0:T(128)S(1)} %neg.27), channel_id=1, replica_groups=mesh['seq'=32,'dp'=8] {'seq','dp'}, use_global_device_ids=true, to_apply=%region_13.14 | all-reduce | flops 64 | bytes 512 | tf_op jit(solution)/shard_map/psum | solution.py:105
  1286.8 172.5 %all-reduce.4.cloned.1.call-done = f32[4096,256]{0,1:T(8,128)} async-done(((f32[4096,256]{0,1:T(8,128)}), f32[4096,256]{0,1:T(8,128)}) %all-reduce.4.cloned.1.call-update) | async-done | bytes 4194320 | tf_op jit(solution)/shard_map/psum | solution.py:105
  (193 shorter events, 243.9 us)
Async XLA Ops:
  7.2 3.7 copy-start
  7.2 442.8 %all-gather.6.cloned.1.call-start = ((), (), s32[]{:S(2)}) async-start(), calls=%async_computation.1 | async-start | bytes 69206016 | tf_op jit(solution)/shard_map/all_gather | solution.py:9
  8.0 1.2 copy-start.16
  15.1 1035.3 %all-gather.8.cloned.1.call-start = ((), (), s32[]{:S(2)}) async-start(), calls=%async_computation.2 | async-start | bytes 69206016 | tf_op jit(solution)/shard_map/all_gather | solution.py:9
  15.3 603.2 %copy-start.14 = (f32[64]{0:T(128)}, f32[64]{0:T(128)S(1)}, u32[]{:S(2)}) copy-start(f32[64]{0:T(128)S(1)} %get-tuple-element.250) | copy-start | bytes 772
  614.1 4.4 copy-start.4
  614.1 5.1 copy-start.1
  619.2 9.0 copy-start.5
  621.8 837.6 %all-reduce.4.cloned.1.call-start = ((), (), s32[]{:S(2)}) async-start(), calls=%async_computation | async-start | bytes 8388608 | tf_op jit(solution)/shard_map/psum | solution.py:105
  622.5 5.7 copy-start.2
  622.5 5.7 copy-start.9
  622.6 10.5 copy-start.12
  1186.4 5.5 copy-start.3
  1194.6 0.7 copy-start.18
  1194.6 0.8 copy-start.6
  1194.6 0.8 copy-start.10
  1194.6 0.8 copy-start.13
  1206.1 3.0 copy-start.7
  1206.1 3.0 copy-start.8
  1206.1 3.0 copy-start.15
  1206.1 4.4 copy-start.11
  1206.1 4.4 copy-start.17
Sparse Core Ops, SparseCore 0:
  15.2 434.7 all-gather.5
  621.9 428.4 all-gather.7
  1194.7 264.5 all-reduce.3
where the time goes:
time: 1470 us
  waiting for transfers between devices  986 us (67%)
  other arithmetic  248 us (17%)
  blocking collectives  112 us (8%)
  local copies, waits for them, and re-layouts  69.7 us (5%)
  matrix products  38.2 us (3%)
    all_gather x2, waiting for transfers between devices, carried_in(): pieces = jax.tree.map(lambda part: lax.all_gather(part, axis), value)  813 us
    select_n x62, other arithmetic, lap(): jnp.where(position < mine, new, old)  240 us
    psum x1, waiting for transfers between devices, shards(): summed, rate_sum = lax.psum((grad_w, grad_rate), ('seq', 'dp'))  173 us
    psum x1, blocking collectives, shards(): summed, rate_sum = lax.psum((grad_w, grad_rate), ('seq', 'dp'))  75.5 us
    rev x2, local copies, waits for them, and re-layouts, carried_in(): pieces = jax.tree.map(lambda part: part[::-1], pieces)  43.6 us
    all_gather x1, blocking collectives, carried_in(): pieces = jax.tree.map(lambda part: lax.all_gather(part, axis), value)  36.1 us
  transfers between devices with their start and end apart: 3, of which 3 were waited for; matrix products, arithmetic and copies ran while one was open for 2% of the time, Pallas kernels for 0%

commit v1 on v0

v1 whole, which is shorter than its diff:
```python
import jax
import jax.numpy as jnp
from jax import lax
from jax.experimental import pallas as pl
from jax.experimental.pallas import tpu as pltpu
from jax.sharding import Mesh
from jax.sharding import PartitionSpec as P

ROWS = 128
HEADS = 64
HALF = 32
PAIRS = 16
TILE = PAIRS * 128
GROUP = 8
GROUPS = HEADS // GROUP
BF = jnp.bfloat16
F32 = jnp.float32
NN = (((1,), (0,)), ((), ()))
NT = (((1,), (1,)), ((), ()))
TN = (((0,), (0,)), ((), ()))
HIGH = lax.Precision.HIGHEST
VMEM = pl.BlockSpec(memory_space=pltpu.VMEM)
SMEM = pl.BlockSpec(memory_space=pltpu.SMEM)
SEQ = ("blk", "par")


def iota(shape, dim):
    return lax.broadcasted_iota(jnp.int32, shape, dim)


def dot(a, b, dims=NN):
    return lax.dot_general(a, b, dims, preferred_element_type=F32)


def dot_exact(a, b):
    return lax.dot_general(a, b, NN, precision=HIGH, preferred_element_type=F32)


def dot_split(a, b):
    head = a.astype(BF)
    tail = (a - head.astype(F32)).astype(BF)
    return dot(head, b) + dot(tail, b)


def spread(cols, pair, left):
    one = cols[:, 2 * pair : 2 * pair + 1]
    two = cols[:, 2 * pair + 1 : 2 * pair + 2]
    return jnp.where(left, one, two)


def turned(values, odd):
    other = jnp.concatenate([values[:, HALF:], values[:, :HALF]], axis=1)
    return jnp.where(odd == 0, values, other)


def lanes(pair, odd):
    half, place = divmod(pair, PAIRS)
    start = (odd if half == 0 else 1 - odd) * TILE + 128 * place
    return pl.ds(pl.multiple_of(start, 128), 128)


def call(kernel, outs, flops, moved, **more):
    return pl.pallas_call(
        kernel,
        out_shape=outs,
        compiler_params=pltpu.CompilerParams(vmem_limit_bytes=48 << 20),
        cost_estimate=pl.CostEstimate(flops=flops, bytes_accessed=moved, transcendentals=0),
        **more,
    )


def shape(*dims, dtype=F32):
    return jax.ShapeDtypeStruct(dims, dtype)


def turn_kernel(tok, out):
    for i in range(32):
        part = tok[:, 128 * i : 128 * i + 128].astype(F32).T
        for d in range(8):
            out[d, i] = part[16 * d : 16 * d + 16, :]


def project_kernel(
    odd_ref, tok, proj, x, logit, rate, bc_ref, c_ref, dt_ref, cg_ref, dtg_ref, ct_ref, rows_ref, keep, send
):
    odd = odd_ref[0]
    bc = dot(tok[...], proj[...]).astype(BF)
    bc_ref[...] = bc
    z = turned(logit[...], odd)
    dt = jnp.maximum(z, 0.0) + jnp.log1p(jnp.exp(-jnp.abs(z)))
    a = -turned(rate[...], odd) * dt
    lower = (iota((ROWS, ROWS), 0) >= iota((ROWS, ROWS), 1)).astype(F32)
    c = dot_exact(lower, a)
    c_ref[...] = c
    dt_ref[...] = dt
    ct_ref[...] = c.T
    for group in range(GROUPS):
        cg_ref[group] = c[:, GROUP * group : GROUP * group + GROUP]
        dtg_ref[group] = dt[:, GROUP * group : GROUP * group + GROUP]
    last = c[ROWS - 1 : ROWS, :]
    to_end = jnp.exp(last - c) * dt
    b_t = bc[:, :128].astype(F32).T.astype(BF)
    left = iota((ROWS, 128), 1) < 64
    left1 = iota((1, 128), 1) < 64
    for half, out in ((1, send), (0, keep)):
        for place in range(PAIRS):
            pair = half * PAIRS + place
            xw = x[:, lanes(pair, odd)].astype(F32) * spread(to_end, pair, left)
            out[128 * place : 128 * place + 128, :] = dot(b_t, xw.astype(BF))
            rows_ref[pair : pair + 1, :] = spread(last, pair, left1)
    send[TILE : TILE + PAIRS, :] = rows_ref[PAIRS : 2 * PAIRS, :]


def adjoint_kernel(odd_ref, bc, c_ref, rows, g, keep, send):
    odd = odd_ref[0]
    ec = jnp.exp(c_ref[...])
    c_t = bc[:, 128:].astype(F32).T.astype(BF)
    left = iota((ROWS, 128), 1) < 64
    for half, out in ((1, send), (0, keep)):
        for place in range(PAIRS):
            pair = half * PAIRS + place
            gw = g[:, lanes(pair, odd)].astype(F32) * spread(ec, pair, left)
            out[128 * place : 128 * place + 128, :] = dot(c_t, gw.astype(BF))
    send[TILE : TILE + PAIRS, :] = rows[PAIRS : 2 * PAIRS, :]


def intra_kernel(odd_ref, bc, cg, dtg, ct, x, g, u_ref, t_ref, s_ref, ds_ref):
    @pl.when(pl.program_id(0) == 0)
    def _():
        ds_ref[...] = jnp.zeros_like(ds_ref)

    sc_t = dot(bc[:, :128], bc[:, 128:], NT)
    causal = iota((ROWS, ROWS), 0) <= iota((ROWS, ROWS), 1)
    left = iota((ROWS, 128), 1) < 64
    ones = (left.astype(F32).astype(BF), (1.0 - left.astype(F32)).astype(BF))
    lane8 = iota((ROWS, GROUP), 1)
    s_all = jnp.zeros((ROWS, GROUP), F32)
    total = ds_ref[...]
    for pair in range(GROUP // 2):
        xs = x[:, 128 * pair : 128 * pair + 128]
        gs = g[:, 128 * pair : 128 * pair + 128]
        parts = []
        for side in range(2):
            h = 2 * pair + side
            gx = dot(xs * ones[side], gs, NT)
            gap = ct[h : h + 1, :] - cg[0, :, h : h + 1]
            decay = jnp.exp(jnp.where(causal, gap, -jnp.inf))
            parts.append(dot((decay * sc_t).astype(BF), gs))
            p = decay * gx * dtg[0, :, h : h + 1]
            total = total + p
            m = p * sc_t
            t_ref[h : h + 1, :] = jnp.sum(m, axis=0, keepdims=True)
            s_all = jnp.where(lane8 == h, jnp.sum(m, axis=1, keepdims=True), s_all)
        u_ref[:, 128 * pair : 128 * pair + 128] = jnp.where(left, parts[0], parts[1])
    s_ref[0] = s_all
    ds_ref[...] = total


def combine_kernel(rows, keep_s, keep_a, got_s, got_a, msg):
    for place in range(PAIRS):
        at = pl.ds(128 * place, 128)
        own = rows[place : place + 1, :]
        decay = jnp.exp(own)
        msg[place, 0:128, :] = decay * got_s[at, :] + keep_s[at, :]
        msg[place, 128:256, :] = decay * got_a[at, :] + keep_a[at, :]
        msg[place, 256:257, :] = own + got_s[TILE + place : TILE + place + 1, :]
        msg[place, 257:258, :] = own + got_a[TILE + place : TILE + place + 1, :]
        msg[place, 258:264, :] = jnp.zeros((6, 128), F32)


def scan_kernel(msg, out):
    state = jnp.zeros((128, 128), F32)
    for i in range(PAIRS):
        out[i, 0:128, :] = state
        state = jnp.exp(msg[i, 256:257, :]) * state + msg[i, 0:128, :]
    state = jnp.zeros((128, 128), F32)
    for i in range(PAIRS - 1, -1, -1):
        out[i, 128:256, :] = state
        state = jnp.exp(msg[i, 257:258, :]) * state + msg[i, 128:256, :]


def unfold_kernel(rows, keep_s, keep_a, got_s, got_a, back, s_own, a_own, s_next, a_next):
    for place in range(PAIRS):
        at = pl.ds(128 * place, 128)
        decay = jnp.exp(rows[place : place + 1, :])
        near_s = jnp.exp(got_s[TILE + place : TILE + place + 1, :])
        near_a = jnp.exp(got_a[TILE + place : TILE + place + 1, :])
        state = near_s * back[place, 0:128, :] + got_s[at, :]
        s_own[at, :] = state
        s_next[at, :] = decay * state + keep_s[at, :]
        adj = near_a * back[place, 128:256, :] + got_a[at, :]
        a_own[at, :] = adj
        a_next[at, :] = decay * adj + keep_a[at, :]


def outer_terms(half, odd, s_in, a_in, x, g, u, c_ref, dt_ref, bc, dots, store):
    cols = slice(HALF * half, HALF * half + HALF)
    c = c_ref[:, cols]
    dt = dt_ref[:, cols]
    last = c[ROWS - 1 : ROWS, :]
    end = jnp.exp(last - c)
    ec = jnp.exp(c)
    b_bf, c_bf = bc[:, :128], bc[:, 128:]
    left = iota((ROWS, 128), 1) < 64
    choice = iota((ROWS, HALF), 1) - (iota((ROWS, HALF), 0) >= 64).astype(jnp.int32)
    role = jnp.zeros((ROWS, HALF), F32)
    outer = jnp.zeros((ROWS, HALF), F32)
    grad_b = jnp.zeros((ROWS, 128), F32)
    grad_c = jnp.zeros((ROWS, 128), F32)
    for place in range(PAIRS):
        at = lanes(half * PAIRS + place, odd)
        rows = pl.ds(128 * place, 128)
        picked = (choice == 2 * place).astype(F32).astype(BF)
        state = s_in[rows, :]
        adj = a_in[rows, :]
        dots[place : place + 1, :] = jnp.sum(adj * state, axis=0, keepdims=True)
        adj = adj.astype(BF)
        state = state.astype(BF)
        gw = g[:, at].astype(F32) * spread(ec, place, left)
        role = role + dot_split(gw * dot(c_bf, state), picked)
        grad_c = grad_c + dot(gw.astype(BF), state, NT)
        wide = spread(end, place, left)
        wide_dt = spread(dt, place, left)
        add = dot(b_bf, adj) * wide
        xs = x[:, at].astype(F32)
        store(place, ((u[:, at] + add) * wide_dt).astype(BF))
        outer = outer + dot_split(xs * add, picked)
        grad_b = grad_b + dot((xs * (wide * wide_dt)).astype(BF), adj, NT)
    row, col = iota((128, HALF), 0), iota((128, HALF), 1)
    side = ((row >= 64).astype(jnp.int32) == col % 2).astype(F32)
    both = dot_exact(dots[...], side)
    mine = iota((PAIRS, HALF), 0) == iota((PAIRS, HALF), 1) // 2
    meet = jnp.exp(last) * jnp.sum(jnp.where(mine, both, 0.0), axis=0, keepdims=True)
    return role, outer, meet, grad_b, grad_c


def outer_kernel(
    odd_ref, s_in, a_in, x, g, u, c_ref, dt_ref, bc, ds, gx_ref, role_ref, outer_ref, meet_ref, gb_ref, gc_ref, dots
):
    def store(place, value):
        gx_ref[:, 128 * place : 128 * place + 128] = value

    role, outer, meet, grad_b, grad_c = outer_terms(
        0, odd_ref[0], s_in, a_in, x, g, u, c_ref, dt_ref, bc, dots, store
    )
    role_ref[...] = role
    outer_ref[...] = outer
    meet_ref[...] = jnp.broadcast_to(meet, (8, HALF))
    inner = ds[...].astype(BF)
    gb_ref[...] = grad_b + dot(inner, bc[:, 128:])
    gc_ref[...] = grad_c + dot(inner, bc[:, :128], TN)


def finish_kernel(
    odd_ref, s_in, a_in, x, g, u, c_ref, dt_ref, bc, gx_own, role_own, outer_own, meet_own, gb_own, gc_own,
    t_rows, s_cols, logit, rate, gx_ref, step_ref, msg, dots,
):
    odd = odd_ref[0]

    def store(place, value):
        gx_ref[:, lanes(PAIRS + place, odd)] = value

    role, outer, meet, grad_b, grad_c = outer_terms(
        1, odd, s_in, a_in, x, g, u, c_ref, dt_ref, bc, dots, store
    )
    for place in range(PAIRS):
        gx_ref[:, lanes(place, odd)] = gx_own[:, 128 * place : 128 * place + 128]
    msg[0:128, 0:128] = (gb_own[...] + grad_b).astype(BF).astype(F32)
    msg[0:128, 128:256] = (gc_own[...] + grad_c).astype(BF).astype(F32)
    dt = dt_ref[...]
    role_t = jnp.concatenate([role_own[...], role], axis=1) + t_rows[...].T
    outer = jnp.concatenate([outer_own[...], outer], axis=1)
    meet = jnp.concatenate([meet_own[0:1, :], meet], axis=1)
    role_s = jnp.concatenate([s_cols[k] for k in range(GROUPS)], axis=1)
    row, col = iota((ROWS, ROWS), 0), iota((ROWS, ROWS), 1)
    later = (col >= row).astype(F32)
    before = (col < row).astype(F32)
    da = dot_exact(later, role_t - role_s) + dot_exact(before, outer * dt) + meet
    ddt = turned(role_s / dt + outer, odd) - rate[...] * turned(da, odd)
    step_ref[...] = ddt / (1.0 + jnp.exp(-logit[...]))
    rate_row = turned(-jnp.sum(dt * da, axis=0, keepdims=True), odd)
    wide = jnp.concatenate([rate_row, jnp.zeros((1, 256 - HEADS), F32)], axis=1)
    msg[128:136, :] = jnp.broadcast_to(wide, (8, 256))


def weight_kernel(tok, got, msg):
    total = jnp.zeros((512, 256), F32)
    rates = jnp.zeros((8, 256), F32)
    for d in range(8):
        total = total + dot(tok[d].astype(BF), got[d, 0:128, :].astype(BF))
        rates = rates + got[d, 128:136, :]
    for i in range(32):
        msg[i, 0:16, :] = total[16 * i : 16 * i + 16, :]
        msg[i, 16:24, :] = rates


def shards(layer_input, projection, ssm_input, step_logit, decay_rate, output_grad):
    tok, x, g, logit = layer_input[0], ssm_input[0], output_grad[0], step_logit[0]
    rate = decay_rate[None, :]
    width = x.shape[1]
    odd = lax.axis_index("par").astype(jnp.int32)[None]
    up = [(i, i + 1) for i in range(31)]
    down = [(i + 1, i) for i in range(31)]

    bc, c, dt, cg, dtg, ct, rows, keep_s, send_s = call(
        project_kernel,
        (
            shape(ROWS, 256, dtype=BF),
            shape(ROWS, HEADS),
            shape(ROWS, HEADS),
            shape(GROUPS, ROWS, GROUP),
            shape(GROUPS, ROWS, GROUP),
            shape(HEADS, ROWS),
            shape(2 * PAIRS, 128),
            shape(TILE, 128),
            shape(TILE + PAIRS, 128),
        ),
        400_000_000,
        6 << 20,
        in_specs=[SMEM] + [VMEM] * 5,
        out_specs=(VMEM,) * 9,
        name="project",
    )(odd, tok, projection, x, logit, rate)
    got_s = lax.ppermute(send_s, SEQ, up)
    keep_a, send_a = call(
        adjoint_kernel,
        (shape(TILE, 128), shape(TILE + PAIRS, 128)),
        140_000_000,
        3 << 20,
        in_specs=[SMEM] + [VMEM] * 4,
        out_specs=(VMEM,) * 2,
        name="adjoint",
    )(odd, bc, c, rows, g)
    got_a = lax.ppermute(send_a, SEQ, down)

    turned_tok = call(
        turn_kernel,
        shape(8, 32, 16, 128),
        1_000_000,
        3 << 20,
        in_specs=[VMEM],
        out_specs=VMEM,
        name="turn",
    )(tok)
    all_tok = lax.all_to_all(turned_tok, "dp", 0, 0).reshape(8, 512, 128)

    wide = GROUP * 64

    def place(i, odd):
        return (i + odd[0] * (GROUPS // 2)) % GROUPS

    u, t_rows, s_cols, ds = call(
        intra_kernel,
        (
            shape(ROWS, width),
            shape(HEADS, ROWS),
            shape(GROUPS, ROWS, GROUP),
            shape(ROWS, ROWS),
        ),
        800_000_000,
        20 << 20,
        grid_spec=pltpu.PrefetchScalarGridSpec(
            num_scalar_prefetch=1,
            grid=(GROUPS,),
            in_specs=[
                pl.BlockSpec((ROWS, 256), lambda i, odd: (0, 0)),
                pl.BlockSpec((1, ROWS, GROUP), lambda i, odd: (i, 0, 0)),
                pl.BlockSpec((1, ROWS, GROUP), lambda i, odd: (i, 0, 0)),
                pl.BlockSpec((GROUP, ROWS), lambda i, odd: (i, 0)),
                pl.BlockSpec((ROWS, wide), lambda i, odd: (0, place(i, odd))),
                pl.BlockSpec((ROWS, wide), lambda i, odd: (0, place(i, odd))),
            ],
            out_specs=(
                pl.BlockSpec((ROWS, wide), lambda i, odd: (0, place(i, odd))),
                pl.BlockSpec((GROUP, ROWS), lambda i, odd: (i, 0)),
                pl.BlockSpec((1, ROWS, GROUP), lambda i, odd: (i, 0, 0)),
                pl.BlockSpec((ROWS, ROWS), lambda i, odd: (0, 0)),
            ),
        ),
        name="intra",
    )(odd, bc, cg, dtg, ct, x, g)

    sent = call(
        combine_kernel,
        shape(PAIRS, 264, 128),
        4_000_000,
        6 << 20,
        in_specs=[VMEM] * 5,
        out_specs=VMEM,
        name="combine",
    )(rows, keep_s, keep_a, got_s, got_a)
    held = lax.all_to_all(sent, "blk", 0, 0)
    scanned = call(
        scan_kernel,
        shape(PAIRS, 256, 128),
        4_000_000,
        4 << 20,
        in_specs=[VMEM],
        out_specs=VMEM,
        name="scan",
    )(held)
    back = lax.all_to_all(scanned, "blk", 0, 0)
    s_own, a_own, s_next, a_next = call(
        unfold_kernel,
        (shape(TILE, 128),) * 4,
        8_000_000,
        10 << 20,
        in_specs=[VMEM] * 6,
        out_specs=(VMEM,) * 4,
        name="unfold",
    )(rows, keep_s, keep_a, got_s, got_a, back)
    s_far = lax.ppermute(s_next, SEQ, up)
    a_far = lax.ppermute(a_next, SEQ, down)

    gx_own, *own = call(
        outer_kernel,
        (
            shape(ROWS, TILE, dtype=BF),
            shape(ROWS, HALF),
            shape(ROWS, HALF),
            shape(8, HALF),
            shape(ROWS, 128),
            shape(ROWS, 128),
        ),
        500_000_000,
        6 << 20,
        in_specs=[SMEM] + [VMEM] * 9,
        out_specs=(VMEM,) * 6,
        scratch_shapes=[pltpu.VMEM((PAIRS, 128), F32)],
        name="outer",
    )(odd, s_own, a_own, x, g, u, c, dt, bc, ds)
    gx, step_grad, part = call(
        finish_kernel,
        (shape(ROWS, width, dtype=BF), shape(ROWS, HEADS), shape(136, 256)),
        500_000_000,
        6 << 20,
        in_specs=[SMEM] + [VMEM] * 18,
        out_specs=(VMEM,) * 3,
        scratch_shapes=[pltpu.VMEM((PAIRS, 128), F32)],
        name="finish",
    )(odd, s_far, a_far, x, g, u, c, dt, bc, gx_own, *own, t_rows, s_cols, logit, rate)

    parts = lax.all_to_all(jnp.broadcast_to(part[None], (8, 136, 256)), "dp", 0, 0)
    weight = call(
        weight_kernel,
        shape(32, 24, 256),
        300_000_000,
        4 << 20,
        in_specs=[VMEM] * 2,
        out_specs=VMEM,
        name="weight",
    )(all_tok, parts)
    summed = jnp.sum(lax.all_to_all(weight, SEQ, 0, 0), axis=0)
    full = lax.all_gather(summed[:16], "dp", tiled=True)
    return gx[None], step_grad[None], summed[16, :HEADS], full


def solution(mesh):
    devices = mesh.devices.reshape(16, 2, 8)
    parts = Mesh(devices, ("blk", "par", "dp"))
    placed = (
        P("dp", SEQ, None),
        P(),
        P("dp", SEQ, None),
        P("dp", SEQ, None),
        P(),
        P("dp", SEQ, None),
    )
    return jax.shard_map(
        shards,
        mesh=parts,
        in_specs=placed,
        out_specs=(P("dp", SEQ, None), P("dp", SEQ, None), P(), P(SEQ, None)),
        check_vma=False,
    )
```

time: 1470 us -> 279 us (0.19)
  waiting for transfers between devices: 986 us -> 89.7 us
  other arithmetic: 248 us -> 0.06 us
  local copies, waits for them, and re-layouts: 69.7 us -> 14.1 us
  starting transfers between devices: 0.12 us -> 46.2 us
  matrix products: 38.2 us -> 0 us
  Pallas kernels: 0 us -> 36.6 us
  blocking collectives: 112 us -> 90.4 us
    all_gather x2 -> x0, waiting for transfers between devices: 813 us -> none  [carried_in(): pieces = jax.tree.map(lambda part: lax.all_gather(part, axis), value)]
    select_n x62 -> x0, other arithmetic: 240 us -> none  [lap(): jnp.where(position < mine, new, old)]
    psum x1 -> x0, waiting for transfers between devices: 173 us -> none  [shards(): summed, rate_sum = lax.psum((grad_w, grad_rate), ('seq', 'dp'))]
    psum x1 -> x0, blocking collectives: 75.5 us -> none  [shards(): summed, rate_sum = lax.psum((grad_w, grad_rate), ('seq', 'dp'))]
    all_to_all x0 -> x2, blocking collectives: none -> 72.9 us  [the longest x1 51.5 us: shards(): held = lax.all_to_all(sent, 'blk', 0, 0)]
    all_to_all x0 -> x3, waiting for transfers between devices: none -> 56.3 us  [the longest x1 37.6 us: shards(): back = lax.all_to_all(scanned, 'blk', 0, 0)]
    rev x2 -> x0, local copies, waits for them, and re-layouts: 43.6 us -> none  [carried_in(): pieces = jax.tree.map(lambda part: part[::-1], pieces)]
    dot_general x13 -> x0, matrix products: 38.2 us -> none  [the longest x2 10.4 us: span_forward(): jnp.einsum('hts,shp->thp', weights, values, precision=lax.Precision.HIGHEST)]
  transfers between devices with their start and end apart: 3 -> 7, of which waited for: 3 -> 6; matrix products, arithmetic and copies ran while one was open for 2% -> 0% of each run, Pallas kernels for 0% -> 10%
where the time goes in v1:
time: 279 us; the launch traced here: 278 us
  blocking collectives  90.4 us (32%)
  waiting for transfers between devices  89.7 us (32%)
  starting transfers between devices  46.2 us (17%)
  Pallas kernels  36.6 us (13%)
  local copies, waits for them, and re-layouts  14.1 us (5%)
    all_to_all x1, blocking collectives, shards(): held = lax.all_to_all(sent, 'blk', 0, 0)  51.5 us
    all_to_all x1, waiting for transfers between devices, shards(): back = lax.all_to_all(scanned, 'blk', 0, 0)  37.6 us
    all_to_all x1, blocking collectives, shards(): lax.all_to_all(jnp.broadcast_to(part[None], (8, 136, 256)), 'dp', 0, 0)  21.4 us
    all_to_all x1, starting transfers between devices, shards(): all_tok = lax.all_to_all(turned_tok, 'dp', 0, 0).reshape(8, 512, 128)  20.3 us
    ppermute x1, waiting for transfers between devices, shards(): got_s = lax.ppermute(send_s, SEQ, up)  19 us
    all_to_all x1, waiting for transfers between devices, shards(): summed = jnp.sum(lax.all_to_all(weight, SEQ, 0, 0), axis=0)  18.6 us
    all_gather x1, blocking collectives, shards(): full = lax.all_gather(summed[:16], 'dp', tiled=True)  17.5 us
    unnamed x43, local copies, waits for them, and re-layouts  13.5 us
  transfers between devices with their start and end apart: 7, of which 6 were waited for; matrix products, arithmetic and copies ran while one was open for 0% of the time, Pallas kernels for 10%

profile of v1, /device:TPU:1, one launch (start us, length us, event | category | flops | bytes accessed | tf_op | source)
XLA Modules:
  0.0 278.0 jit_solution(1500568572852468282)
XLA Ops:
  4.6 3.8 %project.1 = (bf16[128,256]{1,0:T(8,128)(2,1)S(1)}, f32[128,64]{1,0:T(8,128)S(1)}, f32[128,64]{1,0:T(8,128)S(1)}, f32[8,128,8]{2,1,0:T(8,128)S(1)}, f32[8,128,8]...) custom-call(s32[1]{0:T(128)} %bitcast.odd_ref, ...), custom_call_target="tpu_custom_call" | custom-call | flops 400000000 | bytes 6291456 | tf_op jit(solution)/shard_map/project/pallas_call | solution.py:305
  10.0 4.4 %collective-permute-start = (f32[2064,128]{1,0:T(8,128)S(1)}, f32[2064,128]{1,0:T(8,128)S(1)}, u32[]{:S(2)}, u32[]{:S(2)}) collective-permute-start(f32[2064,128]{1,0:T(8,128)S(1)} %get-tuple-element.37), channel_id=1, source_target_pairs={{0,8},{8,16},{16,24},{24,32},{32,40},{40,48},{48,56},{56,64},{64,7... | collective-permute-start | bytes 3170312 | tf_op jit(solution)/shard_map/ppermute | solution.py:324
  14.4 1.6 adjoint.1
  17.3 19.0 %collective-permute-done.got_s = f32[2064,128]{1,0:T(8,128)S(1)} collective-permute-done((f32[2064,128]{1,0:T(8,128)S(1)}, f32[2064,128]{1,0:T(8,128)S(1)}, u32[]{:S(2)}, u32[]{:S(2)}) %collective-permute-start) | collective-permute-done | bytes 1056800 | tf_op jit(solution)/shard_map/ppermute | solution.py:324
  36.3 5.7 %collective-permute-done.1.got_a = f32[2064,128]{1,0:T(8,128)S(1)} collective-permute-done((f32[2064,128]{1,0:T(8,128)S(1)}, f32[2064,128]{1,0:T(8,128)S(1)}, u32[]{:S(2)}, u32[]{:S(2)}) %collective-permute-start.1) | collective-permute-done | bytes 1056800 | tf_op jit(solution)/shard_map/ppermute | solution.py:334
  42.1 1.6 combine.1
  45.8 51.5 %all_to_all.25.msg = f32[16,264,128]{2,1,0:T(8,128)S(1)} all-to-all(f32[16,264,128]{2,1,0:T(8,128)} %combine.1), channel_id=1, replica_groups=mesh['blk'=16,'par'=2,'dp'=8] {'blk'}, dimensions={0} | all-to-all | bytes 4325376 | tf_op jit(solution)/shard_map/all_to_all | solution.py:392
  97.3 1.5 scan.1
  98.8 4.6 %all-to-all-start.1 = ((f32[16,256,128]{2,1,0:T(8,128)}), f32[16,256,128]{2,1,0:T(8,128)}, u32[]{:S(2)}, u32[]{:S(2)}) async-start(f32[16,256,128]{2,1,0:T(8,128)} %scan.1), calls=%async_computation.1 | async-start | bytes 4194304 | tf_op jit(solution)/shard_map/all_to_all | solution.py:402
  105.1 37.6 %all-to-all-done.1.back = f32[16,256,128]{2,1,0:T(8,128)} async-done(((f32[16,256,128]{2,1,0:T(8,128)}), f32[16,256,128]{2,1,0:T(8,128)}, u32[]{:S(2)}, u32[]{:S(2)}) %all-to-all-start.1) | async-done | bytes 2097184 | tf_op jit(solution)/shard_map/all_to_all | solution.py:402
  142.7 20.3 %all-to-all-start.2 = ((f32[8,32,16,128]{3,2,1,0:T(8,128)}), f32[8,32,16,128]{3,2,1,0:T(8,128)S(1)}, u32[]{:S(2)}, u32[]{:S(2)}) async-start(f32[8,32,16,128]{3,2,1,0:T(8,128)} %copy-done.3), calls=%async_computation.2 | async-start | bytes 4194304 | tf_op jit(solution)/shard_map/all_to_all | solution.py:345
  164.3 3.0 %unfold.1 = (f32[2048,128]{1,0:T(8,128)S(1)}, f32[2048,128]{1,0:T(8,128)S(1)}, f32[2048,128]{1,0:T(8,128)S(1)}, f32[2048,128]{1,0:T(8,128)S(1)}) custom-call(f32[32,128]{1,0:T(8,128)S(1)} %get-tuple-element.32.rows, f32[2048,128]{1,0:T(8,128)S(1)} %copy-done.10, f32[2048,128]{1,0:T(8,128)} %copy-done.11, f32[2064,128]{1,0:T(8,128)} %copy-done.5, ...), custom_call_target="tpu_custom_call" | custom-call | flops 8000000 | bytes 10485760 | tf_op jit(solution)/shard_map/unfold/pallas_call | solution.py:403
  167.3 5.0 %collective-permute-start.2 = (f32[2048,128]{1,0:T(8,128)S(1)}, f32[2048,128]{1,0:T(8,128)S(1)}, u32[]{:S(2)}, u32[]{:S(2)}) collective-permute-start(f32[2048,128]{1,0:T(8,128)S(1)} %get-tuple-element.39), channel_id=1, source_target_pairs={{0,8},{8,16},{16,24},{24,32},{32,40},{40,48},{48,56},{56,64},{64,7... | collective-permute-start | bytes 3145736 | tf_op jit(solution)/shard_map/ppermute | solution.py:412
  172.4 1.5 collective-permute-start.3
  173.9 7.9 %intra.1 = (f32[128,4096]{1,0:T(8,128)S(1)}, f32[64,128]{1,0:T(8,128)S(1)}, f32[8,128,8]{2,1,0:T(8,128)S(1)}, f32[128,128]{1,0:T(8,128)S(1)}) custom-call(s32[1]{0:T(128)} %bitcast.odd_ref, bf16[128,256]{1,0:T(8,128)(2,1)S(1)} %get-tuple-element.34.bc, f32[8,128,8]{2,1,0:T(8,128)S(1)} %copy-done.13, f32[8,128,8]{2,1,0:T(8,128)S(1)} %copy-done.15, ...), custom_call_target="tpu_custom_call" | custom-call | flops 800000000 | bytes 20971520 | tf_op jit(solution)/shard_map/intra/pallas_call | solution.py:352
  183.2 6.9 %outer.1 = (bf16[128,2048]{1,0:T(8,128)(2,1)S(1)}, f32[128,32]{1,0:T(8,128)S(1)}, f32[128,32]{1,0:T(8,128)S(1)}, f32[8,32]{1,0:T(8,128)S(1)}, f32[128,128]{1,0:T(8,128)S(1)}, /*index=5*/f32[128,128]{1,0:T(8,128)S(1)}) custom-call(s32[1]{0:T(128)} %bitcast.odd_ref, f32[2048,128]{1,0:T(8,128)S(1)} %get-tuple-element.46.s_in, ...), custom_call_target="tpu_custom_call" | custom-call | flops 500000000 | bytes 6291456 | tf_op jit(solution)/shard_map/outer/pallas_call | solution.py:415
  190.0 4.9 %collective-permute-done.2.s_in = f32[2048,128]{1,0:T(8,128)S(1)} collective-permute-done((f32[2048,128]{1,0:T(8,128)S(1)}, f32[2048,128]{1,0:T(8,128)S(1)}, u32[]{:S(2)}, u32[]{:S(2)}) %collective-permute-start.2) | collective-permute-done | bytes 1048608 | tf_op jit(solution)/shard_map/ppermute | solution.py:412
  194.9 3.9 %collective-permute-done.3.a_in = f32[2048,128]{1,0:T(8,128)S(1)} collective-permute-done((f32[2048,128]{1,0:T(8,128)S(1)}, f32[2048,128]{1,0:T(8,128)S(1)}, u32[]{:S(2)}, u32[]{:S(2)}) %collective-permute-start.3) | collective-permute-done | bytes 1048608 | tf_op jit(solution)/shard_map/ppermute | solution.py:413
  198.8 8.3 %finish.1 = (bf16[128,4096]{1,0:T(8,128)(2,1)}, f32[128,64]{1,0:T(8,128)S(1)}, f32[136,256]{1,0:T(8,128)S(1)}) custom-call(s32[1]{0:T(128)} %bitcast.odd_ref, f32[2048,128]{1,0:T(8,128)S(1)} %collective-permute-done.2.s_in, f32[2048,128]{1,0:T(8,128)S(1)} %collective-permute-done.3.a_in, bf16[128,4096]{1,0:T(8,128)(2,1)S(1)} %bitcast.14, ...), custom_call_target="tpu_custom_call" | custom-call | flops 500000000 | bytes 6291456 | tf_op jit(solution)/shard_map/finish/pallas_call | solution.py:432
  207.8 21.4 %all_to_all.26.got = f32[8,136,256]{2,1,0:T(8,128)S(1)} all-to-all(f32[8,136,256]{2,1,0:T(8,128)S(1)} %broadcast_in_dim.22), channel_id=1, replica_groups=mesh['blk'=16,'par'=2,'dp'=8] {'dp'}, dimensions={0} | all-to-all | bytes 2228224 | tf_op jit(solution)/shard_map/all_to_all | solution.py:443
  229.2 1.6 weight.1
  230.8 9.1 %all-to-all-start.4 = ((f32[32,24,256]{2,1,0:T(8,128)}), f32[32,24,256]{2,1,0:T(8,128)S(1)}, u32[]{:S(2)}, u32[]{:S(2)}) async-start(f32[32,24,256]{2,1,0:T(8,128)} %weight.1), calls=%async_computation.4 | async-start | bytes 1572864 | tf_op jit(solution)/shard_map/all_to_all | solution.py:453
  240.6 18.6 %all-to-all-done.4 = f32[32,24,256]{2,1,0:T(8,128)S(1)} async-done(((f32[32,24,256]{2,1,0:T(8,128)}), f32[32,24,256]{2,1,0:T(8,128)S(1)}, u32[]{:S(2)}, u32[]{:S(2)}) %all-to-all-start.4) | async-done | bytes 786464 | tf_op jit(solution)/shard_map/all_to_all | solution.py:453
  259.8 17.5 %all_gather.3 = f32[128,256]{1,0:T(8,128)S(1)} all-gather(f32[16,256]{1,0:T(8,128)S(1)} %slice.9), channel_id=1, replica_groups=mesh['blk'=16,'par'=2,'dp'=8] {'dp'}, dimensions={0}, use_global_device_ids=true | all-gather | bytes 147456 | tf_op jit(solution)/shard_map/all_gather | solution.py:454
  (50 shorter events, 15.8 us)
Async XLA Ops:
  1.5 1.2 copy-start
  2.7 1.2 copy-start.7
  4.6 9.8 %copy-start.2 = (bf16[1,128,4096]{2,1,0:T(8,128)(2,1)S(1)}, bf16[1,128,4096]{2,1,0:T(8,128)(2,1)}, u32[]{:S(2)}) copy-start(bf16[1,128,4096]{2,1,0:T(8,128)(2,1)} %param.11) | copy-start | bytes 3145732
  9.2 0.8 copy-start.14
  10.0 33.7 %copy-start.9 = (f32[2048,128]{1,0:T(8,128)}, f32[2048,128]{1,0:T(8,128)S(1)}, u32[]{:S(2)}) copy-start(f32[2048,128]{1,0:T(8,128)S(1)} %get-tuple-element.33.keep_s) | copy-start | bytes 3145732
  10.0 26.4 %collective-permute-start = (f32[2064,128]{1,0:T(8,128)S(1)}, f32[2064,128]{1,0:T(8,128)S(1)}, u32[]{:S(2)}, u32[]{:S(2)}) collective-permute-start(f32[2064,128]{1,0:T(8,128)S(1)} %get-tuple-element.37), channel_id=1, source_target_pairs={{0,8},{8,16},{16,24},{24,32},{32,40},{40,48},{48,56},{56,64},{64,7... | collective-permute-start | bytes 3170312 | tf_op jit(solution)/shard_map/ppermute | solution.py:324
  16.0 26.0 %collective-permute-start.1 = (f32[2064,128]{1,0:T(8,128)S(1)}, f32[2064,128]{1,0:T(8,128)S(1)}, u32[]{:S(2)}, u32[]{:S(2)}) collective-permute-start(f32[2064,128]{1,0:T(8,128)S(1)} %get-tuple-element.38), channel_id=1, source_target_pairs={{8,0},{16,8},{24,16},{32,24},{40,32},{48,40},{56,48},{64,56},{72,6... | collective-permute-start | bytes 3170312 | tf_op jit(solution)/shard_map/ppermute | solution.py:334
  36.3 7.3 %copy-start.5 = (f32[2064,128]{1,0:T(8,128)}, f32[2064,128]{1,0:T(8,128)S(1)}, u32[]{:S(2)}) copy-start(f32[2064,128]{1,0:T(8,128)S(1)} %collective-permute-done.got_s) | copy-start | bytes 3170308
  43.7 1.1 copy-start.6
  44.8 1.0 copy-start.11
  98.8 4.6 %copy-start.8 = (bf16[1,128,4096]{2,1,0:T(8,128)(2,1)S(1)}, bf16[1,128,4096]{2,1,0:T(8,128)(2,1)}, u32[]{:S(2)}) copy-start(bf16[1,128,4096]{2,1,0:T(8,128)(2,1)} %param.6) | copy-start | bytes 3145732
  98.8 43.9 %all-to-all-start.1 = ((f32[16,256,128]{2,1,0:T(8,128)}), f32[16,256,128]{2,1,0:T(8,128)}, u32[]{:S(2)}, u32[]{:S(2)}) async-start(f32[16,256,128]{2,1,0:T(8,128)} %scan.1), calls=%async_computation.1 | async-start | bytes 4194304 | tf_op jit(solution)/shard_map/all_to_all | solution.py:402
  103.7 1.4 copy-start.3
  142.7 65.0 %all-to-all-start.2 = ((f32[8,32,16,128]{3,2,1,0:T(8,128)}), f32[8,32,16,128]{3,2,1,0:T(8,128)S(1)}, u32[]{:S(2)}, u32[]{:S(2)}) async-start(f32[8,32,16,128]{3,2,1,0:T(8,128)} %copy-done.3), calls=%async_computation.2 | async-start | bytes 4194304 | tf_op jit(solution)/shard_map/all_to_all | solution.py:345
  163.1 1.2 copy-start.10
  164.3 9.6 %copy-start.1 = (bf16[1,128,4096]{2,1,0:T(8,128)(2,1)S(1)}, bf16[1,128,4096]{2,1,0:T(8,128)(2,1)}, u32[]{:S(2)}) copy-start(bf16[1,128,4096]{2,1,0:T(8,128)(2,1)} %param.8) | copy-start | bytes 3145732
  164.3 9.6 %copy-start.13 = (f32[8,128,8]{2,1,0:T(8,128)S(1)}, f32[8,128,8]{2,1,0:T(8,128)}, u32[]{:S(2)}) copy-start(f32[8,128,8]{2,1,0:T(8,128)} %copy-done.12) | copy-start | bytes 98308
  164.3 9.6 %copy-start.15 = (f32[8,128,8]{2,1,0:T(8,128)S(1)}, f32[8,128,8]{2,1,0:T(8,128)}, u32[]{:S(2)}) copy-start(f32[8,128,8]{2,1,0:T(8,128)} %copy-done.14) | copy-start | bytes 98308
  167.3 27.6 %collective-permute-start.2 = (f32[2048,128]{1,0:T(8,128)S(1)}, f32[2048,128]{1,0:T(8,128)S(1)}, u32[]{:S(2)}, u32[]{:S(2)}) collective-permute-start(f32[2048,128]{1,0:T(8,128)S(1)} %get-tuple-element.39), channel_id=1, source_target_pairs={{0,8},{8,16},{16,24},{24,32},{32,40},{40,48},{48,56},{56,64},{64,7... | collective-permute-start | bytes 3145736 | tf_op jit(solution)/shard_map/ppermute | solution.py:412
  172.4 26.4 %collective-permute-start.3 = (f32[2048,128]{1,0:T(8,128)S(1)}, f32[2048,128]{1,0:T(8,128)S(1)}, u32[]{:S(2)}, u32[]{:S(2)}) collective-permute-start(f32[2048,128]{1,0:T(8,128)S(1)} %get-tuple-element.40), channel_id=1, source_target_pairs={{8,0},{16,8},{24,16},{32,24},{40,32},{48,40},{56,48},{64,56},{72,6... | collective-permute-start | bytes 3145736 | tf_op jit(solution)/shard_map/ppermute | solution.py:413
  181.8 1.3 copy-start.4
  183.2 15.6 %copy-start.19 = (f32[64]{0:T(128)S(1)}, f32[64]{0:T(128)}, u32[]{:S(2)}) copy-start(f32[64]{0:T(128)} %param.10) | copy-start | bytes 772
  229.2 10.7 %copy-start.17 = (f32[128,64]{1,0:T(8,128)S(1)}, f32[128,64]{1,0:T(8,128)}, u32[]{:S(2)}) copy-start(f32[128,64]{1,0:T(8,128)} %copy-done.16) | copy-start | bytes 98308
  230.8 28.5 %all-to-all-start.4 = ((f32[32,24,256]{2,1,0:T(8,128)}), f32[32,24,256]{2,1,0:T(8,128)S(1)}, u32[]{:S(2)}, u32[]{:S(2)}) async-start(f32[32,24,256]{2,1,0:T(8,128)} %weight.1), calls=%async_computation.4 | async-start | bytes 1572864 | tf_op jit(solution)/shard_map/all_to_all | solution.py:453
  (3 other events, 2.1 us)

commit v2 on v1

v2 whole, which is shorter than its diff:
```python
import functools

import jax
import jax.numpy as jnp
from jax import lax
from jax.experimental import pallas as pl
from jax.experimental.pallas import tpu as pltpu
from jax.sharding import Mesh
from jax.sharding import PartitionSpec as P

ROWS = 128
HEADS = 64
SLOTS = 4
PART = HEADS // SLOTS
PAIRS = PART // 2
ALL_PAIRS = HEADS // 2
TILE = PAIRS * 128
MIRROR = (2, 1, 0, 3)
GROUP = 8
GROUPS = HEADS // GROUP
BF = jnp.bfloat16
F32 = jnp.float32
NN = (((1,), (0,)), ((), ()))
NT = (((1,), (1,)), ((), ()))
TN = (((0,), (0,)), ((), ()))
HIGH = lax.Precision.HIGHEST
VMEM = pl.BlockSpec(memory_space=pltpu.VMEM)
SMEM = pl.BlockSpec(memory_space=pltpu.SMEM)
HBM = pl.BlockSpec(memory_space=pltpu.HBM)
SEQ = ("x", "quad", "turn")
BLOCK = ("x", "quad")
CHUNKS = 4
CHUNK = 1024


def iota(shape, dim):
    return lax.broadcasted_iota(jnp.int32, shape, dim)


def dot(a, b, dims=NN):
    return lax.dot_general(a, b, dims, preferred_element_type=F32)


def dot_exact(a, b):
    return lax.dot_general(a, b, NN, precision=HIGH, preferred_element_type=F32)


def dot_split(a, b):
    head = a.astype(BF)
    tail = (a - head.astype(F32)).astype(BF)
    return dot(head, b) + dot(tail, b)


def spread(cols, pair, left):
    one = cols[:, 2 * pair : 2 * pair + 1]
    two = cols[:, 2 * pair + 1 : 2 * pair + 2]
    return jnp.where(left, one, two)


def turned(values, turn):
    parts = [values[:, PART * k : PART * k + PART] for k in range(SLOTS)]
    out = values
    for t in range(SLOTS):
        order = jnp.concatenate([parts[(t + 3 - k) % SLOTS] for k in range(SLOTS)], axis=1)
        out = jnp.where(turn == t, order, out)
    return out


def lanes(pair, turn):
    slot, place = divmod(pair, PAIRS)
    start = lax.rem(turn + 3 - slot, SLOTS) * TILE + 128 * place
    return pl.ds(pl.multiple_of(start, 128), 128)


def tile(place):
    return slice(128 * place, 128 * place + 128)


def call(kernel, outs, flops, moved, room=8, **more):
    return pl.pallas_call(
        kernel,
        out_shape=outs,
        compiler_params=pltpu.CompilerParams(vmem_limit_bytes=room << 20),
        cost_estimate=pl.CostEstimate(flops=flops, bytes_accessed=moved, transcendentals=0),
        **more,
    )


def shape(*dims, dtype=F32):
    return jax.ShapeDtypeStruct(dims, dtype)


def advance(name, kernel, *fixed):
    return call(
        functools.partial(kernel, *fixed),
        shape(TILE + PAIRS if kernel is gather_step_kernel else TILE, 128),
        1_000_000,
        2 << 20,
        in_specs=[VMEM] * 3,
        out_specs=VMEM,
        name=name,
    )


def turn_kernel(tok, out):
    for i in range(32):
        at = slice(128 * i, 128 * i + 128)
        out[at, :] = tok[:, at].astype(F32).T.astype(BF)


def project_kernel(
    turn_ref, logit, rate, tok_hbm, proj_hbm, x_hbm, bc_ref, c_ref, dt_ref, rows_ref, xw_ref, send, tok, proj, x, sems
):
    copies = []
    for k in range(CHUNKS):
        at = pl.ds(k * CHUNK, CHUNK)
        copies.append(
            (
                pltpu.make_async_copy(tok_hbm.at[:, at], tok.at[:, at], sems.at[0, k]),
                pltpu.make_async_copy(proj_hbm.at[at, :], proj.at[at, :], sems.at[1, k]),
            )
        )
        for copy in copies[-1]:
            copy.start()
    fetch_x = pltpu.make_async_copy(x_hbm, x, sems.at[2, 0])
    fetch_x.start()
    turn = turn_ref[0]
    z = turned(logit[...].T, turn)
    dt = jnp.maximum(z, 0.0) + jnp.log1p(jnp.exp(-jnp.abs(z)))
    a = -turned(rate[...], turn) * dt
    lower = (iota((ROWS, ROWS), 0) >= iota((ROWS, ROWS), 1)).astype(F32)
    c = dot_exact(lower, a)
    c_ref[...] = c
    dt_ref[...] = dt
    last = c[ROWS - 1 : ROWS, :]
    to_end = jnp.exp(last - c) * dt
    left = iota((ROWS, 128), 1) < 64
    left1 = iota((1, 128), 1) < 64
    for pair in range(ALL_PAIRS):
        rows_ref[pair : pair + 1, :] = spread(last, pair, left1)
    send[TILE : TILE + PAIRS, :] = rows_ref[0:PAIRS, :]
    total = jnp.zeros((ROWS, 256), F32)
    for k in range(CHUNKS):
        for copy in copies[k]:
            copy.wait()
        at = slice(k * CHUNK, k * CHUNK + CHUNK)
        total = total + dot(tok[:, at], proj[at, :])
    bc = total.astype(BF)
    bc_ref[...] = bc
    b_t = bc[:, :128].astype(F32).T.astype(BF)
    fetch_x.wait()
    for pair in range(ALL_PAIRS):
        at = lanes(pair, turn)
        xw = (x[:, at].astype(F32) * spread(to_end, pair, left)).astype(BF)
        xw_ref[:, at] = xw
        if pair < PAIRS:
            send[tile(pair), :] = dot(b_t, xw)


def adjoint_kernel(turn_ref, bc, c_ref, rows, g, gw_ref, send):
    turn = turn_ref[0]
    ec = jnp.exp(c_ref[...])
    c_t = bc[:, 128:].astype(F32).T.astype(BF)
    left = iota((ROWS, 128), 1) < 64
    first = MIRROR[0] * PAIRS
    for pair in range(ALL_PAIRS):
        at = lanes(pair, turn)
        gw = (g[:, at].astype(F32) * spread(ec, pair, left)).astype(BF)
        gw_ref[:, at] = gw
        if first <= pair < first + PAIRS:
            send[tile(pair - first), :] = dot(c_t, gw)
    send[TILE : TILE + PAIRS, :] = rows[first : first + PAIRS, :]


def rest_kernel(turn_ref, bc, c_ref, dt_ref, xw, gw, rest_s, rest_a, cg_ref, dtg_ref, ct_ref):
    turn = turn_ref[0]
    both = bc[...].astype(F32)
    b_t = both[:, :128].T.astype(BF)
    c_t = both[:, 128:].T.astype(BF)
    for k in range(1, SLOTS):
        for place in range(PAIRS):
            rest_s[k - 1, tile(place), :] = dot(b_t, xw[:, lanes(k * PAIRS + place, turn)])
            rest_a[k - 1, tile(place), :] = dot(c_t, gw[:, lanes(MIRROR[k] * PAIRS + place, turn)])
    c = c_ref[...]
    ct_ref[...] = c.T
    for group in range(GROUPS):
        cg_ref[group] = c[:, GROUP * group : GROUP * group + GROUP]
        dtg_ref[group] = dt_ref[:, GROUP * group : GROUP * group + GROUP]


def gather_step_kernel(slot, k, rows, got, rest, out):
    for place in range(PAIRS):
        own = rows[slot * PAIRS + place : slot * PAIRS + place + 1, :]
        out[tile(place), :] = jnp.exp(own) * got[tile(place), :] + rest[k - 1, tile(place), :]
    out[TILE : TILE + PAIRS, :] = got[TILE : TILE + PAIRS, :] + rows[slot * PAIRS : slot * PAIRS + PAIRS, :]


def spread_step_kernel(slot, rows, state, local, out):
    for place in range(PAIRS):
        own = rows[slot * PAIRS + place : slot * PAIRS + place + 1, :]
        out[tile(place), :] = jnp.exp(own) * state[tile(place), :] + local[tile(place), :]


def spread_rest_kernel(slot, rows, state, rest, out):
    spread_step_kernel(slot, rows, state, rest.at[0], out)


def intra_kernel(turn_ref, bc, cg, dtg, ct, x, g, u_ref, t_ref, s_ref, ds_ref):
    @pl.when(pl.program_id(0) == 0)
    def _():
        ds_ref[...] = jnp.zeros_like(ds_ref)

    sc_t = dot(bc[:, :128], bc[:, 128:], NT)
    causal = iota((ROWS, ROWS), 0) <= iota((ROWS, ROWS), 1)
    left = iota((ROWS, 128), 1) < 64
    ones = (left.astype(F32).astype(BF), (1.0 - left.astype(F32)).astype(BF))
    lane8 = iota((ROWS, GROUP), 1)
    s_all = jnp.zeros((ROWS, GROUP), F32)
    total = ds_ref[...]
    for pair in range(GROUP // 2):
        xs = x[:, 128 * pair : 128 * pair + 128]
        gs = g[:, 128 * pair : 128 * pair + 128]
        parts = []
        for side in range(2):
            h = 2 * pair + side
            gx = dot(xs * ones[side], gs, NT)
            gap = ct[h : h + 1, :] - cg[0, :, h : h + 1]
            decay = jnp.exp(jnp.where(causal, gap, -jnp.inf))
            parts.append(dot((decay * sc_t).astype(BF), gs))
            p = decay * gx * dtg[0, :, h : h + 1]
            total = total + p
            m = p * sc_t
            t_ref[h : h + 1, :] = jnp.sum(m, axis=0, keepdims=True)
            s_all = jnp.where(lane8 == h, jnp.sum(m, axis=1, keepdims=True), s_all)
        u_ref[:, 128 * pair : 128 * pair + 128] = jnp.where(left, parts[0], parts[1])
    s_ref[0] = s_all
    ds_ref[...] = total


def combine_kernel(rows, rest_s, rest_a, got_s, got_a, msg):
    for place in range(PAIRS):
        own = rows[3 * PAIRS + place : 3 * PAIRS + place + 1, :]
        decay = jnp.exp(own)
        msg[place, 0:128, :] = decay * got_s[tile(place), :] + rest_s[2, tile(place), :]
        msg[place, 128:256, :] = decay * got_a[tile(place), :] + rest_a[2, tile(place), :]
        msg[place, 256:257, :] = own + got_s[TILE + place : TILE + place + 1, :]
        msg[place, 257:258, :] = own + got_a[TILE + place : TILE + place + 1, :]
        msg[place, 258:264, :] = jnp.zeros((6, 128), F32)


def scan_kernel(msg, out):
    state = jnp.zeros((128, 128), F32)
    for i in range(PAIRS):
        out[i, 0:128, :] = state
        state = jnp.exp(msg[i, 256:257, :]) * state + msg[i, 0:128, :]
    state = jnp.zeros((128, 128), F32)
    for i in range(PAIRS - 1, -1, -1):
        out[i, 128:256, :] = state
        state = jnp.exp(msg[i, 257:258, :]) * state + msg[i, 128:256, :]


def near_states(got_s, got_a, back, place):
    mark = TILE + place
    state = jnp.exp(got_s[mark : mark + 1, :]) * back[place, 0:128, :] + got_s[tile(place), :]
    adj = jnp.exp(got_a[mark : mark + 1, :]) * back[place, 128:256, :] + got_a[tile(place), :]
    return state, adj


def unfold_kernel(rows, rest_s, rest_a, got_s, got_a, back, s_next, a_next):
    for place in range(PAIRS):
        state, adj = near_states(got_s, got_a, back, place)
        decay = jnp.exp(rows[3 * PAIRS + place : 3 * PAIRS + place + 1, :])
        s_next[tile(place), :] = decay * state + rest_s[2, tile(place), :]
        a_next[tile(place), :] = decay * adj + rest_a[2, tile(place), :]


def outer_terms(slot, turn, s_in, a_in, x, g, u, c_ref, dt_ref, bc, dots, store):
    cols = slice(PART * slot, PART * slot + PART)
    c = c_ref[:, cols]
    dt = dt_ref[:, cols]
    last = c[ROWS - 1 : ROWS, :]
    end = jnp.exp(last - c)
    ec = jnp.exp(c)
    b_bf, c_bf = bc[:, :128], bc[:, 128:]
    left = iota((ROWS, 128), 1) < 64
    choice = iota((ROWS, PART), 1) - (iota((ROWS, PART), 0) >= 64).astype(jnp.int32)
    role = jnp.zeros((ROWS, PART), F32)
    outer = jnp.zeros((ROWS, PART), F32)
    for place in range(PAIRS):
        at = lanes(slot * PAIRS + place, turn)
        picked = (choice == 2 * place).astype(F32).astype(BF)
        state = s_in[tile(place), :]
        adj = a_in[tile(place), :]
        dots[place : place + 1, :] = jnp.sum(adj * state, axis=0, keepdims=True)
        gw = g[:, at].astype(F32) * spread(ec, place, left)
        role = role + dot_split(gw * dot(c_bf, state.astype(BF)), picked)
        add = dot(b_bf, adj.astype(BF)) * spread(end, place, left)
        store(place, ((u[:, at] + add) * spread(dt, place, left)).astype(BF))
        outer = outer + dot_split(x[:, at].astype(F32) * add, picked)
    row, col = iota((128, PART), 0), iota((128, PART), 1)
    side = ((row >= 64).astype(jnp.int32) == col % 2).astype(F32)
    both = dot_exact(dots[...], side)
    mine = iota((PAIRS, PART), 0) == iota((PAIRS, PART), 1) // 2
    meet = jnp.exp(last) * jnp.sum(jnp.where(mine, both, 0.0), axis=0, keepdims=True)
    return role, outer, meet


def outer_kernel(
    slot, turn_ref, s_in, a_in, x, g, u, c_ref, dt_ref, bc, gx_ref, role_ref, outer_ref, meet_ref, dots
):
    def store(place, value):
        gx_ref[:, tile(place)] = value

    role, outer, meet = outer_terms(slot, turn_ref[0], s_in, a_in, x, g, u, c_ref, dt_ref, bc, dots, store)
    role_ref[...] = role
    outer_ref[...] = outer
    meet_ref[...] = jnp.broadcast_to(meet, (8, PART))


def near_kernel(turn_ref, got_s, got_a, back, xw, gw, bc, ds, out, s_own, a_own):
    turn = turn_ref[0]
    inner = ds[...].astype(BF)
    grad_b = dot(inner, bc[:, 128:])
    grad_c = dot(inner, bc[:, :128], TN)
    for place in range(PAIRS):
        at = lanes(3 * PAIRS + place, turn)
        state, adj = near_states(got_s, got_a, back, place)
        s_own[tile(place), :] = state
        a_own[tile(place), :] = adj
        grad_b = grad_b + dot(xw[:, at], adj.astype(BF), NT)
        grad_c = grad_c + dot(gw[:, at], state.astype(BF), NT)
    out[:, :128] = grad_b
    out[:, 128:] = grad_c


def more_terms(turn, k, s_in, a_in, xw, gw, grad_b, grad_c):
    for place in range(PAIRS):
        grad_b = grad_b + dot(xw[:, lanes(MIRROR[k] * PAIRS + place, turn)], a_in[tile(place), :].astype(BF), NT)
        grad_c = grad_c + dot(gw[:, lanes(k * PAIRS + place, turn)], s_in[tile(place), :].astype(BF), NT)
    return grad_b, grad_c


def middle_kernel(turn_ref, s_0, a_0, s_1, a_1, xw, gw, near, out):
    turn = turn_ref[0]
    grads = near[:, :128], near[:, 128:]
    grads = more_terms(turn, 0, s_0, a_0, xw, gw, *grads)
    grads = more_terms(turn, 1, s_1, a_1, xw, gw, *grads)
    out[:, :128] = grads[0]
    out[:, 128:] = grads[1]


def far_kernel(turn_ref, core_ref, s_in, a_in, xw, gw, near, tok_t, keep, send):
    first = core_ref[0] == 0
    grad_b, grad_c = more_terms(turn_ref[0], 2, s_in, a_in, xw, gw, near[:, :128], near[:, 128:])
    both = jnp.concatenate([grad_b.astype(BF), grad_c.astype(BF)], axis=1)
    for i in range(32):
        part = dot(tok_t[128 * i : 128 * i + 128, :], both)
        x, z = divmod(i, 8)
        rows = slice(16 * z, 16 * z + 16)
        for y in range(4):
            one = part[32 * y : 32 * y + 16, :]
            two = part[32 * y + 16 : 32 * y + 32, :]
            keep[4 * x + y, rows, :] = jnp.where(first, one, two)
            send[4 * x + y, rows, :] = jnp.where(first, two, one)


def join_kernel(keep, got, rates, msg):
    for k in range(16):
        msg[k, 0:128, :] = keep[k] + got[k]
        msg[k, 128:136, :] = rates[...]


def fold_kernel(msg, out):
    total = msg[0]
    for k in range(1, 16):
        total = total + msg[k]
    for z in range(8):
        out[z, 0:16, :] = total[16 * z : 16 * z + 16, :]
        out[z, 16:24, :] = total[128:136, :]


def last_kernel(msg, out):
    total = msg[0]
    for k in range(1, 8):
        total = total + msg[k]
    for k in range(8):
        out[k] = total


def finish_kernel(
    turn_ref, s_0, a_0, s_2, a_2, x, g, u, c_ref, dt_ref, bc, gx_1, role_1, outer_1, meet_1, gx_3, role_3, outer_3,
    meet_3, t_rows, s_cols, logit, rate, gx_ref, step_ref, rate_ref, dots,
):
    turn = turn_ref[0]

    def terms(slot, state, adj):
        def store(place, value):
            gx_ref[:, lanes(slot * PAIRS + place, turn)] = value

        return outer_terms(slot, turn, state, adj, x, g, u, c_ref, dt_ref, bc, dots, store)

    zero, two = terms(0, s_0, a_0), terms(2, s_2, a_2)
    for place in range(PAIRS):
        gx_ref[:, lanes(PAIRS + place, turn)] = gx_1[:, tile(place)]
        gx_ref[:, lanes(3 * PAIRS + place, turn)] = gx_3[:, tile(place)]
    dt = dt_ref[...]
    role_t = jnp.concatenate([zero[0], role_1[...], two[0], role_3[...]], axis=1) + t_rows[...].T
    outer = jnp.concatenate([zero[1], outer_1[...], two[1], outer_3[...]], axis=1)
    meet = jnp.concatenate([zero[2], meet_1[0:1, :], two[2], meet_3[0:1, :]], axis=1)
    role_s = jnp.concatenate([s_cols[k] for k in range(GROUPS)], axis=1)
    row, col = iota((ROWS, ROWS), 0), iota((ROWS, ROWS), 1)
    later = (col >= row).astype(F32)
    before = (col < row).astype(F32)
    da = dot_exact(later, role_t - role_s) + dot_exact(before, outer * dt) + meet
    ddt = turned(role_s / dt + outer, turn) - rate[...] * turned(da, turn)
    step_ref[...] = ddt.T / (1.0 + jnp.exp(-logit[...]))
    rate_row = turned(-jnp.sum(dt * da, axis=0, keepdims=True), turn)
    wide = jnp.concatenate([rate_row, jnp.zeros((1, 256 - HEADS), F32)], axis=1)
    rate_ref[...] = jnp.broadcast_to(wide, (8, 256))


def shards(layer_input, projection, ssm_input, step_logit, decay_rate, output_grad):
    tok, x, g, logit = layer_input[0], ssm_input[0], output_grad[0], step_logit[0].T
    rate = decay_rate[None, :]
    width = x.shape[1]
    turn = lax.axis_index("turn").astype(jnp.int32)[None]
    core = lax.axis_index("c").astype(jnp.int32)[None]
    up = [(i, i + 1) for i in range(31)]
    down = [(i + 1, i) for i in range(31)]

    bc, c, dt, rows, xw, send_s = call(
        project_kernel,
        (
            shape(ROWS, 256, dtype=BF),
            shape(ROWS, HEADS),
            shape(ROWS, HEADS),
            shape(ALL_PAIRS, 128),
            shape(ROWS, width, dtype=BF),
            shape(TILE + PAIRS, 128),
        ),
        400_000_000,
        6 << 20,
        room=52,
        in_specs=[SMEM, VMEM, VMEM, HBM, HBM, HBM],
        out_specs=(VMEM,) * 6,
        scratch_shapes=[
            pltpu.VMEM((ROWS, width), BF),
            pltpu.VMEM((width, 256), BF),
            pltpu.VMEM((ROWS, width), BF),
            pltpu.SemaphoreType.DMA((3, CHUNKS)),
        ],
        name="project",
    )(turn, logit, rate, tok, projection, x)
    got_s = lax.ppermute(send_s, SEQ, up)
    gw, send_a = call(
        adjoint_kernel,
        (shape(ROWS, width, dtype=BF), shape(TILE + PAIRS, 128)),
        140_000_000,
        3 << 20,
        in_specs=[SMEM] + [VMEM] * 4,
        out_specs=(VMEM,) * 2,
        name="adjoint",
    )(turn, bc, c, rows, g)
    got_a = lax.ppermute(send_a, SEQ, down)

    rest_s, rest_a, cg, dtg, ct = call(
        rest_kernel,
        (
            shape(3, TILE, 128),
            shape(3, TILE, 128),
            shape(GROUPS, ROWS, GROUP),
            shape(GROUPS, ROWS, GROUP),
            shape(HEADS, ROWS),
        ),
        200_000_000,
        6 << 20,
        in_specs=[SMEM] + [VMEM] * 5,
        out_specs=(VMEM,) * 5,
        name="rest",
    )(turn, bc, c, dt, xw, gw)
    tok_t = call(
        turn_kernel,
        shape(width, ROWS, dtype=BF),
        1_000_000,
        3 << 20,
        in_specs=[VMEM],
        out_specs=VMEM,
        name="turn",
    )(tok)

    wide = GROUP * 64

    def place(i, turn):
        return lax.rem(turn[0] + 3 - i // 2, SLOTS) * 2 + i % 2

    u, t_rows, s_cols, ds = call(
        intra_kernel,
        (
            shape(ROWS, width),
            shape(HEADS, ROWS),
            shape(GROUPS, ROWS, GROUP),
            shape(ROWS, ROWS),
        ),
        800_000_000,
        20 << 20,
        grid_spec=pltpu.PrefetchScalarGridSpec(
            num_scalar_prefetch=1,
            grid=(GROUPS,),
            in_specs=[
                pl.BlockSpec((ROWS, 256), lambda i, turn: (0, 0)),
                pl.BlockSpec((1, ROWS, GROUP), lambda i, turn: (i, 0, 0)),
                pl.BlockSpec((1, ROWS, GROUP), lambda i, turn: (i, 0, 0)),
                pl.BlockSpec((GROUP, ROWS), lambda i, turn: (i, 0)),
                pl.BlockSpec((ROWS, wide), lambda i, turn: (0, place(i, turn))),
                pl.BlockSpec((ROWS, wide), lambda i, turn: (0, place(i, turn))),
            ],
            out_specs=(
                pl.BlockSpec((ROWS, wide), lambda i, turn: (0, place(i, turn))),
                pl.BlockSpec((GROUP, ROWS), lambda i, turn: (i, 0)),
                pl.BlockSpec((1, ROWS, GROUP), lambda i, turn: (i, 0, 0)),
                pl.BlockSpec((ROWS, ROWS), lambda i, turn: (0, 0)),
            ),
        ),
        name="intra",
    )(turn, bc, cg, dtg, ct, x, g)
    for k in (1, 2):
        got_s = lax.ppermute(advance("gather_s", gather_step_kernel, k, k)(rows, got_s, rest_s), SEQ, up)
        got_a = lax.ppermute(advance("gather_a", gather_step_kernel, MIRROR[k], k)(rows, got_a, rest_a), SEQ, down)
    got_s, got_a, u, tok_t = lax.optimization_barrier((got_s, got_a, u, tok_t))

    sent = call(
        combine_kernel,
        shape(PAIRS, 264, 128),
        4_000_000,
        4 << 20,
        in_specs=[VMEM] * 5,
        out_specs=VMEM,
        name="combine",
    )(rows, rest_s, rest_a, got_s, got_a)
    held = lax.all_to_all(sent, BLOCK, 0, 0)
    scanned = call(
        scan_kernel,
        shape(PAIRS, 256, 128),
        4_000_000,
        4 << 20,
        in_specs=[VMEM],
        out_specs=VMEM,
        name="scan",
    )(held)
    back = lax.all_to_all(scanned, BLOCK, 0, 0)
    s_next, a_next = call(
        unfold_kernel,
        (shape(TILE, 128),) * 2,
        8_000_000,
        4 << 20,
        in_specs=[VMEM] * 6,
        out_specs=(VMEM,) * 2,
        name="unfold",
    )(rows, rest_s, rest_a, got_s, got_a, back)
    s_0 = lax.ppermute(s_next, SEQ, up)
    a_0 = lax.ppermute(a_next, SEQ, down)
    near, s_own, a_own = call(
        near_kernel,
        (shape(ROWS, 256), shape(TILE, 128), shape(TILE, 128)),
        140_000_000,
        4 << 20,
        in_specs=[SMEM] + [VMEM] * 7,
        out_specs=(VMEM,) * 3,
        name="near",
    )(turn, got_s, got_a, back, xw, gw, bc, ds)

    def outer_part(slot, state, adj):
        return call(
            functools.partial(outer_kernel, slot),
            (
                shape(ROWS, TILE, dtype=BF),
                shape(ROWS, PART),
                shape(ROWS, PART),
                shape(8, PART),
            ),
            250_000_000,
            6 << 20,
            in_specs=[SMEM] + [VMEM] * 8,
            out_specs=(VMEM,) * 4,
            scratch_shapes=[pltpu.VMEM((PAIRS, 128), F32)],
            name="outer",
        )(turn, state, adj, x, g, u, c, dt, bc)

    own = outer_part(3, s_own, a_own)
    s_1 = lax.ppermute(advance("spread_s", spread_step_kernel, 0)(rows, s_0, send_s), SEQ, up)
    a_1 = lax.ppermute(advance("spread_a", spread_step_kernel, MIRROR[0])(rows, a_0, send_a), SEQ, down)
    s_2 = lax.ppermute(advance("spread_s", spread_rest_kernel, 1)(rows, s_1, rest_s), SEQ, up)
    a_2 = lax.ppermute(advance("spread_a", spread_rest_kernel, MIRROR[1])(rows, a_1, rest_a), SEQ, down)
    middle = call(
        middle_kernel,
        shape(ROWS, 256),
        140_000_000,
        4 << 20,
        in_specs=[SMEM] + [VMEM] * 7,
        out_specs=VMEM,
        name="middle",
    )(turn, s_0, a_0, s_1, a_1, xw, gw, near)
    one = outer_part(1, s_1, a_1)
    s_2, a_2, middle, one, own = lax.optimization_barrier((s_2, a_2, middle, one, own))
    keep, send = call(
        far_kernel,
        (shape(16, 128, 256),) * 2,
        400_000_000,
        7 << 20,
        in_specs=[SMEM] * 2 + [VMEM] * 6,
        out_specs=(VMEM,) * 2,
        name="far",
    )(turn, core, s_2, a_2, xw, gw, middle, tok_t)
    got = lax.ppermute(send, "c", [(0, 1), (1, 0)])
    gx, step_grad, rates = call(
        finish_kernel,
        (shape(ROWS, width, dtype=BF), shape(HEADS, ROWS), shape(8, 256)),
        500_000_000,
        6 << 20,
        in_specs=[SMEM] + [VMEM] * 22,
        out_specs=(VMEM,) * 3,
        scratch_shapes=[pltpu.VMEM((PAIRS, 128), F32)],
        name="finish",
    )(turn, s_0, a_2, s_2, a_0, x, g, u, c, dt, bc, *one, *own, t_rows, s_cols, logit, rate)
    joined = call(
        join_kernel,
        shape(16, 136, 256),
        1_000_000,
        6 << 20,
        in_specs=[VMEM] * 3,
        out_specs=VMEM,
        name="join",
    )(keep, got, rates)
    folded = call(
        fold_kernel,
        shape(8, 24, 256),
        1_000_000,
        2 << 20,
        in_specs=[VMEM],
        out_specs=VMEM,
        name="fold",
    )(lax.all_to_all(joined, ("x", "y"), 0, 0))
    summed = call(
        last_kernel,
        shape(8, 24, 256),
        1_000_000,
        1 << 20,
        in_specs=[VMEM],
        out_specs=VMEM,
        name="last",
    )(lax.all_to_all(folded, ("quad", "turn"), 0, 0))
    last = lax.all_to_all(summed, ("y", "c"), 0, 0)
    rate_grad = last[0, 16, :HEADS] + last[1, 16, :HEADS]
    return gx[None], step_grad.T[None], rate_grad, last[:, :16].reshape(ROWS, 256)


def solution(mesh):
    devices = mesh.devices.reshape(4, 2, 4, 4, 2)
    parts = Mesh(devices, ("x", "quad", "turn", "y", "c"))
    rows = P(("y", "c"), SEQ, None)
    return jax.shard_map(
        shards,
        mesh=parts,
        in_specs=(rows, P(), rows, rows, P(), rows),
        out_specs=(rows, rows, P(), P(SEQ, None)),
        check_vma=False,
    )
```

time: 279 us -> 248 us (0.89)
  waiting for transfers between devices: 89.7 us -> 37.1 us
  blocking collectives: 90.4 us -> 111 us
  starting transfers between devices: 46.2 us -> 54 us
  Pallas kernels: 36.6 us -> 30.6 us
    all_to_all x3 -> x0, waiting for transfers between devices: 56.3 us -> none  [the longest x1 37.6 us: shards(): back = lax.all_to_all(scanned, 'blk', 0, 0)]
    ppermute x2 -> x11, starting transfers between devices: 6.52 us -> 47.6 us  [the longest x1 17.9 us: shards(): lax.ppermute(advance('spread_s', spread_step_kernel, 0)(rows, s_0, send_s...]
    all_to_all x2 -> x5, blocking collectives: 72.9 us -> 111 us  [the longest x1 39.1 us: shards(): lax.all_to_all(joined, ('x', 'y'), 0, 0)]
    all_to_all x3 -> x0, starting transfers between devices: 34 us -> none  [the longest x1 20.3 us: shards(): all_tok = lax.all_to_all(turned_tok, 'dp', 0, 0).reshape(8, 512, 128)]
    ppermute x2 -> x11, waiting for transfers between devices: 8.73 us -> 30 us  [the longest x1 14.6 us: shards(): a_0 = lax.ppermute(a_next, SEQ, down)]
    ppermute x1, waiting for transfers between devices: 19 us -> 0.01 us  [shards(): got_s = lax.ppermute(send_s, SEQ, up)]
    all_gather x1 -> x0, blocking collectives: 17.5 us -> none  [shards(): full = lax.all_gather(summed[:16], 'dp', tiled=True)]
    pallas_call x7 -> x22, Pallas kernels: 23.4 us -> 18.6 us  [the longest x1 5.58 us: shards(): call(finish_kernel, (shape(ROWS, width, dtype=BF), shape(HEADS, ROWS), sh...]
  transfers between devices with their start and end apart: 7 -> 13, of which waited for: 6 -> 4; matrix products, arithmetic and copies ran while one was open for 0% -> 0% of each run, Pallas kernels for 10% -> 9%
where the time goes in v2:
time: 248 us; the launch traced here: 247 us
  blocking collectives  111 us (45%)
  starting transfers between devices  54 us (22%)
  waiting for transfers between devices  37.1 us (15%)
  Pallas kernels  30.6 us (12%)
  local copies, waits for them, and re-layouts  13.1 us (5%)
    all_to_all x1, blocking collectives, shards(): lax.all_to_all(joined, ('x', 'y'), 0, 0)  39.1 us
    all_to_all x1, blocking collectives, shards(): held = lax.all_to_all(sent, BLOCK, 0, 0)  29.5 us
    all_to_all x1, blocking collectives, shards(): back = lax.all_to_all(scanned, BLOCK, 0, 0)  19.8 us
    ppermute x1, starting transfers between devices, shards(): lax.ppermute(advance('spread_s', spread_step_kernel, 0)(rows, s_0, send_s...  17.9 us
    ppermute x1, waiting for transfers between devices, shards(): a_0 = lax.ppermute(a_next, SEQ, down)  14.6 us
    unnamed x60, local copies, waits for them, and re-layouts  12.5 us
    all_to_all x1, blocking collectives, shards(): last = lax.all_to_all(summed, ('y', 'c'), 0, 0)  11.4 us
    all_to_all x1, blocking collectives, shards(): lax.all_to_all(folded, ('quad', 'turn'), 0, 0)  11 us
  transfers between devices with their start and end apart: 13, of which 4 were waited for; matrix products, arithmetic and copies ran while one was open for 0% of the time, Pallas kernels for 9%

profile of v2, /device:TPU:1, one launch (start us, length us, event | category | flops | bytes accessed | tf_op | source)
XLA Modules:
  0.0 247.2 jit_solution(12232647996282934510)
XLA Ops:
  2.1 3.9 %project.1 = (bf16[128,256]{1,0:T(8,128)(2,1)S(1)}, f32[128,64]{1,0:T(8,128)S(1)}, f32[128,64]{1,0:T(8,128)S(1)}, f32[32,128]{1,0:T(8,128)S(1)}, bf16[128,4096]{1,0:T(8,128)(2,1)S(1)}, /*index=5*/f32[1032,128]{1,0:T(8,128)S(1)}) custom-call(s32[1]{0:T(128)} %bitcast.turn_ref, f32[64,128]{1,0:T(8,128)S(1)} %bitcast.28, f32[1,64]{1,0:T(1,128)S(1)} %bitcast.30, ...), custom_call_target="tpu_custom_call" | custom-call | flops 400000000 | bytes 6291456 | tf_op jit(solution)/shard_map/project/pallas_call | solution.py:431
  8.6 5.0 %collective-permute-start = (f32[1032,128]{1,0:T(8,128)S(1)}, f32[1032,128]{1,0:T(8,128)S(1)}, u32[]{:S(2)}, u32[]{:S(2)}) collective-permute-start(f32[1032,128]{1,0:T(8,128)S(1)} %get-tuple-element.62.local), channel_id=1, source_target_pairs={{0,8},{8,16},{16,24},{24,32},{32,40},{40,48},{48,56},{56,64},{64,7... | collective-permute-start | bytes 1585160 | tf_op jit(solution)/shard_map/ppermute | solution.py:454
  14.3 7.2 %collective-permute-done.3.got = f32[1032,128]{1,0:T(8,128)S(1)} collective-permute-done((f32[1032,128]{1,0:T(8,128)S(1)}, f32[1032,128]{1,0:T(8,128)S(1)}, u32[]{:S(2)}, u32[]{:S(2)}) %collective-permute-start.3) | collective-permute-done | bytes 528416 | tf_op jit(solution)/shard_map/ppermute | solution.py:464
  23.0 6.1 %collective-permute-start.1 = (f32[1032,128]{1,0:T(8,128)S(1)}, f32[1032,128]{1,0:T(8,128)S(1)}, u32[]{:S(2)}, u32[]{:S(2)}) collective-permute-start(f32[1032,128]{1,0:T(8,128)S(1)} %gather_s.2), channel_id=1, source_target_pairs={{0,8},{8,16},{16,24},{24,32},{32,40},{40,48},{48,56},{56,64},{64,7... | collective-permute-start | bytes 1585160 | tf_op jit(solution)/shard_map/ppermute | solution.py:527
  29.1 8.7 %collective-permute-done.4.got = f32[1032,128]{1,0:T(8,128)S(1)} collective-permute-done((f32[1032,128]{1,0:T(8,128)S(1)}, f32[1032,128]{1,0:T(8,128)S(1)}, u32[]{:S(2)}, u32[]{:S(2)}) %collective-permute-start.4) | collective-permute-done | bytes 528416 | tf_op jit(solution)/shard_map/ppermute | solution.py:528
  37.9 1.4 collective-permute-start.5
  39.4 4.2 %collective-permute-start.2 = (f32[1032,128]{1,0:T(8,128)S(1)}, f32[1032,128]{1,0:T(8,128)S(1)}, u32[]{:S(2)}, u32[]{:S(2)}) collective-permute-start(f32[1032,128]{1,0:T(8,128)S(1)} %gather_s.3), channel_id=1, source_target_pairs={{0,8},{8,16},{16,24},{24,32},{32,40},{40,48},{48,56},{56,64},{64,7... | collective-permute-start | bytes 1585160 | tf_op jit(solution)/shard_map/ppermute | solution.py:527
  45.0 8.0 %intra.1 = (f32[128,4096]{1,0:T(8,128)S(1)}, f32[64,128]{1,0:T(8,128)S(1)}, f32[8,128,8]{2,1,0:T(8,128)S(1)}, f32[128,128]{1,0:T(8,128)S(1)}) custom-call(s32[1]{0:T(128)} %bitcast.turn_ref, bf16[128,256]{1,0:T(8,128)(2,1)S(1)} %get-tuple-element.55.bc, f32[8,128,8]{2,1,0:T(8,128)S(1)} %get-tuple-element.64.cg, f32[8,128,8]{2,1,0:T(8,128)S(1)} %get-tuple-element.65.dtg, ...), custom_call_target="tpu_custom_call" | custom-call | flops 800000000 | bytes 20971520 | tf_op jit(solution)/shard_map/intra/pallas_call | solution.py:496
  53.0 1.3 copy-done.2
  55.1 29.5 %all_to_all.25.msg = f32[8,264,128]{2,1,0:T(8,128)S(1)} all-to-all(f32[8,264,128]{2,1,0:T(8,128)S(1)} %combine.1), channel_id=1, replica_groups=mesh['x'=4,'quad'=2,'turn'=4,'y'=4,'c'=2] {'x','quad'}, dimensions={0} | all-to-all | bytes 2162688 | tf_op jit(solution)/shard_map/all_to_all | solution.py:540
  84.7 19.8 %all_to_all.26.back = f32[8,256,128]{2,1,0:T(8,128)S(1)} all-to-all(f32[8,256,128]{2,1,0:T(8,128)S(1)} %scan.1), channel_id=1, replica_groups=mesh['x'=4,'quad'=2,'turn'=4,'y'=4,'c'=2] {'x','quad'}, dimensions={0} | all-to-all | bytes 2097152 | tf_op jit(solution)/shard_map/all_to_all | solution.py:550
  106.7 4.0 %collective-permute-start.6 = (f32[1024,128]{1,0:T(8,128)S(1)}, f32[1024,128]{1,0:T(8,128)S(1)}, u32[]{:S(2)}, u32[]{:S(2)}) collective-permute-start(f32[1024,128]{1,0:T(8,128)S(1)} %get-tuple-element.70), channel_id=1, source_target_pairs={{0,8},{8,16},{16,24},{24,32},{32,40},{40,48},{48,56},{56,64},{64,7... | collective-permute-start | bytes 1572872 | tf_op jit(solution)/shard_map/ppermute | solution.py:560
  110.8 14.6 %collective-permute-done.9.state.a_0.a_2 = f32[1024,128]{1,0:T(8,128)S(1)} collective-permute-done((f32[1024,128]{1,0:T(8,128)S(1)}, f32[1024,128]{1,0:T(8,128)S(1)}, u32[]{:S(2)}, u32[]{:S(2)}) %collective-permute-start.9) | collective-permute-done | bytes 524320 | tf_op jit(solution)/shard_map/ppermute | solution.py:561
  128.5 17.9 %collective-permute-start.7 = (f32[1024,128]{1,0:T(8,128)S(1)}, f32[1024,128]{1,0:T(8,128)S(1)}, u32[]{:S(2)}, u32[]{:S(2)}) collective-permute-start(f32[1024,128]{1,0:T(8,128)S(1)} %spread_s.2), channel_id=1, source_target_pairs={{0,8},{8,16},{16,24},{24,32},{32,40},{40,48},{48,56},{56,64},{64,7... | collective-permute-start | bytes 1572872 | tf_op jit(solution)/shard_map/ppermute | solution.py:590
  146.5 6.6 %collective-permute-done.10.state.a_1.a_in = f32[1024,128]{1,0:T(8,128)S(1)} collective-permute-done((f32[1024,128]{1,0:T(8,128)S(1)}, f32[1024,128]{1,0:T(8,128)S(1)}, u32[]{:S(2)}, u32[]{:S(2)}) %collective-permute-start.10) | collective-permute-done | bytes 524320 | tf_op jit(solution)/shard_map/ppermute | solution.py:591
  156.4 4.8 %collective-permute-start.8 = (f32[1024,128]{1,0:T(8,128)}, f32[1024,128]{1,0:T(8,128)}, u32[]{:S(2)}, u32[]{:S(2)}) collective-permute-start(f32[1024,128]{1,0:T(8,128)} %spread_s.3), channel_id=1, source_target_pairs={{0,8},{8,16},{16,24},{24,32},{32,40},{40,48},{48,56},{56,64},{64,7... | collective-permute-start | bytes 1572872 | tf_op jit(solution)/shard_map/ppermute | solution.py:592
  167.3 1.9 outer.3
  170.1 1.9 outer.2
  172.1 2.4 far.1
  174.5 4.0 %collective-permute-start.12 = (f32[16,128,256]{2,1,0:T(8,128)S(1)}, f32[16,128,256]{2,1,0:T(8,128)S(1)}, u32[]{:S(2)}, u32[]{:S(2)}) collective-permute-start(f32[16,128,256]{2,1,0:T(8,128)S(1)} %get-tuple-element.102), channel_id=1, source_target_pairs={{0,1},{1,0},{2,3},{3,2},{4,5},{5,4},{6,7},{7,6},{8,9},{9,8},{10,11... | collective-permute-start | bytes 6291464 | tf_op jit(solution)/shard_map/ppermute | solution.py:614
  178.5 5.6 %finish.1 = (bf16[128,4096]{1,0:T(8,128)(2,1)}, f32[64,128]{1,0:T(8,128)}, f32[8,256]{1,0:T(8,128)S(1)}) custom-call(s32[1]{0:T(128)} %bitcast.turn_ref, f32[1024,128]{1,0:T(8,128)S(1)} %copy-done.16, f32[1024,128]{1,0:T(8,128)} %collective-permute-done.11.a_0.a_in, f32[1024,128]{1,0:T(8,128)} %collective-permute-done.8.s_2.s_in, ...), custom_call_target="tpu_custom_call" | custom-call | flops 500000000 | bytes 6291456 | tf_op jit(solution)/shard_map/finish/pallas_call | solution.py:615
  184.3 39.1 %all_to_all.27.msg = f32[16,136,256]{2,1,0:T(8,128)S(1)} all-to-all(f32[16,136,256]{2,1,0:T(8,128)S(1)} %join.1), channel_id=1, replica_groups=mesh['x'=4,'quad'=2,'turn'=4,'y'=4,'c'=2] {'x','y'}, dimensions={0} | all-to-all | bytes 4456448 | tf_op jit(solution)/shard_map/all_to_all | solution.py:642
  223.5 11.0 %all_to_all.28.msg = f32[8,24,256]{2,1,0:T(8,128)S(1)} all-to-all(f32[8,24,256]{2,1,0:T(8,128)S(1)} %fold.1), channel_id=1, replica_groups=mesh['x'=4,'quad'=2,'turn'=4,'y'=4,'c'=2] {'quad','turn'}, dimensions={0} | all-to-all | bytes 393216 | tf_op jit(solution)/shard_map/all_to_all | solution.py:651
  234.6 11.4 %all_to_all.29 = f32[8,24,256]{2,1,0:T(8,128)S(1)} all-to-all(f32[8,24,256]{2,1,0:T(8,128)S(1)} %last.1), channel_id=1, replica_groups=mesh['x'=4,'quad'=2,'turn'=4,'y'=4,'c'=2] {'y','c'}, dimensions={0} | all-to-all | bytes 393216 | tf_op jit(solution)/shard_map/all_to_all | solution.py:652
  (94 shorter events, 25.6 us)
Async XLA Ops:
  2.1 3.9 %copy-start.1 = (bf16[1,128,4096]{2,1,0:T(8,128)(2,1)S(1)}, bf16[1,128,4096]{2,1,0:T(8,128)(2,1)}, u32[]{:S(2)}) copy-start(bf16[1,128,4096]{2,1,0:T(8,128)(2,1)} %param.11) | copy-start | bytes 3145732
  7.3 14.3 %copy-start.4 = (bf16[128,4096]{1,0:T(8,128)(2,1)}, bf16[128,4096]{1,0:T(8,128)(2,1)S(1)}, u32[]{:S(2)}) copy-start(bf16[128,4096]{1,0:T(8,128)(2,1)S(1)} %get-tuple-element.59.gw) | copy-start | bytes 3145732
  7.3 14.2 %collective-permute-start.3 = (f32[1032,128]{1,0:T(8,128)S(1)}, f32[1032,128]{1,0:T(8,128)S(1)}, u32[]{:S(2)}, u32[]{:S(2)}) collective-permute-start(f32[1032,128]{1,0:T(8,128)S(1)} %get-tuple-element.63.local), channel_id=1, source_target_pairs={{8,0},{16,8},{24,16},{32,24},{40,32},{48,40},{56,48},{64,56},{72,6... | collective-permute-start | bytes 1585160 | tf_op jit(solution)/shard_map/ppermute | solution.py:464
  8.6 14.3 %collective-permute-start = (f32[1032,128]{1,0:T(8,128)S(1)}, f32[1032,128]{1,0:T(8,128)S(1)}, u32[]{:S(2)}, u32[]{:S(2)}) collective-permute-start(f32[1032,128]{1,0:T(8,128)S(1)} %get-tuple-element.62.local), channel_id=1, source_target_pairs={{0,8},{8,16},{16,24},{24,32},{32,40},{40,48},{48,56},{56,64},{64,7... | collective-permute-start | bytes 1585160 | tf_op jit(solution)/shard_map/ppermute | solution.py:454
  21.6 16.2 %collective-permute-start.4 = (f32[1032,128]{1,0:T(8,128)S(1)}, f32[1032,128]{1,0:T(8,128)S(1)}, u32[]{:S(2)}, u32[]{:S(2)}) collective-permute-start(f32[1032,128]{1,0:T(8,128)S(1)} %gather_a.2), channel_id=1, source_target_pairs={{8,0},{16,8},{24,16},{32,24},{40,32},{48,40},{56,48},{64,56},{72,6... | collective-permute-start | bytes 1585160 | tf_op jit(solution)/shard_map/ppermute | solution.py:528
  23.0 20.7 %copy-start.21 = (bf16[1,128,4096]{2,1,0:T(8,128)(2,1)S(1)}, bf16[1,128,4096]{2,1,0:T(8,128)(2,1)}, u32[]{:S(2)}) copy-start(bf16[1,128,4096]{2,1,0:T(8,128)(2,1)} %param.6) | copy-start | bytes 3145732
  23.0 16.4 %collective-permute-start.1 = (f32[1032,128]{1,0:T(8,128)S(1)}, f32[1032,128]{1,0:T(8,128)S(1)}, u32[]{:S(2)}, u32[]{:S(2)}) collective-permute-start(f32[1032,128]{1,0:T(8,128)S(1)} %gather_s.2), channel_id=1, source_target_pairs={{0,8},{8,16},{16,24},{24,32},{32,40},{40,48},{48,56},{56,64},{64,7... | collective-permute-start | bytes 1585160 | tf_op jit(solution)/shard_map/ppermute | solution.py:527
  37.9 7.1 %copy-start = (bf16[1,128,4096]{2,1,0:T(8,128)(2,1)S(1)}, bf16[1,128,4096]{2,1,0:T(8,128)(2,1)}, u32[]{:S(2)}) copy-start(bf16[1,128,4096]{2,1,0:T(8,128)(2,1)} %param.8) | copy-start | bytes 3145732
  37.9 16.4 %collective-permute-start.5 = (f32[1032,128]{1,0:T(8,128)S(1)}, f32[1032,128]{1,0:T(8,128)S(1)}, u32[]{:S(2)}, u32[]{:S(2)}) collective-permute-start(f32[1032,128]{1,0:T(8,128)S(1)} %gather_a.3), channel_id=1, source_target_pairs={{8,0},{16,8},{24,16},{32,24},{40,32},{48,40},{56,48},{64,56},{72,6... | collective-permute-start | bytes 1585160 | tf_op jit(solution)/shard_map/ppermute | solution.py:528
  39.4 14.9 %collective-permute-start.2 = (f32[1032,128]{1,0:T(8,128)S(1)}, f32[1032,128]{1,0:T(8,128)S(1)}, u32[]{:S(2)}, u32[]{:S(2)}) collective-permute-start(f32[1032,128]{1,0:T(8,128)S(1)} %gather_s.3), channel_id=1, source_target_pairs={{0,8},{8,16},{16,24},{24,32},{32,40},{40,48},{48,56},{56,64},{64,7... | collective-permute-start | bytes 1585160 | tf_op jit(solution)/shard_map/ppermute | solution.py:527
  54.3 50.2 %copy-start.9 = (f32[1032,128]{1,0:T(8,128)}, f32[1032,128]{1,0:T(8,128)S(1)}, u32[]{:S(2)}) copy-start(f32[1032,128]{1,0:T(8,128)S(1)} %collective-permute-done.5.got_a) | copy-start | bytes 1585156
  54.3 50.2 %copy-start.11 = (f32[1032,128]{1,0:T(8,128)}, f32[1032,128]{1,0:T(8,128)S(1)}, u32[]{:S(2)}) copy-start(f32[1032,128]{1,0:T(8,128)S(1)} %collective-permute-done.2.got_s) | copy-start | bytes 1585156
  105.5 19.9 %collective-permute-start.9 = (f32[1024,128]{1,0:T(8,128)S(1)}, f32[1024,128]{1,0:T(8,128)S(1)}, u32[]{:S(2)}, u32[]{:S(2)}) collective-permute-start(f32[1024,128]{1,0:T(8,128)S(1)} %get-tuple-element.71), channel_id=1, source_target_pairs={{8,0},{16,8},{24,16},{32,24},{40,32},{48,40},{56,48},{64,56},{72,6... | collective-permute-start | bytes 1572872 | tf_op jit(solution)/shard_map/ppermute | solution.py:561
  106.7 20.9 %collective-permute-start.6 = (f32[1024,128]{1,0:T(8,128)S(1)}, f32[1024,128]{1,0:T(8,128)S(1)}, u32[]{:S(2)}, u32[]{:S(2)}) collective-permute-start(f32[1024,128]{1,0:T(8,128)S(1)} %get-tuple-element.70), channel_id=1, source_target_pairs={{0,8},{8,16},{16,24},{24,32},{32,40},{40,48},{48,56},{56,64},{64,7... | collective-permute-start | bytes 1572872 | tf_op jit(solution)/shard_map/ppermute | solution.py:560
  126.3 26.8 %collective-permute-start.10 = (f32[1024,128]{1,0:T(8,128)S(1)}, f32[1024,128]{1,0:T(8,128)S(1)}, u32[]{:S(2)}, u32[]{:S(2)}) collective-permute-start(f32[1024,128]{1,0:T(8,128)S(1)} %spread_a.2), channel_id=1, source_target_pairs={{8,0},{16,8},{24,16},{32,24},{40,32},{48,40},{56,48},{64,56},{72,6... | collective-permute-start | bytes 1572872 | tf_op jit(solution)/shard_map/ppermute | solution.py:591
  128.5 26.8 %collective-permute-start.7 = (f32[1024,128]{1,0:T(8,128)S(1)}, f32[1024,128]{1,0:T(8,128)S(1)}, u32[]{:S(2)}, u32[]{:S(2)}) collective-permute-start(f32[1024,128]{1,0:T(8,128)S(1)} %spread_s.2), channel_id=1, source_target_pairs={{0,8},{8,16},{16,24},{24,32},{32,40},{40,48},{48,56},{56,64},{64,7... | collective-permute-start | bytes 1572872 | tf_op jit(solution)/shard_map/ppermute | solution.py:590
  153.1 3.3 %copy-start.17 = (f32[1024,128]{1,0:T(8,128)}, f32[1024,128]{1,0:T(8,128)S(1)}, u32[]{:S(2)}) copy-start(f32[1024,128]{1,0:T(8,128)S(1)} %collective-permute-done.10.state.a_1.a_in) | copy-start | bytes 1572868
  154.1 17.9 %collective-permute-start.11 = (f32[1024,128]{1,0:T(8,128)}, f32[1024,128]{1,0:T(8,128)}, u32[]{:S(2)}, u32[]{:S(2)}) collective-permute-start(f32[1024,128]{1,0:T(8,128)} %spread_a.3), channel_id=1, source_target_pairs={{8,0},{16,8},{24,16},{32,24},{40,32},{48,40},{56,48},{64,56},{72,6... | collective-permute-start | bytes 1572872 | tf_op jit(solution)/shard_map/ppermute | solution.py:593
  156.4 15.6 %collective-permute-start.8 = (f32[1024,128]{1,0:T(8,128)}, f32[1024,128]{1,0:T(8,128)}, u32[]{:S(2)}, u32[]{:S(2)}) collective-permute-start(f32[1024,128]{1,0:T(8,128)} %spread_s.3), channel_id=1, source_target_pairs={{0,8},{8,16},{16,24},{24,32},{32,40},{40,48},{48,56},{56,64},{64,7... | collective-permute-start | bytes 1572872 | tf_op jit(solution)/shard_map/ppermute | solution.py:592
  167.3 1.9 copy-start.20
  172.0 6.5 %copy-start.25 = (f32[8,128,8]{2,1,0:T(8,128)S(1)}, f32[8,128,8]{2,1,0:T(8,128)}, u32[]{:S(2)}) copy-start(f32[8,128,8]{2,1,0:T(8,128)} %copy-done.24) | copy-start | bytes 98308
  172.0 6.5 %copy-start.27 = (f32[1,128,64]{1,2,0:T(8,128)S(1)}, f32[1,128,64]{1,2,0:T(8,128)}, u32[]{:S(2)}) copy-start(f32[1,128,64]{1,2,0:T(8,128)} %param.9) | copy-start | bytes 98308
  172.0 6.5 %copy-start.29 = (f32[64]{0:T(128)S(1)}, f32[64]{0:T(128)}, u32[]{:S(2)}) copy-start(f32[64]{0:T(128)} %param.10) | copy-start | bytes 772
  174.5 9.6 %collective-permute-start.12 = (f32[16,128,256]{2,1,0:T(8,128)S(1)}, f32[16,128,256]{2,1,0:T(8,128)S(1)}, u32[]{:S(2)}, u32[]{:S(2)}) collective-permute-start(f32[16,128,256]{2,1,0:T(8,128)S(1)} %get-tuple-element.102), channel_id=1, source_target_pairs={{0,1},{1,0},{2,3},{3,2},{4,5},{5,4},{6,7},{7,6},{8,9},{9,8},{10,11... | collective-permute-start | bytes 6291464 | tf_op jit(solution)/shard_map/ppermute | solution.py:614
  (19 other events, 23.9 us)

commit v3 on v2

--- a/solution.py
+++ b/solution.py
@@ -102,10 +102,21 @@
     )
 
 
-def turn_kernel(tok, out):
+def turn_kernel(core_ref, tok, mine, other):
+    first = core_ref[0] == 0
     for i in range(32):
-        at = slice(128 * i, 128 * i + 128)
-        out[at, :] = tok[:, at].astype(F32).T.astype(BF)
+        part = tok[:, tile(i)].astype(F32).T
+        x, z = divmod(i, 8)
+        for y in range(4):
+            one = part[32 * y : 32 * y + 16, :]
+            two = part[32 * y + 16 : 32 * y + 32, :]
+            rows = slice(512 * x + 128 * y + 16 * z, 512 * x + 128 * y + 16 * z + 16)
+            mine[rows, :] = jnp.where(first, one, two).astype(BF)
+            other[rows, :] = jnp.where(first, two, one)
+
+
+def narrow_kernel(wide, out):
+    out[...] = wide[...].astype(BF)
 
 
 def project_kernel(
@@ -349,34 +360,25 @@
     out[:, 128:] = grads[1]
 
 
-def far_kernel(turn_ref, core_ref, s_in, a_in, xw, gw, near, tok_t, keep, send):
-    first = core_ref[0] == 0
+def far_kernel(turn_ref, s_in, a_in, xw, gw, near, out):
     grad_b, grad_c = more_terms(turn_ref[0], 2, s_in, a_in, xw, gw, near[:, :128], near[:, 128:])
-    both = jnp.concatenate([grad_b.astype(BF), grad_c.astype(BF)], axis=1)
-    for i in range(32):
-        part = dot(tok_t[128 * i : 128 * i + 128, :], both)
-        x, z = divmod(i, 8)
-        rows = slice(16 * z, 16 * z + 16)
-        for y in range(4):
-            one = part[32 * y : 32 * y + 16, :]
-            two = part[32 * y + 16 : 32 * y + 32, :]
-            keep[4 * x + y, rows, :] = jnp.where(first, one, two)
-            send[4 * x + y, rows, :] = jnp.where(first, two, one)
-
-
-def join_kernel(keep, got, rates, msg):
+    out[:, :128] = grad_b.astype(BF).astype(F32)
+    out[:, 128:] = grad_c.astype(BF).astype(F32)
+
+
+def weight_kernel(tok_mine, tok_got, mine, got, msg):
+    here, there = mine[...].astype(BF), got[...].astype(BF)
     for k in range(16):
-        msg[k, 0:128, :] = keep[k] + got[k]
-        msg[k, 128:136, :] = rates[...]
-
-
-def fold_kernel(msg, out):
+        msg[k] = dot(tok_mine[tile(k), :], here) + dot(tok_got[tile(k), :], there)
+
+
+def fold_kernel(msg, rates, one, two, three, out):
     total = msg[0]
     for k in range(1, 16):
         total = total + msg[k]
     for z in range(8):
         out[z, 0:16, :] = total[16 * z : 16 * z + 16, :]
-        out[z, 16:24, :] = total[128:136, :]
+        out[z, 16:24, :] = rates[...] + one[...] + two[...] + three[...]
 
 
 def last_kernel(msg, out):
@@ -478,15 +480,25 @@
         out_specs=(VMEM,) * 5,
         name="rest",
     )(turn, bc, c, dt, xw, gw)
-    tok_t = call(
+    tok_mine, tok_other = call(
         turn_kernel,
-        shape(width, ROWS, dtype=BF),
+        (shape(width // 2, ROWS, dtype=BF), shape(width // 2, ROWS)),
         1_000_000,
         3 << 20,
+        in_specs=[SMEM, VMEM],
+        out_specs=(VMEM,) * 2,
+        name="turn",
+    )(core, tok)
+    swap = [(0, 1), (1, 0)]
+    tok_got = call(
+        narrow_kernel,
+        shape(width // 2, ROWS, dtype=BF),
+        1_000_000,
+        2 << 20,
         in_specs=[VMEM],
         out_specs=VMEM,
-        name="turn",
-    )(tok)
+        name="narrow",
+    )(lax.ppermute(tok_other, "c", swap))
 
     wide = GROUP * 64
 
@@ -526,7 +538,7 @@
     for k in (1, 2):
         got_s = lax.ppermute(advance("gather_s", gather_step_kernel, k, k)(rows, got_s, rest_s), SEQ, up)
         got_a = lax.ppermute(advance("gather_a", gather_step_kernel, MIRROR[k], k)(rows, got_a, rest_a), SEQ, down)
-    got_s, got_a, u, tok_t = lax.optimization_barrier((got_s, got_a, u, tok_t))
+    got_s, got_a, u, tok_mine, tok_got = lax.optimization_barrier((got_s, got_a, u, tok_mine, tok_got))
 
     sent = call(
         combine_kernel,
@@ -602,16 +614,26 @@
     )(turn, s_0, a_0, s_1, a_1, xw, gw, near)
     one = outer_part(1, s_1, a_1)
     s_2, a_2, middle, one, own = lax.optimization_barrier((s_2, a_2, middle, one, own))
-    keep, send = call(
+    part = call(
         far_kernel,
-        (shape(16, 128, 256),) * 2,
-        400_000_000,
-        7 << 20,
-        in_specs=[SMEM] * 2 + [VMEM] * 6,
-        out_specs=(VMEM,) * 2,
+        shape(ROWS, 256),
+        70_000_000,
+        3 << 20,
+        in_specs=[SMEM] + [VMEM] * 5,
+        out_specs=VMEM,
         name="far",
-    )(turn, core, s_2, a_2, xw, gw, middle, tok_t)
-    got = lax.ppermute(send, "c", [(0, 1), (1, 0)])
+    )(turn, s_2, a_2, xw, gw, middle)
+    weight = call(
+        weight_kernel,
+        shape(16, 128, 256),
+        300_000_000,
+        4 << 20,
+        in_specs=[VMEM] * 4,
+        out_specs=VMEM,
+        name="weight",
+    )(tok_mine, tok_got, part, lax.ppermute(part, "c", swap))
+    weight, s_2, a_2 = lax.optimization_barrier((weight, s_2, a_2))
+    over_xy = lax.all_to_all(weight, ("x", "y"), 0, 0)
     gx, step_grad, rates = call(
         finish_kernel,
         (shape(ROWS, width, dtype=BF), shape(HEADS, ROWS), shape(8, 256)),
@@ -622,24 +644,16 @@
         scratch_shapes=[pltpu.VMEM((PAIRS, 128), F32)],
         name="finish",
     )(turn, s_0, a_2, s_2, a_0, x, g, u, c, dt, bc, *one, *own, t_rows, s_cols, logit, rate)
-    joined = call(
-        join_kernel,
-        shape(16, 136, 256),
-        1_000_000,
-        6 << 20,
-        in_specs=[VMEM] * 3,
-        out_specs=VMEM,
-        name="join",
-    )(keep, got, rates)
+    far_rates = [lax.ppermute(rates, "x", [(i, (i + hop) % 4) for i in range(4)]) for hop in (1, 2, 3)]
     folded = call(
         fold_kernel,
         shape(8, 24, 256),
         1_000_000,
         2 << 20,
-        in_specs=[VMEM],
+        in_specs=[VMEM] * 5,
         out_specs=VMEM,
         name="fold",
-    )(lax.all_to_all(joined, ("x", "y"), 0, 0))
+    )(over_xy, rates, *far_rates)
     summed = call(
         last_kernel,
         shape(8, 24, 256),
@@ -650,7 +664,7 @@
         name="last",
     )(lax.all_to_all(folded, ("quad", "turn"), 0, 0))
     last = lax.all_to_all(summed, ("y", "c"), 0, 0)
-    rate_grad = last[0, 16, :HEADS] + last[1, 16, :HEADS]
+    rate_grad = jnp.sum(last[:, 16, :HEADS], axis=0)
     return gx[None], step_grad.T[None], rate_grad, last[:, :16].reshape(ROWS, 256)
 
 

time: 248 us -> 243 us (0.980)
  blocking collectives: 111 us -> 90.9 us
  starting transfers between devices: 54 us -> 62.8 us
    all_to_all x1 -> x0, blocking collectives: 39.1 us -> none  [shards(): lax.all_to_all(joined, ('x', 'y'), 0, 0)]
    all_to_all x0 -> x1, starting transfers between devices: none -> 14.8 us  [shards(): over_xy = lax.all_to_all(weight, ('x', 'y'), 0, 0)]
    ppermute x1, starting transfers between devices: 17.9 us -> 4.15 us  [shards(): lax.ppermute(advance('spread_s', spread_step_kernel, 0)(rows, s_0, send_s...]
    all_to_all x1, blocking collectives: 29.5 us -> 41.7 us  [shards(): held = lax.all_to_all(sent, BLOCK, 0, 0)]
    ppermute x1 -> x5, waiting for transfers between devices: 0.01 us -> 9.86 us  [the longest x3 8.87 us: shards(): lax.ppermute(rates, 'x', [(i, (i + hop) % 4) for i in range(4)])]
    ppermute x1 -> x5, starting transfers between devices: 4 us -> 11.7 us  [the longest x1 5.04 us: shards(): lax.ppermute(part, 'c', swap)]
    ppermute x1, waiting for transfers between devices: 14.6 us -> 8.07 us  [shards(): a_0 = lax.ppermute(a_next, SEQ, down)]
    all_to_all x1, blocking collectives: 19.8 us -> 26.1 us  [shards(): back = lax.all_to_all(scanned, BLOCK, 0, 0)]
  transfers between devices with their start and end apart: 13 -> 18, of which waited for: 4 -> 11; matrix products, arithmetic and copies ran while one was open for 0% -> 0% of each run, Pallas kernels for 9% -> 9%
where the time goes in v3:
time: 243 us; the launch traced here: 241 us
  blocking collectives  90.9 us (37%)
  starting transfers between devices  62.8 us (26%)
  waiting for transfers between devices  39.4 us (16%)
  Pallas kernels  31.4 us (13%)
  local copies, waits for them, and re-layouts  15.3 us (6%)
    all_to_all x1, blocking collectives, shards(): held = lax.all_to_all(sent, BLOCK, 0, 0)  41.7 us
    all_to_all x1, blocking collectives, shards(): back = lax.all_to_all(scanned, BLOCK, 0, 0)  26.1 us
    all_to_all x1, starting transfers between devices, shards(): over_xy = lax.all_to_all(weight, ('x', 'y'), 0, 0)  14.8 us
    unnamed x86, local copies, waits for them, and re-layouts  14.6 us
    all_to_all x1, blocking collectives, shards(): last = lax.all_to_all(summed, ('y', 'c'), 0, 0)  12 us
    all_to_all x1, blocking collectives, shards(): lax.all_to_all(folded, ('quad', 'turn'), 0, 0)  11 us
    ppermute x2, starting transfers between devices, shards(): lax.ppermute(advance('gather_s', gather_step_kernel, k, k)(rows, got_s, r...  11 us
    ppermute x3, waiting for transfers between devices, shards(): lax.ppermute(rates, 'x', [(i, (i + hop) % 4) for i in range(4)])  8.87 us
  transfers between devices with their start and end apart: 18, of which 11 were waited for; matrix products, arithmetic and copies ran while one was open for 0% of the time, Pallas kernels for 9%

profile of v3, /device:TPU:1, one launch (start us, length us, event | category | flops | bytes accessed | tf_op | source)
XLA Modules:
  0.0 241.4 jit_solution(3354890982025864108)
XLA Ops:
  2.1 3.9 %project.1 = (bf16[128,256]{1,0:T(8,128)(2,1)S(1)}, f32[128,64]{1,0:T(8,128)S(1)}, f32[128,64]{1,0:T(8,128)S(1)}, f32[32,128]{1,0:T(8,128)S(1)}, bf16[128,4096]{1,0:T(8,128)(2,1)S(1)}, /*index=5*/f32[1032,128]{1,0:T(8,128)S(1)}) custom-call(s32[1]{0:T(128)} %bitcast.turn_ref, f32[64,128]{1,0:T(8,128)S(1)} %bitcast.26, f32[1,64]{1,0:T(1,128)S(1)} %bitcast.28, ...), custom_call_target="tpu_custom_call" | custom-call | flops 400000000 | bytes 6291456 | tf_op jit(solution)/shard_map/project/pallas_call | solution.py:433
  8.7 5.0 %collective-permute-start = (f32[1032,128]{1,0:T(8,128)S(1)}, f32[1032,128]{1,0:T(8,128)S(1)}, u32[]{:S(2)}, u32[]{:S(2)}) collective-permute-start(f32[1032,128]{1,0:T(8,128)S(1)} %get-tuple-element.66.local), channel_id=1, source_target_pairs={{0,8},{8,16},{16,24},{24,32},{32,40},{40,48},{48,56},{56,64},{64,7... | collective-permute-start | bytes 1585160 | tf_op jit(solution)/shard_map/ppermute | solution.py:456
  15.2 6.4 %collective-permute-done.3.got = f32[1032,128]{1,0:T(8,128)S(1)} collective-permute-done((f32[1032,128]{1,0:T(8,128)S(1)}, f32[1032,128]{1,0:T(8,128)S(1)}, u32[]{:S(2)}, u32[]{:S(2)}) %collective-permute-start.3) | collective-permute-done | bytes 528416 | tf_op jit(solution)/shard_map/ppermute | solution.py:466
  24.6 6.8 %collective-permute-start.1 = (f32[1032,128]{1,0:T(8,128)}, f32[1032,128]{1,0:T(8,128)}, u32[]{:S(2)}, u32[]{:S(2)}) collective-permute-start(f32[1032,128]{1,0:T(8,128)} %gather_s.2), channel_id=1, source_target_pairs={{0,8},{8,16},{16,24},{24,32},{32,40},{40,48},{48,56},{56,64},{64,7... | collective-permute-start | bytes 1585160 | tf_op jit(solution)/shard_map/ppermute | solution.py:539
  34.8 4.2 %collective-permute-done.4.got = f32[1032,128]{1,0:T(8,128)} collective-permute-done((f32[1032,128]{1,0:T(8,128)}, f32[1032,128]{1,0:T(8,128)}, u32[]{:S(2)}, u32[]{:S(2)}) %collective-permute-start.4) | collective-permute-done | bytes 528416 | tf_op jit(solution)/shard_map/ppermute | solution.py:540
  42.5 4.2 %collective-permute-start.2 = (f32[1032,128]{1,0:T(8,128)S(1)}, f32[1032,128]{1,0:T(8,128)S(1)}, u32[]{:S(2)}, u32[]{:S(2)}) collective-permute-start(f32[1032,128]{1,0:T(8,128)S(1)} %gather_s.3), channel_id=1, source_target_pairs={{0,8},{8,16},{16,24},{24,32},{32,40},{40,48},{48,56},{56,64},{64,7... | collective-permute-start | bytes 1585160 | tf_op jit(solution)/shard_map/ppermute | solution.py:539
  46.8 8.0 %intra.1 = (f32[128,4096]{1,0:T(8,128)S(1)}, f32[64,128]{1,0:T(8,128)S(1)}, f32[8,128,8]{2,1,0:T(8,128)S(1)}, f32[128,128]{1,0:T(8,128)S(1)}) custom-call(s32[1]{0:T(128)} %bitcast.turn_ref, bf16[128,256]{1,0:T(8,128)(2,1)S(1)} %get-tuple-element.59.bc, f32[8,128,8]{2,1,0:T(8,128)S(1)} %copy-done.28, f32[8,128,8]{2,1,0:T(8,128)S(1)} %copy-done.30, ...), custom_call_target="tpu_custom_call" | custom-call | flops 800000000 | bytes 20971520 | tf_op jit(solution)/shard_map/intra/pallas_call | solution.py:508
  55.9 41.7 %all_to_all.25.msg = f32[8,264,128]{2,1,0:T(8,128)S(1)} all-to-all(f32[8,264,128]{2,1,0:T(8,128)S(1)} %combine.1), channel_id=1, replica_groups=mesh['x'=4,'quad'=2,'turn'=4,'y'=4,'c'=2] {'x','quad'}, dimensions={0} | all-to-all | bytes 2162688 | tf_op jit(solution)/shard_map/all_to_all | solution.py:552
  97.7 26.1 %all_to_all.26.back = f32[8,256,128]{2,1,0:T(8,128)S(1)} all-to-all(f32[8,256,128]{2,1,0:T(8,128)S(1)} %scan.1), channel_id=1, replica_groups=mesh['x'=4,'quad'=2,'turn'=4,'y'=4,'c'=2] {'x','quad'}, dimensions={0} | all-to-all | bytes 2097152 | tf_op jit(solution)/shard_map/all_to_all | solution.py:562
  125.5 4.0 %collective-permute-start.7 = (f32[1024,128]{1,0:T(8,128)S(1)}, f32[1024,128]{1,0:T(8,128)S(1)}, u32[]{:S(2)}, u32[]{:S(2)}) collective-permute-start(f32[1024,128]{1,0:T(8,128)S(1)} %get-tuple-element.76), channel_id=1, source_target_pairs={{0,8},{8,16},{16,24},{24,32},{32,40},{40,48},{48,56},{56,64},{64,7... | collective-permute-start | bytes 1572872 | tf_op jit(solution)/shard_map/ppermute | solution.py:572
  129.5 8.1 %collective-permute-done.10.state.a_0.a_2 = f32[1024,128]{1,0:T(8,128)S(1)} collective-permute-done((f32[1024,128]{1,0:T(8,128)S(1)}, f32[1024,128]{1,0:T(8,128)S(1)}, u32[]{:S(2)}, u32[]{:S(2)}) %collective-permute-start.10) | collective-permute-done | bytes 524320 | tf_op jit(solution)/shard_map/ppermute | solution.py:573
  139.1 4.2 %collective-permute-start.8 = (f32[1024,128]{1,0:T(8,128)S(1)}, f32[1024,128]{1,0:T(8,128)S(1)}, u32[]{:S(2)}, u32[]{:S(2)}) collective-permute-start(f32[1024,128]{1,0:T(8,128)S(1)} %spread_s.2), channel_id=1, source_target_pairs={{0,8},{8,16},{16,24},{24,32},{32,40},{40,48},{48,56},{56,64},{64,7... | collective-permute-start | bytes 1572872 | tf_op jit(solution)/shard_map/ppermute | solution.py:602
  143.2 6.9 %collective-permute-done.11.state.a_1.a_in = f32[1024,128]{1,0:T(8,128)S(1)} collective-permute-done((f32[1024,128]{1,0:T(8,128)S(1)}, f32[1024,128]{1,0:T(8,128)S(1)}, u32[]{:S(2)}, u32[]{:S(2)}) %collective-permute-start.11) | collective-permute-done | bytes 524320 | tf_op jit(solution)/shard_map/ppermute | solution.py:603
  151.6 4.2 %collective-permute-start.9 = (f32[1024,128]{1,0:T(8,128)S(1)}, f32[1024,128]{1,0:T(8,128)S(1)}, u32[]{:S(2)}, u32[]{:S(2)}) collective-permute-start(f32[1024,128]{1,0:T(8,128)S(1)} %spread_s.3), channel_id=1, source_target_pairs={{0,8},{8,16},{16,24},{24,32},{32,40},{40,48},{48,56},{56,64},{64,7... | collective-permute-start | bytes 1572872 | tf_op jit(solution)/shard_map/ppermute | solution.py:604
  159.1 1.9 outer.2
  163.2 5.0 %collective-permute-start.13 = (f32[128,256]{1,0:T(8,128)S(1)}, f32[128,256]{1,0:T(8,128)S(1)}, u32[]{:S(2)}, u32[]{:S(2)}) collective-permute-start(f32[128,256]{1,0:T(8,128)S(1)} %far.1.mine), channel_id=1, source_target_pairs={{0,1},{1,0},{2,3},{3,2},{4,5},{5,4},{6,7},{7,6},{8,9},{9,8},{10,11... | collective-permute-start | bytes 393224 | tf_op jit(solution)/shard_map/ppermute | solution.py:634
  171.4 14.8 %all-to-all-start.2 = ((f32[16,128,256]{2,1,0:T(8,128)}), f32[16,128,256]{2,1,0:T(8,128)}, u32[]{:S(2)}, u32[]{:S(2)}) async-start(f32[16,128,256]{2,1,0:T(8,128)} %copy-done.11), calls=%async_computation.2 | async-start | bytes 4194304 | tf_op jit(solution)/shard_map/all_to_all | solution.py:636
  195.2 4.3 %finish.1 = (bf16[128,4096]{1,0:T(8,128)(2,1)}, f32[64,128]{1,0:T(8,128)}, f32[8,256]{1,0:T(8,128)S(1)}) custom-call(s32[1]{0:T(128)} %bitcast.turn_ref, f32[1024,128]{1,0:T(8,128)S(1)} %copy-done.15, f32[1024,128]{1,0:T(8,128)S(1)} %copy-done.18, f32[1024,128]{1,0:T(8,128)S(1)} %copy-done.20, f32[1024,128]{1,0:T(8,128)S(1)} %copy-done.13, ...), custom_call_target="tpu_custom_call" | custom-call | flops 500000000 | bytes 6291456 | tf_op jit(solution)/shard_map/finish/pallas_call | solution.py:637
  200.8 2.4 collective-permute-start.15
  204.4 6.3 %collective-permute-done.14.one = f32[8,256]{1,0:T(8,128)S(1)} collective-permute-done((f32[8,256]{1,0:T(8,128)S(1)}, f32[8,256]{1,0:T(8,128)S(1)}, u32[]{:S(2)}, u32[]{:S(2)}) %collective-permute-start.14) | collective-permute-done | bytes 8224 | tf_op jit(solution)/shard_map/ppermute | solution.py:647
  210.7 2.6 %collective-permute-done.15.two = f32[8,256]{1,0:T(8,128)S(1)} collective-permute-done((f32[8,256]{1,0:T(8,128)S(1)}, f32[8,256]{1,0:T(8,128)S(1)}, u32[]{:S(2)}, u32[]{:S(2)}) %collective-permute-start.15) | collective-permute-done | bytes 8224 | tf_op jit(solution)/shard_map/ppermute | solution.py:647
  213.3 2.2 all-to-all-done.2.msg
  217.1 11.0 %all_to_all.27.msg = f32[8,24,256]{2,1,0:T(8,128)S(1)} all-to-all(f32[8,24,256]{2,1,0:T(8,128)S(1)} %fold.1), channel_id=1, replica_groups=mesh['x'=4,'quad'=2,'turn'=4,'y'=4,'c'=2] {'quad','turn'}, dimensions={0} | all-to-all | bytes 393216 | tf_op jit(solution)/shard_map/all_to_all | solution.py:665
  228.2 12.0 %all_to_all.28 = f32[8,24,256]{2,1,0:T(8,128)S(1)} all-to-all(f32[8,24,256]{2,1,0:T(8,128)S(1)} %last.1), channel_id=1, replica_groups=mesh['x'=4,'quad'=2,'turn'=4,'y'=4,'c'=2] {'y','c'}, dimensions={0} | all-to-all | bytes 393216 | tf_op jit(solution)/shard_map/all_to_all | solution.py:666
  (130 shorter events, 44.0 us)
Async XLA Ops:
  6.0 16.4 %copy-start.7 = (bf16[128,4096]{1,0:T(8,128)(2,1)}, bf16[128,4096]{1,0:T(8,128)(2,1)S(1)}, u32[]{:S(2)}) copy-start(bf16[128,4096]{1,0:T(8,128)(2,1)S(1)} %get-tuple-element.62.xw) | copy-start | bytes 3145732
  7.4 14.2 %collective-permute-start.3 = (f32[1032,128]{1,0:T(8,128)S(1)}, f32[1032,128]{1,0:T(8,128)S(1)}, u32[]{:S(2)}, u32[]{:S(2)}) collective-permute-start(f32[1032,128]{1,0:T(8,128)S(1)} %get-tuple-element.67.local), channel_id=1, source_target_pairs={{8,0},{16,8},{24,16},{32,24},{40,32},{48,40},{56,48},{64,56},{72,6... | collective-permute-start | bytes 1585160 | tf_op jit(solution)/shard_map/ppermute | solution.py:466
  8.7 15.1 %collective-permute-start = (f32[1032,128]{1,0:T(8,128)S(1)}, f32[1032,128]{1,0:T(8,128)S(1)}, u32[]{:S(2)}, u32[]{:S(2)}) collective-permute-start(f32[1032,128]{1,0:T(8,128)S(1)} %get-tuple-element.66.local), channel_id=1, source_target_pairs={{0,8},{8,16},{16,24},{24,32},{32,40},{40,48},{48,56},{56,64},{64,7... | collective-permute-start | bytes 1585160 | tf_op jit(solution)/shard_map/ppermute | solution.py:456
  22.4 16.6 %collective-permute-start.4 = (f32[1032,128]{1,0:T(8,128)}, f32[1032,128]{1,0:T(8,128)}, u32[]{:S(2)}, u32[]{:S(2)}) collective-permute-start(f32[1032,128]{1,0:T(8,128)} %gather_a.2), channel_id=1, source_target_pairs={{8,0},{16,8},{24,16},{32,24},{40,32},{48,40},{56,48},{64,56},{72,6... | collective-permute-start | bytes 1585160 | tf_op jit(solution)/shard_map/ppermute | solution.py:540
  24.6 16.8 %collective-permute-start.1 = (f32[1032,128]{1,0:T(8,128)}, f32[1032,128]{1,0:T(8,128)}, u32[]{:S(2)}, u32[]{:S(2)}) collective-permute-start(f32[1032,128]{1,0:T(8,128)} %gather_s.2), channel_id=1, source_target_pairs={{0,8},{8,16},{16,24},{24,32},{32,40},{40,48},{48,56},{56,64},{64,7... | collective-permute-start | bytes 1585160 | tf_op jit(solution)/shard_map/ppermute | solution.py:539
  33.0 22.6 %collective-permute-start.6 = (f32[2048,128]{1,0:T(8,128)S(1)}, f32[2048,128]{1,0:T(8,128)S(1)}, u32[]{:S(2)}, u32[]{:S(2)}) collective-permute-start(f32[2048,128]{1,0:T(8,128)S(1)} %get-tuple-element.73), channel_id=1, source_target_pairs={{0,1},{1,0},{2,3},{3,2},{4,5},{5,4},{6,7},{7,6},{8,9},{9,8},{10,11... | collective-permute-start | bytes 3145736 | tf_op jit(solution)/shard_map/ppermute | solution.py:501
  40.1 15.6 %collective-permute-start.5 = (f32[1032,128]{1,0:T(8,128)S(1)}, f32[1032,128]{1,0:T(8,128)S(1)}, u32[]{:S(2)}, u32[]{:S(2)}) collective-permute-start(f32[1032,128]{1,0:T(8,128)S(1)} %gather_a.3), channel_id=1, source_target_pairs={{8,0},{16,8},{24,16},{32,24},{40,32},{48,40},{56,48},{64,56},{72,6... | collective-permute-start | bytes 1585160 | tf_op jit(solution)/shard_map/ppermute | solution.py:540
  42.5 13.3 %collective-permute-start.2 = (f32[1032,128]{1,0:T(8,128)S(1)}, f32[1032,128]{1,0:T(8,128)S(1)}, u32[]{:S(2)}, u32[]{:S(2)}) collective-permute-start(f32[1032,128]{1,0:T(8,128)S(1)} %gather_s.3), channel_id=1, source_target_pairs={{0,8},{8,16},{16,24},{24,32},{32,40},{40,48},{48,56},{56,64},{64,7... | collective-permute-start | bytes 1585160 | tf_op jit(solution)/shard_map/ppermute | solution.py:539
  55.6 103.5 %copy-start.5 = (f32[128,4096]{1,0:T(8,128)}, f32[128,4096]{1,0:T(8,128)S(1)}, u32[]{:S(2)}) copy-start(f32[128,4096]{1,0:T(8,128)S(1)} %get-tuple-element.82.u) | copy-start | bytes 6291460
  124.0 13.5 %collective-permute-start.10 = (f32[1024,128]{1,0:T(8,128)S(1)}, f32[1024,128]{1,0:T(8,128)S(1)}, u32[]{:S(2)}, u32[]{:S(2)}) collective-permute-start(f32[1024,128]{1,0:T(8,128)S(1)} %get-tuple-element.79), channel_id=1, source_target_pairs={{8,0},{16,8},{24,16},{32,24},{40,32},{48,40},{56,48},{64,56},{72,6... | collective-permute-start | bytes 1572872 | tf_op jit(solution)/shard_map/ppermute | solution.py:573
  125.5 13.5 %collective-permute-start.7 = (f32[1024,128]{1,0:T(8,128)S(1)}, f32[1024,128]{1,0:T(8,128)S(1)}, u32[]{:S(2)}, u32[]{:S(2)}) collective-permute-start(f32[1024,128]{1,0:T(8,128)S(1)} %get-tuple-element.76), channel_id=1, source_target_pairs={{0,8},{8,16},{16,24},{24,32},{32,40},{40,48},{48,56},{56,64},{64,7... | collective-permute-start | bytes 1572872 | tf_op jit(solution)/shard_map/ppermute | solution.py:572
  137.6 20.7 %copy-start.12 = (f32[1024,128]{1,0:T(8,128)}, f32[1024,128]{1,0:T(8,128)S(1)}, u32[]{:S(2)}) copy-start(f32[1024,128]{1,0:T(8,128)S(1)} %collective-permute-done.10.state.a_0.a_2) | copy-start | bytes 1572868
  137.6 12.5 %collective-permute-start.11 = (f32[1024,128]{1,0:T(8,128)S(1)}, f32[1024,128]{1,0:T(8,128)S(1)}, u32[]{:S(2)}, u32[]{:S(2)}) collective-permute-start(f32[1024,128]{1,0:T(8,128)S(1)} %spread_a.2), channel_id=1, source_target_pairs={{8,0},{16,8},{24,16},{32,24},{40,32},{48,40},{56,48},{64,56},{72,6... | collective-permute-start | bytes 1572872 | tf_op jit(solution)/shard_map/ppermute | solution.py:603
  139.0 19.3 %copy-start.14 = (f32[1024,128]{1,0:T(8,128)}, f32[1024,128]{1,0:T(8,128)S(1)}, u32[]{:S(2)}) copy-start(f32[1024,128]{1,0:T(8,128)S(1)} %collective-permute-done.7.state.s_0) | copy-start | bytes 1572868
  139.0 16.7 %copy-start.8 = (bf16[128,4096]{1,0:T(8,128)(2,1)S(1)}, bf16[128,4096]{1,0:T(8,128)(2,1)}, u32[]{:S(2)}) copy-start(bf16[128,4096]{1,0:T(8,128)(2,1)} %copy-done.7) | copy-start | bytes 3145732
  139.1 16.7 %copy-start.10 = (bf16[128,4096]{1,0:T(8,128)(2,1)S(1)}, bf16[128,4096]{1,0:T(8,128)(2,1)}, u32[]{:S(2)}) copy-start(bf16[128,4096]{1,0:T(8,128)(2,1)} %copy-done.9) | copy-start | bytes 3145732
  139.1 12.4 %collective-permute-start.8 = (f32[1024,128]{1,0:T(8,128)S(1)}, f32[1024,128]{1,0:T(8,128)S(1)}, u32[]{:S(2)}, u32[]{:S(2)}) collective-permute-start(f32[1024,128]{1,0:T(8,128)S(1)} %spread_s.2), channel_id=1, source_target_pairs={{0,8},{8,16},{16,24},{24,32},{32,40},{40,48},{48,56},{56,64},{64,7... | collective-permute-start | bytes 1572872 | tf_op jit(solution)/shard_map/ppermute | solution.py:602
  150.2 11.6 %collective-permute-start.12 = (f32[1024,128]{1,0:T(8,128)S(1)}, f32[1024,128]{1,0:T(8,128)S(1)}, u32[]{:S(2)}, u32[]{:S(2)}) collective-permute-start(f32[1024,128]{1,0:T(8,128)S(1)} %spread_a.3), channel_id=1, source_target_pairs={{8,0},{16,8},{24,16},{32,24},{40,32},{48,40},{56,48},{64,56},{72,6... | collective-permute-start | bytes 1572872 | tf_op jit(solution)/shard_map/ppermute | solution.py:605
  151.6 11.2 %collective-permute-start.9 = (f32[1024,128]{1,0:T(8,128)S(1)}, f32[1024,128]{1,0:T(8,128)S(1)}, u32[]{:S(2)}, u32[]{:S(2)}) collective-permute-start(f32[1024,128]{1,0:T(8,128)S(1)} %spread_s.3), channel_id=1, source_target_pairs={{0,8},{8,16},{16,24},{24,32},{32,40},{40,48},{48,56},{56,64},{64,7... | collective-permute-start | bytes 1572872 | tf_op jit(solution)/shard_map/ppermute | solution.py:604
  163.2 6.0 %collective-permute-start.13 = (f32[128,256]{1,0:T(8,128)S(1)}, f32[128,256]{1,0:T(8,128)S(1)}, u32[]{:S(2)}, u32[]{:S(2)}) collective-permute-start(f32[128,256]{1,0:T(8,128)S(1)} %far.1.mine), channel_id=1, source_target_pairs={{0,1},{1,0},{2,3},{3,2},{4,5},{5,4},{6,7},{7,6},{8,9},{9,8},{10,11... | collective-permute-start | bytes 393224 | tf_op jit(solution)/shard_map/ppermute | solution.py:634
  171.4 44.1 %all-to-all-start.2 = ((f32[16,128,256]{2,1,0:T(8,128)}), f32[16,128,256]{2,1,0:T(8,128)}, u32[]{:S(2)}, u32[]{:S(2)}) async-start(f32[16,128,256]{2,1,0:T(8,128)} %copy-done.11), calls=%async_computation.2 | async-start | bytes 4194304 | tf_op jit(solution)/shard_map/all_to_all | solution.py:636
  199.5 11.2 %collective-permute-start.14 = (f32[8,256]{1,0:T(8,128)S(1)}, f32[8,256]{1,0:T(8,128)S(1)}, u32[]{:S(2)}, u32[]{:S(2)}) collective-permute-start(f32[8,256]{1,0:T(8,128)S(1)} %get-tuple-element.111.rates), channel_id=1, source_target_pairs={{0,64},{64,128},{128,192},{192,0},{1,65},{65,129},{129,193},{193,1... | collective-permute-start | bytes 24584 | tf_op jit(solution)/shard_map/ppermute | solution.py:647
  200.8 12.5 %collective-permute-start.15 = (f32[8,256]{1,0:T(8,128)S(1)}, f32[8,256]{1,0:T(8,128)S(1)}, u32[]{:S(2)}, u32[]{:S(2)}) collective-permute-start(f32[8,256]{1,0:T(8,128)S(1)} %get-tuple-element.111.rates), channel_id=1, source_target_pairs={{0,128},{64,192},{128,0},{192,64},{1,129},{65,193},{129,1},{193,65... | collective-permute-start | bytes 24584 | tf_op jit(solution)/shard_map/ppermute | solution.py:647
  203.2 10.0 %collective-permute-start.16 = (f32[8,256]{1,0:T(8,128)S(1)}, f32[8,256]{1,0:T(8,128)S(1)}, u32[]{:S(2)}, u32[]{:S(2)}) collective-permute-start(f32[8,256]{1,0:T(8,128)S(1)} %get-tuple-element.111.rates), channel_id=1, source_target_pairs={{0,192},{64,0},{128,64},{192,128},{1,193},{65,1},{129,65},{193,129... | collective-permute-start | bytes 24584 | tf_op jit(solution)/shard_map/ppermute | solution.py:647
  (37 other events, 272.2 us)

commit v4 on v3

--- a/solution.py
+++ b/solution.py
@@ -102,21 +102,20 @@
     )
 
 
-def turn_kernel(core_ref, tok, mine, other):
-    first = core_ref[0] == 0
+def turn_kernel(place_ref, tok, *refs):
+    y, core = place_ref[1], place_ref[2]
+    outs, held = refs[:8], refs[8]
     for i in range(32):
-        part = tok[:, tile(i)].astype(F32).T
-        x, z = divmod(i, 8)
-        for y in range(4):
-            one = part[32 * y : 32 * y + 16, :]
-            two = part[32 * y + 16 : 32 * y + 32, :]
-            rows = slice(512 * x + 128 * y + 16 * z, 512 * x + 128 * y + 16 * z + 16)
-            mine[rows, :] = jnp.where(first, one, two).astype(BF)
-            other[rows, :] = jnp.where(first, two, one)
-
-
-def narrow_kernel(wide, out):
-    out[...] = wide[...].astype(BF)
+        held[...] = tok[:, tile(i)].astype(F32).T
+        for hop in range(4):
+            for side in range(2):
+                start = lax.rem(y + hop, 4) * 32 + lax.rem(core + side, 2) * 16
+                outs[4 * side + hop][16 * i : 16 * i + 16, :] = held[pl.ds(pl.multiple_of(start, 16), 16), :]
+
+
+def narrow_kernel(*refs):
+    for k in range(8):
+        refs[8][k] = refs[k][...].astype(BF)
 
 
 def project_kernel(
@@ -366,24 +365,21 @@
     out[:, 128:] = grad_c.astype(BF).astype(F32)
 
 
-def weight_kernel(tok_mine, tok_got, mine, got, msg):
-    here, there = mine[...].astype(BF), got[...].astype(BF)
-    for k in range(16):
-        msg[k] = dot(tok_mine[tile(k), :], here) + dot(tok_got[tile(k), :], there)
-
-
-def fold_kernel(msg, rates, one, two, three, out):
-    total = msg[0]
-    for k in range(1, 16):
-        total = total + msg[k]
-    for z in range(8):
-        out[z, 0:16, :] = total[16 * z : 16 * z + 16, :]
-        out[z, 16:24, :] = rates[...] + one[...] + two[...] + three[...]
+def weight_kernel(tok, *refs):
+    grads, rates, msg = refs[:8], refs[8], refs[9]
+    total = jnp.zeros((512, 256), F32)
+    for k in range(8):
+        total = total + dot(tok[k], grads[k][...].astype(BF))
+    for i in range(32):
+        rows = slice(16 * i, 16 * i + 16)
+        msg[i, 0:16, :] = total[rows, 0:128]
+        msg[i, 16:32, :] = total[rows, 128:256]
+        msg[i, 32:40, :] = rates[...]
 
 
 def last_kernel(msg, out):
     total = msg[0]
-    for k in range(1, 8):
+    for k in range(1, 32):
         total = total + msg[k]
     for k in range(8):
         out[k] = total
@@ -417,16 +413,17 @@
     ddt = turned(role_s / dt + outer, turn) - rate[...] * turned(da, turn)
     step_ref[...] = ddt.T / (1.0 + jnp.exp(-logit[...]))
     rate_row = turned(-jnp.sum(dt * da, axis=0, keepdims=True), turn)
-    wide = jnp.concatenate([rate_row, jnp.zeros((1, 256 - HEADS), F32)], axis=1)
-    rate_ref[...] = jnp.broadcast_to(wide, (8, 256))
+    wide = jnp.concatenate([rate_row, jnp.zeros((1, 128 - HEADS), F32)], axis=1)
+    rate_ref[...] = jnp.broadcast_to(wide, (8, 128))
 
 
 def shards(layer_input, projection, ssm_input, step_logit, decay_rate, output_grad):
     tok, x, g, logit = layer_input[0], ssm_input[0], output_grad[0], step_logit[0].T
     rate = decay_rate[None, :]
     width = x.shape[1]
-    turn = lax.axis_index("turn").astype(jnp.int32)[None]
-    core = lax.axis_index("c").astype(jnp.int32)[None]
+    turn = jnp.stack([lax.axis_index(name) for name in ("turn", "y", "c")]).astype(jnp.int32)
+    swap = [(0, 1), (1, 0)]
+    around = [[(i, (i + hop) % 4) for i in range(4)] for hop in range(4)]
     up = [(i, i + 1) for i in range(31)]
     down = [(i + 1, i) for i in range(31)]
 
@@ -480,25 +477,18 @@
         out_specs=(VMEM,) * 5,
         name="rest",
     )(turn, bc, c, dt, xw, gw)
-    tok_mine, tok_other = call(
+    columns = call(
         turn_kernel,
-        (shape(width // 2, ROWS, dtype=BF), shape(width // 2, ROWS)),
+        (shape(512, ROWS),) * 8,
         1_000_000,
         3 << 20,
         in_specs=[SMEM, VMEM],
-        out_specs=(VMEM,) * 2,
+        out_specs=(VMEM,) * 8,
+        scratch_shapes=[pltpu.VMEM((ROWS, ROWS), F32)],
         name="turn",
-    )(core, tok)
-    swap = [(0, 1), (1, 0)]
-    tok_got = call(
-        narrow_kernel,
-        shape(width // 2, ROWS, dtype=BF),
-        1_000_000,
-        2 << 20,
-        in_specs=[VMEM],
-        out_specs=VMEM,
-        name="narrow",
-    )(lax.ppermute(tok_other, "c", swap))
+    )(turn, tok)
+    tok_mine = columns[:4]
+    tok_swapped = [lax.ppermute(piece, "c", swap) for piece in columns[4:]]
 
     wide = GROUP * 64
 
@@ -535,10 +525,15 @@
         ),
         name="intra",
     )(turn, bc, cg, dtg, ct, x, g)
+    got_s, got_a, *tok_swapped = lax.optimization_barrier((got_s, got_a, *tok_swapped))
     for k in (1, 2):
         got_s = lax.ppermute(advance("gather_s", gather_step_kernel, k, k)(rows, got_s, rest_s), SEQ, up)
         got_a = lax.ppermute(advance("gather_a", gather_step_kernel, MIRROR[k], k)(rows, got_a, rest_a), SEQ, down)
-    got_s, got_a, u, tok_mine, tok_got = lax.optimization_barrier((got_s, got_a, u, tok_mine, tok_got))
+    got_s, got_a, u = lax.optimization_barrier((got_s, got_a, u))
+
+    def columns_from(hop, after):
+        one, two, _ = lax.optimization_barrier((tok_mine[hop], tok_swapped[hop], after))
+        return [lax.ppermute(one, "y", around[hop]), lax.ppermute(two, "y", around[hop])]
 
     sent = call(
         combine_kernel,
@@ -549,7 +544,9 @@
         out_specs=VMEM,
         name="combine",
     )(rows, rest_s, rest_a, got_s, got_a)
+    near_columns = columns_from(1, sent) + columns_from(3, sent)
     held = lax.all_to_all(sent, BLOCK, 0, 0)
+    held, *near_columns = lax.optimization_barrier((held, *near_columns))
     scanned = call(
         scan_kernel,
         shape(PAIRS, 256, 128),
@@ -559,7 +556,10 @@
         out_specs=VMEM,
         name="scan",
     )(held)
+    far_columns = columns_from(2, scanned)
     back = lax.all_to_all(scanned, BLOCK, 0, 0)
+    back, *far_columns = lax.optimization_barrier((back, *far_columns))
+    tok_got = [tok_mine[0], tok_swapped[0], *near_columns[:2], *far_columns, *near_columns[2:]]
     s_next, a_next = call(
         unfold_kernel,
         (shape(TILE, 128),) * 2,
@@ -599,6 +599,15 @@
         )(turn, state, adj, x, g, u, c, dt, bc)
 
     own = outer_part(3, s_own, a_own)
+    all_tok = call(
+        narrow_kernel,
+        shape(8, 512, ROWS, dtype=BF),
+        1_000_000,
+        3 << 20,
+        in_specs=[VMEM] * 8,
+        out_specs=VMEM,
+        name="narrow",
+    )(*tok_got)
     s_1 = lax.ppermute(advance("spread_s", spread_step_kernel, 0)(rows, s_0, send_s), SEQ, up)
     a_1 = lax.ppermute(advance("spread_a", spread_step_kernel, MIRROR[0])(rows, a_0, send_a), SEQ, down)
     s_2 = lax.ppermute(advance("spread_s", spread_rest_kernel, 1)(rows, s_1, rest_s), SEQ, up)
@@ -613,7 +622,7 @@
         name="middle",
     )(turn, s_0, a_0, s_1, a_1, xw, gw, near)
     one = outer_part(1, s_1, a_1)
-    s_2, a_2, middle, one, own = lax.optimization_barrier((s_2, a_2, middle, one, own))
+    s_2, a_2, middle, one, own, all_tok = lax.optimization_barrier((s_2, a_2, middle, one, own, all_tok))
     part = call(
         far_kernel,
         shape(ROWS, 256),
@@ -623,20 +632,11 @@
         out_specs=VMEM,
         name="far",
     )(turn, s_2, a_2, xw, gw, middle)
-    weight = call(
-        weight_kernel,
-        shape(16, 128, 256),
-        300_000_000,
-        4 << 20,
-        in_specs=[VMEM] * 4,
-        out_specs=VMEM,
-        name="weight",
-    )(tok_mine, tok_got, part, lax.ppermute(part, "c", swap))
-    weight, s_2, a_2 = lax.optimization_barrier((weight, s_2, a_2))
-    over_xy = lax.all_to_all(weight, ("x", "y"), 0, 0)
+    mine = [part] + [lax.ppermute(part, "y", around[hop]) for hop in (1, 2, 3)]
+    other = [lax.ppermute(piece, "c", swap) for piece in mine]
     gx, step_grad, rates = call(
         finish_kernel,
-        (shape(ROWS, width, dtype=BF), shape(HEADS, ROWS), shape(8, 256)),
+        (shape(ROWS, width, dtype=BF), shape(HEADS, ROWS), shape(8, 128)),
         500_000_000,
         6 << 20,
         in_specs=[SMEM] + [VMEM] * 22,
@@ -644,28 +644,28 @@
         scratch_shapes=[pltpu.VMEM((PAIRS, 128), F32)],
         name="finish",
     )(turn, s_0, a_2, s_2, a_0, x, g, u, c, dt, bc, *one, *own, t_rows, s_cols, logit, rate)
-    far_rates = [lax.ppermute(rates, "x", [(i, (i + hop) % 4) for i in range(4)]) for hop in (1, 2, 3)]
-    folded = call(
-        fold_kernel,
-        shape(8, 24, 256),
-        1_000_000,
-        2 << 20,
-        in_specs=[VMEM] * 5,
-        out_specs=VMEM,
-        name="fold",
-    )(over_xy, rates, *far_rates)
+    grads = [piece for pair in zip(mine, other) for piece in pair]
+    weight = call(
+        weight_kernel,
+        shape(32, 40, 128),
+        300_000_000,
+        3 << 20,
+        in_specs=[VMEM] * 10,
+        out_specs=VMEM,
+        name="weight",
+    )(all_tok, *grads, rates)
     summed = call(
         last_kernel,
-        shape(8, 24, 256),
+        shape(8, 40, 128),
         1_000_000,
         1 << 20,
         in_specs=[VMEM],
         out_specs=VMEM,
         name="last",
-    )(lax.all_to_all(folded, ("quad", "turn"), 0, 0))
+    )(lax.all_to_all(weight, SEQ, 0, 0))
     last = lax.all_to_all(summed, ("y", "c"), 0, 0)
-    rate_grad = jnp.sum(last[:, 16, :HEADS], axis=0)
-    return gx[None], step_grad.T[None], rate_grad, last[:, :16].reshape(ROWS, 256)
+    full = jnp.concatenate([last[:, :16].reshape(ROWS, 128), last[:, 16:32].reshape(ROWS, 128)], axis=1)
+    return gx[None], step_grad.T[None], jnp.sum(last[:, 32, :HEADS], axis=0), full
 
 
 def solution(mesh):

time: 243 us -> 240 us (0.988)
  blocking collectives: 90.9 us -> 36.4 us
  starting transfers between devices: 62.8 us -> 93.4 us
  waiting for transfers between devices: 39.4 us -> 54.7 us
  Pallas kernels: 31.4 us -> 35.6 us
    all_to_all x3 -> x1, blocking collectives: 78.9 us -> 24.1 us  [shards(): lax.all_to_all(weight, SEQ, 0, 0)]
    ppermute x1, starting transfers between devices: 4.15 us -> 19.2 us  [shards(): lax.ppermute(advance('spread_s', spread_step_kernel, 0)(rows, s_0, send_s...]
    ppermute x5 -> x17, starting transfers between devices: 11.7 us -> 23.8 us  [the longest x4 7.61 us: shards(): other = [lax.ppermute(piece, 'c', swap) for piece in mine]]
    all_to_all x1 -> x2, waiting for transfers between devices: 2.17 us -> 9.94 us  [the longest x1 6.22 us: shards(): held = lax.all_to_all(sent, BLOCK, 0, 0)]
    ppermute x1, waiting for transfers between devices: 6.38 us -> 1.05 us  [shards(): got_a = lax.ppermute(send_a, SEQ, down)]
    ppermute x5 -> x17, waiting for transfers between devices: 9.86 us -> 14.1 us  [the longest x3 7.33 us: columns_from(): lax.ppermute(two, 'y', around[hop])]
    ppermute x1, waiting for transfers between devices: 0.01 us -> 3.92 us  [shards(): s_0 = lax.ppermute(s_next, SEQ, up)]
    ppermute x2, waiting for transfers between devices: 4.16 us -> 8.02 us  [shards(): lax.ppermute(advance('gather_a', gather_step_kernel, MIRROR[k], k)(rows,...]
  transfers between devices with their start and end apart: 18 -> 31, of which waited for: 11 -> 14; matrix products, arithmetic and copies ran while one was open for 0% -> 0% of each run, Pallas kernels for 9% -> 10%
where the time goes in v4:
time: 240 us; the launch traced here: 238 us
  starting transfers between devices  93.4 us (39%)
  waiting for transfers between devices  54.7 us (23%)
  blocking collectives  36.4 us (15%)
  Pallas kernels  35.6 us (15%)
  local copies, waits for them, and re-layouts  15.6 us (6%)
    all_to_all x1, blocking collectives, shards(): lax.all_to_all(weight, SEQ, 0, 0)  24.1 us
    ppermute x1, starting transfers between devices, shards(): lax.ppermute(advance('spread_s', spread_step_kernel, 0)(rows, s_0, send_s...  19.2 us
    unnamed x102, local copies, waits for them, and re-layouts  15.6 us
    all_to_all x1, starting transfers between devices, shards(): held = lax.all_to_all(sent, BLOCK, 0, 0)  13.7 us
    all_to_all x1, blocking collectives, shards(): last = lax.all_to_all(summed, ('y', 'c'), 0, 0)  12.3 us
    ppermute x2, starting transfers between devices, shards(): lax.ppermute(advance('gather_s', gather_step_kernel, k, k)(rows, got_s, r...  11.2 us
    pallas_call x1, Pallas kernels, shards(): call(intra_kernel, (shape(ROWS, width), shape(HEADS, ROWS), shape(GROUPS,...  8.65 us
    ppermute x1, waiting for transfers between devices, shards(): a_0 = lax.ppermute(a_next, SEQ, down)  8.57 us
  transfers between devices with their start and end apart: 31, of which 14 were waited for; matrix products, arithmetic and copies ran while one was open for 0% of the time, Pallas kernels for 10%

profile of v4, /device:TPU:1, one launch (start us, length us, event | category | flops | bytes accessed | tf_op | source)
XLA Modules:
  0.0 238.5 jit_solution(8975454960543206230)
XLA Ops:
  2.1 4.4 %project.1 = (bf16[128,256]{1,0:T(8,128)(2,1)S(1)}, f32[128,64]{1,0:T(8,128)S(1)}, f32[128,64]{1,0:T(8,128)S(1)}, f32[32,128]{1,0:T(8,128)S(1)}, bf16[128,4096]{1,0:T(8,128)(2,1)S(1)}, /*index=5*/f32[1032,128]{1,0:T(8,128)S(1)}) custom-call(s32[3]{0:T(128)S(1)} %pad_add_fusion.turn_ref.place_ref, f32[64,128]{1,0:T(8,128)S(1)} %bitcast.28, ...), custom_call_target="tpu_custom_call" | custom-call | flops 400000000 | bytes 6291456 | tf_op jit(solution)/shard_map/project/pallas_call | solution.py:430
  9.8 5.0 %collective-permute-start = (f32[1032,128]{1,0:T(8,128)S(1)}, f32[1032,128]{1,0:T(8,128)S(1)}, u32[]{:S(2)}, u32[]{:S(2)}) collective-permute-start(f32[1032,128]{1,0:T(8,128)S(1)} %get-tuple-element.88.local), channel_id=1, source_target_pairs={{0,8},{8,16},{16,24},{24,32},{32,40},{40,48},{48,56},{56,64},{64,7... | collective-permute-start | bytes 1585160 | tf_op jit(solution)/shard_map/ppermute | solution.py:453
  15.9 2.9 %collective-permute-start.2 = (f32[512,128]{1,0:T(8,128)S(1)}, f32[512,128]{1,0:T(8,128)S(1)}, u32[]{:S(2)}, u32[]{:S(2)}) collective-permute-start(f32[512,128]{1,0:T(8,128)S(1)} %get-tuple-element.90), channel_id=1, source_target_pairs={{0,1},{1,0},{2,3},{3,2},{4,5},{5,4},{6,7},{7,6},{8,9},{9,8},{10,11... | collective-permute-start | bytes 786440 | tf_op jit(solution)/shard_map/ppermute | solution.py:491
  25.1 6.0 %collective-permute-start.6 = (f32[1032,128]{1,0:T(8,128)S(1)}, f32[1032,128]{1,0:T(8,128)S(1)}, u32[]{:S(2)}, u32[]{:S(2)}) collective-permute-start(f32[1032,128]{1,0:T(8,128)S(1)} %gather_s.2), channel_id=1, source_target_pairs={{0,8},{8,16},{16,24},{24,32},{32,40},{40,48},{48,56},{56,64},{64,7... | collective-permute-start | bytes 1585160 | tf_op jit(solution)/shard_map/ppermute | solution.py:530
  31.1 8.0 %collective-permute-done.8.got = f32[1032,128]{1,0:T(8,128)S(1)} collective-permute-done((f32[1032,128]{1,0:T(8,128)S(1)}, f32[1032,128]{1,0:T(8,128)S(1)}, u32[]{:S(2)}, u32[]{:S(2)}) %collective-permute-start.8) | collective-permute-done | bytes 528416 | tf_op jit(solution)/shard_map/ppermute | solution.py:531
  40.7 5.2 %collective-permute-start.7 = (f32[1032,128]{1,0:T(8,128)S(1)}, f32[1032,128]{1,0:T(8,128)S(1)}, u32[]{:S(2)}, u32[]{:S(2)}) collective-permute-start(f32[1032,128]{1,0:T(8,128)S(1)} %gather_s.3), channel_id=1, source_target_pairs={{0,8},{8,16},{16,24},{24,32},{32,40},{40,48},{48,56},{56,64},{64,7... | collective-permute-start | bytes 1585160 | tf_op jit(solution)/shard_map/ppermute | solution.py:530
  46.0 8.6 %intra.1 = (f32[128,4096]{1,0:T(8,128)S(1)}, f32[64,128]{1,0:T(8,128)S(1)}, f32[8,128,8]{2,1,0:T(8,128)S(1)}, f32[128,128]{1,0:T(8,128)S(1)}) custom-call(s32[3]{0:T(128)S(1)} %pad_add_fusion.turn_ref.place_ref, bf16[128,256]{1,0:T(8,128)(2,1)S(1)} %get-tuple-element.81.bc, f32[8,128,8]{2,1,0:T(8,128)S(1)} %get-tuple-element.96.cg, ...), custom_call_target="tpu_custom_call" | custom-call | flops 800000000 | bytes 20971520 | tf_op jit(solution)/shard_map/intra/pallas_call | solution.py:498
  59.5 13.7 %all-to-all-start = ((f32[8,264,128]{2,1,0:T(8,128)}), f32[8,264,128]{2,1,0:T(8,128)}, u32[]{:S(2)}, u32[]{:S(2)}) async-start(f32[8,264,128]{2,1,0:T(8,128)} %copy-done.16), calls=%async_computation | async-start | bytes 2162688 | tf_op jit(solution)/shard_map/all_to_all | solution.py:548
  80.3 3.2 %collective-permute-done.13.refs_7_ = f32[512,128]{1,0:T(8,128)S(1)} collective-permute-done((f32[512,128]{1,0:T(8,128)}, f32[512,128]{1,0:T(8,128)S(1)}, u32[]{:S(2)}, u32[]{:S(2)}) %collective-permute-start.13) | collective-permute-done | bytes 262176 | tf_op jit(solution)/shard_map/ppermute | solution.py:536
  87.5 6.2 %all-to-all-done.msg = f32[8,264,128]{2,1,0:T(8,128)} async-done(((f32[8,264,128]{2,1,0:T(8,128)}), f32[8,264,128]{2,1,0:T(8,128)}, u32[]{:S(2)}, u32[]{:S(2)}) %all-to-all-start) | async-done | bytes 1081376 | tf_op jit(solution)/shard_map/all_to_all | solution.py:548
  96.0 4.2 %all-to-all-start.1 = ((f32[8,256,128]{2,1,0:T(8,128)}), f32[8,256,128]{2,1,0:T(8,128)}, u32[]{:S(2)}, u32[]{:S(2)}) async-start(f32[8,256,128]{2,1,0:T(8,128)} %copy-done.18), calls=%async_computation.1 | async-start | bytes 2097152 | tf_op jit(solution)/shard_map/all_to_all | solution.py:560
  100.2 3.0 %collective-permute-start.14 = (f32[512,128]{1,0:T(8,128)}, f32[512,128]{1,0:T(8,128)S(1)}, u32[]{:S(2)}, u32[]{:S(2)}) collective-permute-start(f32[512,128]{1,0:T(8,128)} %copy-done.45), channel_id=1, source_target_pairs={{0,4},{2,6},{4,0},{6,2},{1,5},{3,7},{5,1},{7,3},{8,12},{10,14},{12... | collective-permute-start | bytes 786440 | tf_op jit(solution)/shard_map/ppermute | solution.py:536
  103.3 3.9 %collective-permute-done.14.refs_4_ = f32[512,128]{1,0:T(8,128)S(1)} collective-permute-done((f32[512,128]{1,0:T(8,128)}, f32[512,128]{1,0:T(8,128)S(1)}, u32[]{:S(2)}, u32[]{:S(2)}) %collective-permute-start.14) | collective-permute-done | bytes 262176 | tf_op jit(solution)/shard_map/ppermute | solution.py:536
  110.9 3.7 %all-to-all-done.1.back = f32[8,256,128]{2,1,0:T(8,128)} async-done(((f32[8,256,128]{2,1,0:T(8,128)}), f32[8,256,128]{2,1,0:T(8,128)}, u32[]{:S(2)}, u32[]{:S(2)}) %all-to-all-start.1) | async-done | bytes 1048608 | tf_op jit(solution)/shard_map/all_to_all | solution.py:560
  119.6 4.0 %collective-permute-start.16 = (f32[1024,128]{1,0:T(8,128)S(1)}, f32[1024,128]{1,0:T(8,128)S(1)}, u32[]{:S(2)}, u32[]{:S(2)}) collective-permute-start(f32[1024,128]{1,0:T(8,128)S(1)} %get-tuple-element.116), channel_id=1, source_target_pairs={{0,8},{8,16},{16,24},{24,32},{32,40},{40,48},{48,56},{56,64},{64,7... | collective-permute-start | bytes 1572872 | tf_op jit(solution)/shard_map/ppermute | solution.py:572
  123.6 8.6 %collective-permute-done.19.state.a_0.a_2 = f32[1024,128]{1,0:T(8,128)S(1)} collective-permute-done((f32[1024,128]{1,0:T(8,128)S(1)}, f32[1024,128]{1,0:T(8,128)S(1)}, u32[]{:S(2)}, u32[]{:S(2)}) %collective-permute-start.19) | collective-permute-done | bytes 524320 | tf_op jit(solution)/shard_map/ppermute | solution.py:573
  133.6 3.9 %collective-permute-done.16.state.s_0 = f32[1024,128]{1,0:T(8,128)S(1)} collective-permute-done((f32[1024,128]{1,0:T(8,128)S(1)}, f32[1024,128]{1,0:T(8,128)S(1)}, u32[]{:S(2)}, u32[]{:S(2)}) %collective-permute-start.16) | collective-permute-done | bytes 524320 | tf_op jit(solution)/shard_map/ppermute | solution.py:572
  137.6 19.2 %collective-permute-start.17 = (f32[1024,128]{1,0:T(8,128)S(1)}, f32[1024,128]{1,0:T(8,128)S(1)}, u32[]{:S(2)}, u32[]{:S(2)}) collective-permute-start(f32[1024,128]{1,0:T(8,128)S(1)} %spread_s.2), channel_id=1, source_target_pairs={{0,8},{8,16},{16,24},{24,32},{32,40},{40,48},{48,56},{56,64},{64,7... | collective-permute-start | bytes 1572872 | tf_op jit(solution)/shard_map/ppermute | solution.py:611
  156.8 8.2 %collective-permute-done.20.state.a_1.a_in = f32[1024,128]{1,0:T(8,128)S(1)} collective-permute-done((f32[1024,128]{1,0:T(8,128)S(1)}, f32[1024,128]{1,0:T(8,128)S(1)}, u32[]{:S(2)}, u32[]{:S(2)}) %collective-permute-start.20) | collective-permute-done | bytes 524320 | tf_op jit(solution)/shard_map/ppermute | solution.py:612
  166.7 4.2 %collective-permute-start.18 = (f32[1024,128]{1,0:T(8,128)S(1)}, f32[1024,128]{1,0:T(8,128)S(1)}, u32[]{:S(2)}, u32[]{:S(2)}) collective-permute-start(f32[1024,128]{1,0:T(8,128)S(1)} %spread_s.3), channel_id=1, source_target_pairs={{0,8},{8,16},{16,24},{24,32},{32,40},{40,48},{48,56},{56,64},{64,7... | collective-permute-start | bytes 1572872 | tf_op jit(solution)/shard_map/ppermute | solution.py:613
  187.5 4.0 %collective-permute-start.22 = (f32[128,256]{1,0:T(8,128)S(1)}, f32[128,256]{1,0:T(8,128)S(1)}, u32[]{:S(2)}, u32[]{:S(2)}) collective-permute-start(f32[128,256]{1,0:T(8,128)S(1)} %far.1.refs_0_), channel_id=1, source_target_pairs={{0,1},{1,0},{2,3},{3,2},{4,5},{5,4},{6,7},{7,6},{8,9},{9,8},{10,11... | collective-permute-start | bytes 393224 | tf_op jit(solution)/shard_map/ppermute | solution.py:636
  195.2 5.0 %finish.1 = (bf16[128,4096]{1,0:T(8,128)(2,1)}, f32[64,128]{1,0:T(8,128)}, f32[8,128]{1,0:T(8,128)S(1)}) custom-call(s32[3]{0:T(128)S(1)} %pad_add_fusion.turn_ref.place_ref, f32[1024,128]{1,0:T(8,128)S(1)} %collective-permute-done.16.state.s_0, f32[1024,128]{1,0:T(8,128)S(1)} %collective-permute-done.21.a_0.a_in, ...), custom_call_target="tpu_custom_call" | custom-call | flops 500000000 | bytes 6291456 | tf_op jit(solution)/shard_map/finish/pallas_call | solution.py:637
  200.8 24.1 %all_to_all.20.msg = f32[32,40,128]{2,1,0:T(8,128)S(1)} all-to-all(f32[32,40,128]{2,1,0:T(8,128)S(1)} %weight.1), channel_id=1, replica_groups=mesh['x'=4,'quad'=2,'turn'=4,'y'=4,'c'=2] {'x','quad','turn'}, dimensions={0} | all-to-all | bytes 1310720 | tf_op jit(solution)/shard_map/all_to_all | solution.py:665
  225.0 12.3 %all_to_all.21 = f32[8,40,128]{2,1,0:T(8,128)S(1)} all-to-all(f32[8,40,128]{2,1,0:T(8,128)S(1)} %last.1), channel_id=1, replica_groups=mesh['x'=4,'quad'=2,'turn'=4,'y'=4,'c'=2] {'y','c'}, dimensions={0} | all-to-all | bytes 327680 | tf_op jit(solution)/shard_map/all_to_all | solution.py:666
  (171 shorter events, 65.5 us)
Async XLA Ops:
  8.5 14.2 %collective-permute-start.1 = (f32[1032,128]{1,0:T(8,128)S(1)}, f32[1032,128]{1,0:T(8,128)S(1)}, u32[]{:S(2)}, u32[]{:S(2)}) collective-permute-start(f32[1032,128]{1,0:T(8,128)S(1)} %get-tuple-element.89.local), channel_id=1, source_target_pairs={{8,0},{16,8},{24,16},{32,24},{40,32},{48,40},{56,48},{64,56},{72,6... | collective-permute-start | bytes 1585160 | tf_op jit(solution)/shard_map/ppermute | solution.py:463
  9.8 13.8 %collective-permute-start = (f32[1032,128]{1,0:T(8,128)S(1)}, f32[1032,128]{1,0:T(8,128)S(1)}, u32[]{:S(2)}, u32[]{:S(2)}) collective-permute-start(f32[1032,128]{1,0:T(8,128)S(1)} %get-tuple-element.88.local), channel_id=1, source_target_pairs={{0,8},{8,16},{16,24},{24,32},{32,40},{40,48},{48,56},{56,64},{64,7... | collective-permute-start | bytes 1585160 | tf_op jit(solution)/shard_map/ppermute | solution.py:453
  23.7 15.4 %collective-permute-start.8 = (f32[1032,128]{1,0:T(8,128)S(1)}, f32[1032,128]{1,0:T(8,128)S(1)}, u32[]{:S(2)}, u32[]{:S(2)}) collective-permute-start(f32[1032,128]{1,0:T(8,128)S(1)} %gather_a.2), channel_id=1, source_target_pairs={{8,0},{16,8},{24,16},{32,24},{40,32},{48,40},{56,48},{64,56},{72,6... | collective-permute-start | bytes 1585160 | tf_op jit(solution)/shard_map/ppermute | solution.py:531
  25.1 15.5 %collective-permute-start.6 = (f32[1032,128]{1,0:T(8,128)S(1)}, f32[1032,128]{1,0:T(8,128)S(1)}, u32[]{:S(2)}, u32[]{:S(2)}) collective-permute-start(f32[1032,128]{1,0:T(8,128)S(1)} %gather_s.2), channel_id=1, source_target_pairs={{0,8},{8,16},{16,24},{24,32},{32,40},{40,48},{48,56},{56,64},{64,7... | collective-permute-start | bytes 1585160 | tf_op jit(solution)/shard_map/ppermute | solution.py:530
  39.2 17.5 %collective-permute-start.9 = (f32[1032,128]{1,0:T(8,128)S(1)}, f32[1032,128]{1,0:T(8,128)S(1)}, u32[]{:S(2)}, u32[]{:S(2)}) collective-permute-start(f32[1032,128]{1,0:T(8,128)S(1)} %gather_a.3), channel_id=1, source_target_pairs={{8,0},{16,8},{24,16},{32,24},{40,32},{48,40},{56,48},{64,56},{72,6... | collective-permute-start | bytes 1585160 | tf_op jit(solution)/shard_map/ppermute | solution.py:531
  40.7 16.0 %collective-permute-start.7 = (f32[1032,128]{1,0:T(8,128)S(1)}, f32[1032,128]{1,0:T(8,128)S(1)}, u32[]{:S(2)}, u32[]{:S(2)}) collective-permute-start(f32[1032,128]{1,0:T(8,128)S(1)} %gather_s.3), channel_id=1, source_target_pairs={{0,8},{8,16},{16,24},{24,32},{32,40},{40,48},{48,56},{56,64},{64,7... | collective-permute-start | bytes 1585160 | tf_op jit(solution)/shard_map/ppermute | solution.py:530
  59.5 34.2 %all-to-all-start = ((f32[8,264,128]{2,1,0:T(8,128)}), f32[8,264,128]{2,1,0:T(8,128)}, u32[]{:S(2)}, u32[]{:S(2)}) async-start(f32[8,264,128]{2,1,0:T(8,128)} %copy-done.16), calls=%async_computation | async-start | bytes 2162688 | tf_op jit(solution)/shard_map/all_to_all | solution.py:548
  75.9 7.5 %collective-permute-start.13 = (f32[512,128]{1,0:T(8,128)}, f32[512,128]{1,0:T(8,128)S(1)}, u32[]{:S(2)}, u32[]{:S(2)}) collective-permute-start(f32[512,128]{1,0:T(8,128)} %copy-done.50), channel_id=1, source_target_pairs={{0,6},{2,0},{4,2},{6,4},{1,7},{3,1},{5,3},{7,5},{8,14},{10,8},{12,... | collective-permute-start | bytes 786440 | tf_op jit(solution)/shard_map/ppermute | solution.py:536
  76.4 7.8 %collective-permute-start.10 = (f32[512,128]{1,0:T(8,128)}, f32[512,128]{1,0:T(8,128)S(1)}, u32[]{:S(2)}, u32[]{:S(2)}) collective-permute-start(f32[512,128]{1,0:T(8,128)} %copy-done.46), channel_id=1, source_target_pairs={{0,2},{2,4},{4,6},{6,0},{1,3},{3,5},{5,7},{7,1},{8,10},{10,12},{12... | collective-permute-start | bytes 786440 | tf_op jit(solution)/shard_map/ppermute | solution.py:536
  77.4 9.4 %collective-permute-start.11 = (f32[512,128]{1,0:T(8,128)}, f32[512,128]{1,0:T(8,128)S(1)}, u32[]{:S(2)}, u32[]{:S(2)}) collective-permute-start(f32[512,128]{1,0:T(8,128)} %copy-done.49), channel_id=1, source_target_pairs={{0,2},{2,4},{4,6},{6,0},{1,3},{3,5},{5,7},{7,1},{8,10},{10,12},{12... | collective-permute-start | bytes 786440 | tf_op jit(solution)/shard_map/ppermute | solution.py:536
  96.0 18.6 %all-to-all-start.1 = ((f32[8,256,128]{2,1,0:T(8,128)}), f32[8,256,128]{2,1,0:T(8,128)}, u32[]{:S(2)}, u32[]{:S(2)}) async-start(f32[8,256,128]{2,1,0:T(8,128)} %copy-done.18), calls=%async_computation.1 | async-start | bytes 2097152 | tf_op jit(solution)/shard_map/all_to_all | solution.py:560
  100.2 7.0 %collective-permute-start.14 = (f32[512,128]{1,0:T(8,128)}, f32[512,128]{1,0:T(8,128)S(1)}, u32[]{:S(2)}, u32[]{:S(2)}) collective-permute-start(f32[512,128]{1,0:T(8,128)} %copy-done.45), channel_id=1, source_target_pairs={{0,4},{2,6},{4,0},{6,2},{1,5},{3,7},{5,1},{7,3},{8,12},{10,14},{12... | collective-permute-start | bytes 786440 | tf_op jit(solution)/shard_map/ppermute | solution.py:536
  118.2 14.0 %collective-permute-start.19 = (f32[1024,128]{1,0:T(8,128)S(1)}, f32[1024,128]{1,0:T(8,128)S(1)}, u32[]{:S(2)}, u32[]{:S(2)}) collective-permute-start(f32[1024,128]{1,0:T(8,128)S(1)} %get-tuple-element.117), channel_id=1, source_target_pairs={{8,0},{16,8},{24,16},{32,24},{40,32},{48,40},{56,48},{64,56},{72,6... | collective-permute-start | bytes 1572872 | tf_op jit(solution)/shard_map/ppermute | solution.py:573
  119.6 17.9 %collective-permute-start.16 = (f32[1024,128]{1,0:T(8,128)S(1)}, f32[1024,128]{1,0:T(8,128)S(1)}, u32[]{:S(2)}, u32[]{:S(2)}) collective-permute-start(f32[1024,128]{1,0:T(8,128)S(1)} %get-tuple-element.116), channel_id=1, source_target_pairs={{0,8},{8,16},{16,24},{24,32},{32,40},{40,48},{48,56},{56,64},{64,7... | collective-permute-start | bytes 1572872 | tf_op jit(solution)/shard_map/ppermute | solution.py:572
  132.3 32.7 %collective-permute-start.20 = (f32[1024,128]{1,0:T(8,128)S(1)}, f32[1024,128]{1,0:T(8,128)S(1)}, u32[]{:S(2)}, u32[]{:S(2)}) collective-permute-start(f32[1024,128]{1,0:T(8,128)S(1)} %spread_a.2), channel_id=1, source_target_pairs={{8,0},{16,8},{24,16},{32,24},{40,32},{48,40},{56,48},{64,56},{72,6... | collective-permute-start | bytes 1572872 | tf_op jit(solution)/shard_map/ppermute | solution.py:612
  137.6 29.0 %collective-permute-start.17 = (f32[1024,128]{1,0:T(8,128)S(1)}, f32[1024,128]{1,0:T(8,128)S(1)}, u32[]{:S(2)}, u32[]{:S(2)}) collective-permute-start(f32[1024,128]{1,0:T(8,128)S(1)} %spread_s.2), channel_id=1, source_target_pairs={{0,8},{8,16},{16,24},{24,32},{32,40},{40,48},{48,56},{56,64},{64,7... | collective-permute-start | bytes 1572872 | tf_op jit(solution)/shard_map/ppermute | solution.py:611
  165.1 16.3 %collective-permute-start.21 = (f32[1024,128]{1,0:T(8,128)S(1)}, f32[1024,128]{1,0:T(8,128)S(1)}, u32[]{:S(2)}, u32[]{:S(2)}) collective-permute-start(f32[1024,128]{1,0:T(8,128)S(1)} %spread_a.3), channel_id=1, source_target_pairs={{8,0},{16,8},{24,16},{32,24},{40,32},{48,40},{56,48},{64,56},{72,6... | collective-permute-start | bytes 1572872 | tf_op jit(solution)/shard_map/ppermute | solution.py:614
  166.7 14.7 %collective-permute-start.18 = (f32[1024,128]{1,0:T(8,128)S(1)}, f32[1024,128]{1,0:T(8,128)S(1)}, u32[]{:S(2)}, u32[]{:S(2)}) collective-permute-start(f32[1024,128]{1,0:T(8,128)S(1)} %spread_s.3), channel_id=1, source_target_pairs={{0,8},{8,16},{16,24},{24,32},{32,40},{40,48},{48,56},{56,64},{64,7... | collective-permute-start | bytes 1572872 | tf_op jit(solution)/shard_map/ppermute | solution.py:613
  182.5 9.1 %collective-permute-start.23 = (f32[128,256]{1,0:T(8,128)S(1)}, f32[128,256]{1,0:T(8,128)S(1)}, u32[]{:S(2)}, u32[]{:S(2)}) collective-permute-start(f32[128,256]{1,0:T(8,128)S(1)} %far.1.refs_0_), channel_id=1, source_target_pairs={{0,2},{2,4},{4,6},{6,0},{1,3},{3,5},{5,7},{7,1},{8,10},{10,12},{12... | collective-permute-start | bytes 393224 | tf_op jit(solution)/shard_map/ppermute | solution.py:635
  183.9 8.5 %collective-permute-start.25 = (f32[128,256]{1,0:T(8,128)S(1)}, f32[128,256]{1,0:T(8,128)S(1)}, u32[]{:S(2)}, u32[]{:S(2)}) collective-permute-start(f32[128,256]{1,0:T(8,128)S(1)} %far.1.refs_0_), channel_id=1, source_target_pairs={{0,4},{2,6},{4,0},{6,2},{1,5},{3,7},{5,1},{7,3},{8,12},{10,14},{12... | collective-permute-start | bytes 393224 | tf_op jit(solution)/shard_map/ppermute | solution.py:635
  186.5 8.1 %collective-permute-start.27 = (f32[128,256]{1,0:T(8,128)S(1)}, f32[128,256]{1,0:T(8,128)S(1)}, u32[]{:S(2)}, u32[]{:S(2)}) collective-permute-start(f32[128,256]{1,0:T(8,128)S(1)} %far.1.refs_0_), channel_id=1, source_target_pairs={{0,6},{2,0},{4,2},{6,4},{1,7},{3,1},{5,3},{7,5},{8,14},{10,8},{12,... | collective-permute-start | bytes 393224 | tf_op jit(solution)/shard_map/ppermute | solution.py:635
  187.5 12.6 %collective-permute-start.22 = (f32[128,256]{1,0:T(8,128)S(1)}, f32[128,256]{1,0:T(8,128)S(1)}, u32[]{:S(2)}, u32[]{:S(2)}) collective-permute-start(f32[128,256]{1,0:T(8,128)S(1)} %far.1.refs_0_), channel_id=1, source_target_pairs={{0,1},{1,0},{2,3},{3,2},{4,5},{5,4},{6,7},{7,6},{8,9},{9,8},{10,11... | collective-permute-start | bytes 393224 | tf_op jit(solution)/shard_map/ppermute | solution.py:636
  191.5 8.6 %collective-permute-start.24 = (f32[128,256]{1,0:T(8,128)S(1)}, f32[128,256]{1,0:T(8,128)S(1)}, u32[]{:S(2)}, u32[]{:S(2)}) collective-permute-start(f32[128,256]{1,0:T(8,128)S(1)} %collective-permute-done.23.refs_2_), channel_id=1, source_target_pairs={{0,1},{1,0},{2,3},{3,2},{4,5},{5,4},{6,7},{7,6},{8,9},{9,8},{10,11... | collective-permute-start | bytes 393224 | tf_op jit(solution)/shard_map/ppermute | solution.py:636
  192.3 7.8 %collective-permute-start.26 = (f32[128,256]{1,0:T(8,128)S(1)}, f32[128,256]{1,0:T(8,128)S(1)}, u32[]{:S(2)}, u32[]{:S(2)}) collective-permute-start(f32[128,256]{1,0:T(8,128)S(1)} %collective-permute-done.25.refs_4_), channel_id=1, source_target_pairs={{0,1},{1,0},{2,3},{3,2},{4,5},{5,4},{6,7},{7,6},{8,9},{9,8},{10,11... | collective-permute-start | bytes 393224 | tf_op jit(solution)/shard_map/ppermute | solution.py:636
  (58 other events, 301.8 us)

commit v5 on v4

--- a/solution.py
+++ b/solution.py
@@ -556,10 +556,7 @@
         out_specs=VMEM,
         name="scan",
     )(held)
-    far_columns = columns_from(2, scanned)
     back = lax.all_to_all(scanned, BLOCK, 0, 0)
-    back, *far_columns = lax.optimization_barrier((back, *far_columns))
-    tok_got = [tok_mine[0], tok_swapped[0], *near_columns[:2], *far_columns, *near_columns[2:]]
     s_next, a_next = call(
         unfold_kernel,
         (shape(TILE, 128),) * 2,
@@ -571,6 +568,7 @@
     )(rows, rest_s, rest_a, got_s, got_a, back)
     s_0 = lax.ppermute(s_next, SEQ, up)
     a_0 = lax.ppermute(a_next, SEQ, down)
+    far_columns = columns_from(2, s_next)
     near, s_own, a_own = call(
         near_kernel,
         (shape(ROWS, 256), shape(TILE, 128), shape(TILE, 128)),
@@ -599,6 +597,10 @@
         )(turn, state, adj, x, g, u, c, dt, bc)
 
     own = outer_part(3, s_own, a_own)
+    s_1 = lax.ppermute(advance("spread_s", spread_step_kernel, 0)(rows, s_0, send_s), SEQ, up)
+    a_1 = lax.ppermute(advance("spread_a", spread_step_kernel, MIRROR[0])(rows, a_0, send_a), SEQ, down)
+    s_1, a_1, *far_columns = lax.optimization_barrier((s_1, a_1, *far_columns))
+    tok_got = [tok_mine[0], tok_swapped[0], *near_columns[:2], *far_columns, *near_columns[2:]]
     all_tok = call(
         narrow_kernel,
         shape(8, 512, ROWS, dtype=BF),
@@ -608,8 +610,6 @@
         out_specs=VMEM,
         name="narrow",
     )(*tok_got)
-    s_1 = lax.ppermute(advance("spread_s", spread_step_kernel, 0)(rows, s_0, send_s), SEQ, up)
-    a_1 = lax.ppermute(advance("spread_a", spread_step_kernel, MIRROR[0])(rows, a_0, send_a), SEQ, down)
     s_2 = lax.ppermute(advance("spread_s", spread_rest_kernel, 1)(rows, s_1, rest_s), SEQ, up)
     a_2 = lax.ppermute(advance("spread_a", spread_rest_kernel, MIRROR[1])(rows, a_1, rest_a), SEQ, down)
     middle = call(

time: 240 us -> 235 us (0.979)
  blocking collectives: 36.4 us -> 58.3 us
  waiting for transfers between devices: 54.7 us -> 42.1 us
  starting transfers between devices: 93.4 us -> 86.1 us
  local copies, waits for them, and re-layouts: 15.6 us -> 11.8 us
    all_to_all x0 -> x1, blocking collectives: none -> 17.2 us  [shards(): back = lax.all_to_all(scanned, BLOCK, 0, 0)]
    ppermute x1, waiting for transfers between devices: 8.22 us -> 0.01 us  [shards(): lax.ppermute(advance('spread_a', spread_step_kernel, MIRROR[0])(rows, a_0...]
    ppermute x1, starting transfers between devices: 19.2 us -> 12.6 us  [shards(): lax.ppermute(advance('spread_s', spread_step_kernel, 0)(rows, s_0, send_s...]
    all_to_all x1, blocking collectives: 24.1 us -> 29 us  [shards(): lax.all_to_all(weight, SEQ, 0, 0)]
    ppermute x1, waiting for transfers between devices: 8.57 us -> 13.2 us  [shards(): a_0 = lax.ppermute(a_next, SEQ, down)]
    all_to_all x1 -> x0, starting transfers between devices: 4.24 us -> none  [shards(): back = lax.all_to_all(scanned, BLOCK, 0, 0)]
    ppermute x4, starting transfers between devices: 7.61 us -> 11.6 us  [shards(): other = [lax.ppermute(piece, 'c', swap) for piece in mine]]
    ppermute x1, waiting for transfers between devices: 3.92 us -> 0.01 us  [shards(): s_0 = lax.ppermute(s_next, SEQ, up)]
  transfers between devices with their start and end apart: 31 -> 30, of which waited for: 14 -> 10; matrix products, arithmetic and copies ran while one was open for 0% -> 0% of each run, Pallas kernels for 10% -> 10%
where the time goes in v5:
time: 235 us; the launch traced here: 234 us
  starting transfers between devices  86.1 us (37%)
  blocking collectives  58.3 us (25%)
  waiting for transfers between devices  42.1 us (18%)
  Pallas kernels  33.5 us (14%)
  local copies, waits for them, and re-layouts  11.8 us (5%)
    all_to_all x1, blocking collectives, shards(): lax.all_to_all(weight, SEQ, 0, 0)  29 us
    all_to_all x1, blocking collectives, shards(): back = lax.all_to_all(scanned, BLOCK, 0, 0)  17.2 us
    all_to_all x1, starting transfers between devices, shards(): held = lax.all_to_all(sent, BLOCK, 0, 0)  13.6 us
    ppermute x1, waiting for transfers between devices, shards(): a_0 = lax.ppermute(a_next, SEQ, down)  13.2 us
    ppermute x1, starting transfers between devices, shards(): lax.ppermute(advance('spread_s', spread_step_kernel, 0)(rows, s_0, send_s...  12.6 us
    all_to_all x1, blocking collectives, shards(): last = lax.all_to_all(summed, ('y', 'c'), 0, 0)  12.1 us
    unnamed x92, local copies, waits for them, and re-layouts  11.8 us
    ppermute x4, starting transfers between devices, shards(): other = [lax.ppermute(piece, 'c', swap) for piece in mine]  11.6 us
  transfers between devices with their start and end apart: 30, of which 10 were waited for; matrix products, arithmetic and copies ran while one was open for 0% of the time, Pallas kernels for 10%

profile of v5, /device:TPU:1, one launch (start us, length us, event | category | flops | bytes accessed | tf_op | source)
XLA Modules:
  0.0 234.5 jit_solution(8696236886247561355)
XLA Ops:
  2.1 4.4 %project.1 = (bf16[128,256]{1,0:T(8,128)(2,1)S(1)}, f32[128,64]{1,0:T(8,128)S(1)}, f32[128,64]{1,0:T(8,128)S(1)}, f32[32,128]{1,0:T(8,128)S(1)}, bf16[128,4096]{1,0:T(8,128)(2,1)S(1)}, /*index=5*/f32[1032,128]{1,0:T(8,128)S(1)}) custom-call(s32[3]{0:T(128)S(1)} %pad_add_fusion.turn_ref.place_ref, f32[64,128]{1,0:T(8,128)S(1)} %bitcast.28, ...), custom_call_target="tpu_custom_call" | custom-call | flops 400000000 | bytes 6291456 | tf_op jit(solution)/shard_map/project/pallas_call | solution.py:430
  9.8 5.0 %collective-permute-start = (f32[1032,128]{1,0:T(8,128)S(1)}, f32[1032,128]{1,0:T(8,128)S(1)}, u32[]{:S(2)}, u32[]{:S(2)}) collective-permute-start(f32[1032,128]{1,0:T(8,128)S(1)} %get-tuple-element.89.local), channel_id=1, source_target_pairs={{0,8},{8,16},{16,24},{24,32},{32,40},{40,48},{48,56},{56,64},{64,7... | collective-permute-start | bytes 1585160 | tf_op jit(solution)/shard_map/ppermute | solution.py:453
  17.3 2.8 %collective-permute-start.2 = (f32[512,128]{1,0:T(8,128)S(1)}, f32[512,128]{1,0:T(8,128)S(1)}, u32[]{:S(2)}, u32[]{:S(2)}) collective-permute-start(f32[512,128]{1,0:T(8,128)S(1)} %get-tuple-element.91), channel_id=1, source_target_pairs={{0,1},{1,0},{2,3},{3,2},{4,5},{5,4},{6,7},{7,6},{8,9},{9,8},{10,11... | collective-permute-start | bytes 786440 | tf_op jit(solution)/shard_map/ppermute | solution.py:491
  25.1 6.0 %collective-permute-start.6 = (f32[1032,128]{1,0:T(8,128)S(1)}, f32[1032,128]{1,0:T(8,128)S(1)}, u32[]{:S(2)}, u32[]{:S(2)}) collective-permute-start(f32[1032,128]{1,0:T(8,128)S(1)} %gather_s.2), channel_id=1, source_target_pairs={{0,8},{8,16},{16,24},{24,32},{32,40},{40,48},{48,56},{56,64},{64,7... | collective-permute-start | bytes 1585160 | tf_op jit(solution)/shard_map/ppermute | solution.py:530
  31.1 8.0 %collective-permute-done.8.got = f32[1032,128]{1,0:T(8,128)S(1)} collective-permute-done((f32[1032,128]{1,0:T(8,128)S(1)}, f32[1032,128]{1,0:T(8,128)S(1)}, u32[]{:S(2)}, u32[]{:S(2)}) %collective-permute-start.8) | collective-permute-done | bytes 528416 | tf_op jit(solution)/shard_map/ppermute | solution.py:531
  40.7 5.2 %collective-permute-start.7 = (f32[1032,128]{1,0:T(8,128)S(1)}, f32[1032,128]{1,0:T(8,128)S(1)}, u32[]{:S(2)}, u32[]{:S(2)}) collective-permute-start(f32[1032,128]{1,0:T(8,128)S(1)} %gather_s.3), channel_id=1, source_target_pairs={{0,8},{8,16},{16,24},{24,32},{32,40},{40,48},{48,56},{56,64},{64,7... | collective-permute-start | bytes 1585160 | tf_op jit(solution)/shard_map/ppermute | solution.py:530
  45.9 8.6 %intra.1 = (f32[128,4096]{1,0:T(8,128)S(1)}, f32[64,128]{1,0:T(8,128)S(1)}, f32[8,128,8]{2,1,0:T(8,128)S(1)}, f32[128,128]{1,0:T(8,128)S(1)}) custom-call(s32[3]{0:T(128)S(1)} %pad_add_fusion.turn_ref.place_ref, bf16[128,256]{1,0:T(8,128)(2,1)S(1)} %get-tuple-element.82.bc, f32[8,128,8]{2,1,0:T(8,128)S(1)} %get-tuple-element.97.cg, ...), custom_call_target="tpu_custom_call" | custom-call | flops 800000000 | bytes 20971520 | tf_op jit(solution)/shard_map/intra/pallas_call | solution.py:498
  59.6 13.6 %all-to-all-start = ((f32[8,264,128]{2,1,0:T(8,128)}), f32[8,264,128]{2,1,0:T(8,128)}, u32[]{:S(2)}, u32[]{:S(2)}) async-start(f32[8,264,128]{2,1,0:T(8,128)} %copy-done.14), calls=%async_computation | async-start | bytes 2162688 | tf_op jit(solution)/shard_map/all_to_all | solution.py:548
  73.2 2.7 %collective-permute-start.12 = (f32[512,128]{1,0:T(8,128)}, f32[512,128]{1,0:T(8,128)S(1)}, u32[]{:S(2)}, u32[]{:S(2)}) collective-permute-start(f32[512,128]{1,0:T(8,128)} %copy-done.41), channel_id=1, source_target_pairs={{0,6},{2,0},{4,2},{6,4},{1,7},{3,1},{5,3},{7,5},{8,14},{10,8},{12,... | collective-permute-start | bytes 786440 | tf_op jit(solution)/shard_map/ppermute | solution.py:536
  80.3 3.2 %collective-permute-done.13.refs_7_ = f32[512,128]{1,0:T(8,128)S(1)} collective-permute-done((f32[512,128]{1,0:T(8,128)}, f32[512,128]{1,0:T(8,128)S(1)}, u32[]{:S(2)}, u32[]{:S(2)}) %collective-permute-start.13) | collective-permute-done | bytes 262176 | tf_op jit(solution)/shard_map/ppermute | solution.py:536
  87.5 5.8 %all-to-all-done.msg = f32[8,264,128]{2,1,0:T(8,128)} async-done(((f32[8,264,128]{2,1,0:T(8,128)}), f32[8,264,128]{2,1,0:T(8,128)}, u32[]{:S(2)}, u32[]{:S(2)}) %all-to-all-start) | async-done | bytes 1081376 | tf_op jit(solution)/shard_map/all_to_all | solution.py:548
  94.6 17.2 %all_to_all.20.back = f32[8,256,128]{2,1,0:T(8,128)S(1)} all-to-all(f32[8,256,128]{2,1,0:T(8,128)S(1)} %scan.1), channel_id=1, replica_groups=mesh['x'=4,'quad'=2,'turn'=4,'y'=4,'c'=2] {'x','quad'}, dimensions={0} | all-to-all | bytes 2097152 | tf_op jit(solution)/shard_map/all_to_all | solution.py:559
  113.4 4.2 %collective-permute-start.14 = (f32[1024,128]{1,0:T(8,128)S(1)}, f32[1024,128]{1,0:T(8,128)S(1)}, u32[]{:S(2)}, u32[]{:S(2)}) collective-permute-start(f32[1024,128]{1,0:T(8,128)S(1)} %get-tuple-element.112), channel_id=1, source_target_pairs={{0,8},{8,16},{16,24},{24,32},{32,40},{40,48},{48,56},{56,64},{64,7... | collective-permute-start | bytes 1572872 | tf_op jit(solution)/shard_map/ppermute | solution.py:569
  117.6 13.2 %collective-permute-done.16.state.a_0.a_2 = f32[1024,128]{1,0:T(8,128)S(1)} collective-permute-done((f32[1024,128]{1,0:T(8,128)S(1)}, f32[1024,128]{1,0:T(8,128)S(1)}, u32[]{:S(2)}, u32[]{:S(2)}) %collective-permute-start.16) | collective-permute-done | bytes 524320 | tf_op jit(solution)/shard_map/ppermute | solution.py:570
  132.3 12.6 %collective-permute-start.15 = (f32[1024,128]{1,0:T(8,128)S(1)}, f32[1024,128]{1,0:T(8,128)S(1)}, u32[]{:S(2)}, u32[]{:S(2)}) collective-permute-start(f32[1024,128]{1,0:T(8,128)S(1)} %spread_s.2), channel_id=1, source_target_pairs={{0,8},{8,16},{16,24},{24,32},{32,40},{40,48},{48,56},{56,64},{64,7... | collective-permute-start | bytes 1572872 | tf_op jit(solution)/shard_map/ppermute | solution.py:600
  144.8 2.8 %collective-permute-start.18 = (f32[512,128]{1,0:T(8,128)S(1)}, f32[512,128]{1,0:T(8,128)S(1)}, u32[]{:S(2)}, u32[]{:S(2)}) collective-permute-start(f32[512,128]{1,0:T(8,128)S(1)} %copy-done.39), channel_id=1, source_target_pairs={{0,4},{2,6},{4,0},{6,2},{1,5},{3,7},{5,1},{7,3},{8,12},{10,14},{12... | collective-permute-start | bytes 786440 | tf_op jit(solution)/shard_map/ppermute | solution.py:536
  147.9 3.8 %collective-permute-done.18.refs_4_ = f32[512,128]{1,0:T(8,128)S(1)} collective-permute-done((f32[512,128]{1,0:T(8,128)S(1)}, f32[512,128]{1,0:T(8,128)S(1)}, u32[]{:S(2)}, u32[]{:S(2)}) %collective-permute-start.18) | collective-permute-done | bytes 262176 | tf_op jit(solution)/shard_map/ppermute | solution.py:536
  151.7 2.8 %collective-permute-done.19.refs_5_ = f32[512,128]{1,0:T(8,128)S(1)} collective-permute-done((f32[512,128]{1,0:T(8,128)S(1)}, f32[512,128]{1,0:T(8,128)S(1)}, u32[]{:S(2)}, u32[]{:S(2)}) %collective-permute-start.19) | collective-permute-done | bytes 262176 | tf_op jit(solution)/shard_map/ppermute | solution.py:536
  156.1 4.0 %collective-permute-start.20 = (f32[1024,128]{1,0:T(8,128)S(1)}, f32[1024,128]{1,0:T(8,128)S(1)}, u32[]{:S(2)}, u32[]{:S(2)}) collective-permute-start(f32[1024,128]{1,0:T(8,128)S(1)} %spread_s.3), channel_id=1, source_target_pairs={{0,8},{8,16},{16,24},{24,32},{32,40},{40,48},{48,56},{56,64},{64,7... | collective-permute-start | bytes 1572872 | tf_op jit(solution)/shard_map/ppermute | solution.py:613
  171.1 2.6 %collective-permute-start.25 = (f32[128,256]{1,0:T(8,128)S(1)}, f32[128,256]{1,0:T(8,128)S(1)}, u32[]{:S(2)}, u32[]{:S(2)}) collective-permute-start(f32[128,256]{1,0:T(8,128)S(1)} %far.1.refs_0_), channel_id=1, source_target_pairs={{0,4},{2,6},{4,0},{6,2},{1,5},{3,7},{5,1},{7,3},{8,12},{10,14},{12... | collective-permute-start | bytes 393224 | tf_op jit(solution)/shard_map/ppermute | solution.py:635
  174.8 8.0 %collective-permute-start.22 = (f32[128,256]{1,0:T(8,128)S(1)}, f32[128,256]{1,0:T(8,128)S(1)}, u32[]{:S(2)}, u32[]{:S(2)}) collective-permute-start(f32[128,256]{1,0:T(8,128)S(1)} %far.1.refs_0_), channel_id=1, source_target_pairs={{0,1},{1,0},{2,3},{3,2},{4,5},{5,4},{6,7},{7,6},{8,9},{9,8},{10,11... | collective-permute-start | bytes 393224 | tf_op jit(solution)/shard_map/ppermute | solution.py:636
  186.4 5.0 %finish.1 = (bf16[128,4096]{1,0:T(8,128)(2,1)}, f32[64,128]{1,0:T(8,128)}, f32[8,128]{1,0:T(8,128)S(1)}) custom-call(s32[3]{0:T(128)S(1)} %pad_add_fusion.turn_ref.place_ref, f32[1024,128]{1,0:T(8,128)S(1)} %collective-permute-done.14.state.s_0, f32[1024,128]{1,0:T(8,128)S(1)} %collective-permute-done.21.a_0.a_in, ...), custom_call_target="tpu_custom_call" | custom-call | flops 500000000 | bytes 6291456 | tf_op jit(solution)/shard_map/finish/pallas_call | solution.py:637
  192.1 29.0 %all_to_all.21.msg = f32[32,40,128]{2,1,0:T(8,128)S(1)} all-to-all(f32[32,40,128]{2,1,0:T(8,128)S(1)} %weight.1), channel_id=1, replica_groups=mesh['x'=4,'quad'=2,'turn'=4,'y'=4,'c'=2] {'x','quad','turn'}, dimensions={0} | all-to-all | bytes 1310720 | tf_op jit(solution)/shard_map/all_to_all | solution.py:665
  221.1 12.1 %all_to_all.22 = f32[8,40,128]{2,1,0:T(8,128)S(1)} all-to-all(f32[8,40,128]{2,1,0:T(8,128)S(1)} %last.1), channel_id=1, replica_groups=mesh['x'=4,'quad'=2,'turn'=4,'y'=4,'c'=2] {'y','c'}, dimensions={0} | all-to-all | bytes 327680 | tf_op jit(solution)/shard_map/all_to_all | solution.py:666
  (160 shorter events, 50.5 us)
Async XLA Ops:
  8.5 14.4 %collective-permute-start.1 = (f32[1032,128]{1,0:T(8,128)S(1)}, f32[1032,128]{1,0:T(8,128)S(1)}, u32[]{:S(2)}, u32[]{:S(2)}) collective-permute-start(f32[1032,128]{1,0:T(8,128)S(1)} %get-tuple-element.90.local), channel_id=1, source_target_pairs={{8,0},{16,8},{24,16},{32,24},{40,32},{48,40},{56,48},{64,56},{72,6... | collective-permute-start | bytes 1585160 | tf_op jit(solution)/shard_map/ppermute | solution.py:463
  9.8 13.8 %collective-permute-start = (f32[1032,128]{1,0:T(8,128)S(1)}, f32[1032,128]{1,0:T(8,128)S(1)}, u32[]{:S(2)}, u32[]{:S(2)}) collective-permute-start(f32[1032,128]{1,0:T(8,128)S(1)} %get-tuple-element.89.local), channel_id=1, source_target_pairs={{0,8},{8,16},{16,24},{24,32},{32,40},{40,48},{48,56},{56,64},{64,7... | collective-permute-start | bytes 1585160 | tf_op jit(solution)/shard_map/ppermute | solution.py:453
  23.7 15.4 %collective-permute-start.8 = (f32[1032,128]{1,0:T(8,128)S(1)}, f32[1032,128]{1,0:T(8,128)S(1)}, u32[]{:S(2)}, u32[]{:S(2)}) collective-permute-start(f32[1032,128]{1,0:T(8,128)S(1)} %gather_a.2), channel_id=1, source_target_pairs={{8,0},{16,8},{24,16},{32,24},{40,32},{48,40},{56,48},{64,56},{72,6... | collective-permute-start | bytes 1585160 | tf_op jit(solution)/shard_map/ppermute | solution.py:531
  25.1 15.5 %collective-permute-start.6 = (f32[1032,128]{1,0:T(8,128)S(1)}, f32[1032,128]{1,0:T(8,128)S(1)}, u32[]{:S(2)}, u32[]{:S(2)}) collective-permute-start(f32[1032,128]{1,0:T(8,128)S(1)} %gather_s.2), channel_id=1, source_target_pairs={{0,8},{8,16},{16,24},{24,32},{32,40},{40,48},{48,56},{56,64},{64,7... | collective-permute-start | bytes 1585160 | tf_op jit(solution)/shard_map/ppermute | solution.py:530
  39.2 17.6 %collective-permute-start.9 = (f32[1032,128]{1,0:T(8,128)S(1)}, f32[1032,128]{1,0:T(8,128)S(1)}, u32[]{:S(2)}, u32[]{:S(2)}) collective-permute-start(f32[1032,128]{1,0:T(8,128)S(1)} %gather_a.3), channel_id=1, source_target_pairs={{8,0},{16,8},{24,16},{32,24},{40,32},{48,40},{56,48},{64,56},{72,6... | collective-permute-start | bytes 1585160 | tf_op jit(solution)/shard_map/ppermute | solution.py:531
  40.7 16.1 %collective-permute-start.7 = (f32[1032,128]{1,0:T(8,128)S(1)}, f32[1032,128]{1,0:T(8,128)S(1)}, u32[]{:S(2)}, u32[]{:S(2)}) collective-permute-start(f32[1032,128]{1,0:T(8,128)S(1)} %gather_s.3), channel_id=1, source_target_pairs={{0,8},{8,16},{16,24},{24,32},{32,40},{40,48},{48,56},{56,64},{64,7... | collective-permute-start | bytes 1585160 | tf_op jit(solution)/shard_map/ppermute | solution.py:530
  59.6 33.7 %all-to-all-start = ((f32[8,264,128]{2,1,0:T(8,128)}), f32[8,264,128]{2,1,0:T(8,128)}, u32[]{:S(2)}, u32[]{:S(2)}) async-start(f32[8,264,128]{2,1,0:T(8,128)} %copy-done.14), calls=%async_computation | async-start | bytes 2162688 | tf_op jit(solution)/shard_map/all_to_all | solution.py:548
  75.9 7.5 %collective-permute-start.13 = (f32[512,128]{1,0:T(8,128)}, f32[512,128]{1,0:T(8,128)S(1)}, u32[]{:S(2)}, u32[]{:S(2)}) collective-permute-start(f32[512,128]{1,0:T(8,128)} %copy-done.45), channel_id=1, source_target_pairs={{0,6},{2,0},{4,2},{6,4},{1,7},{3,1},{5,3},{7,5},{8,14},{10,8},{12,... | collective-permute-start | bytes 786440 | tf_op jit(solution)/shard_map/ppermute | solution.py:536
  76.4 7.8 %collective-permute-start.10 = (f32[512,128]{1,0:T(8,128)}, f32[512,128]{1,0:T(8,128)S(1)}, u32[]{:S(2)}, u32[]{:S(2)}) collective-permute-start(f32[512,128]{1,0:T(8,128)} %copy-done.40), channel_id=1, source_target_pairs={{0,2},{2,4},{4,6},{6,0},{1,3},{3,5},{5,7},{7,1},{8,10},{10,12},{12... | collective-permute-start | bytes 786440 | tf_op jit(solution)/shard_map/ppermute | solution.py:536
  77.4 9.4 %collective-permute-start.11 = (f32[512,128]{1,0:T(8,128)}, f32[512,128]{1,0:T(8,128)S(1)}, u32[]{:S(2)}, u32[]{:S(2)}) collective-permute-start(f32[512,128]{1,0:T(8,128)} %copy-done.44), channel_id=1, source_target_pairs={{0,2},{2,4},{4,6},{6,0},{1,3},{3,5},{5,7},{7,1},{8,10},{10,12},{12... | collective-permute-start | bytes 786440 | tf_op jit(solution)/shard_map/ppermute | solution.py:536
  112.0 18.8 %collective-permute-start.16 = (f32[1024,128]{1,0:T(8,128)S(1)}, f32[1024,128]{1,0:T(8,128)S(1)}, u32[]{:S(2)}, u32[]{:S(2)}) collective-permute-start(f32[1024,128]{1,0:T(8,128)S(1)} %get-tuple-element.113), channel_id=1, source_target_pairs={{8,0},{16,8},{24,16},{32,24},{40,32},{48,40},{56,48},{64,56},{72,6... | collective-permute-start | bytes 1572872 | tf_op jit(solution)/shard_map/ppermute | solution.py:570
  113.4 18.7 %collective-permute-start.14 = (f32[1024,128]{1,0:T(8,128)S(1)}, f32[1024,128]{1,0:T(8,128)S(1)}, u32[]{:S(2)}, u32[]{:S(2)}) collective-permute-start(f32[1024,128]{1,0:T(8,128)S(1)} %get-tuple-element.112), channel_id=1, source_target_pairs={{0,8},{8,16},{16,24},{24,32},{32,40},{40,48},{48,56},{56,64},{64,7... | collective-permute-start | bytes 1572872 | tf_op jit(solution)/shard_map/ppermute | solution.py:569
  130.9 23.6 %collective-permute-start.17 = (f32[1024,128]{1,0:T(8,128)S(1)}, f32[1024,128]{1,0:T(8,128)S(1)}, u32[]{:S(2)}, u32[]{:S(2)}) collective-permute-start(f32[1024,128]{1,0:T(8,128)S(1)} %spread_a.2), channel_id=1, source_target_pairs={{8,0},{16,8},{24,16},{32,24},{40,32},{48,40},{56,48},{64,56},{72,6... | collective-permute-start | bytes 1572872 | tf_op jit(solution)/shard_map/ppermute | solution.py:601
  132.3 22.2 %collective-permute-start.15 = (f32[1024,128]{1,0:T(8,128)S(1)}, f32[1024,128]{1,0:T(8,128)S(1)}, u32[]{:S(2)}, u32[]{:S(2)}) collective-permute-start(f32[1024,128]{1,0:T(8,128)S(1)} %spread_s.2), channel_id=1, source_target_pairs={{0,8},{8,16},{16,24},{24,32},{32,40},{40,48},{48,56},{56,64},{64,7... | collective-permute-start | bytes 1572872 | tf_op jit(solution)/shard_map/ppermute | solution.py:600
  144.8 6.8 %collective-permute-start.18 = (f32[512,128]{1,0:T(8,128)S(1)}, f32[512,128]{1,0:T(8,128)S(1)}, u32[]{:S(2)}, u32[]{:S(2)}) collective-permute-start(f32[512,128]{1,0:T(8,128)S(1)} %copy-done.39), channel_id=1, source_target_pairs={{0,4},{2,6},{4,0},{6,2},{1,5},{3,7},{5,1},{7,3},{8,12},{10,14},{12... | collective-permute-start | bytes 786440 | tf_op jit(solution)/shard_map/ppermute | solution.py:536
  147.7 6.8 %collective-permute-start.19 = (f32[512,128]{1,0:T(8,128)S(1)}, f32[512,128]{1,0:T(8,128)S(1)}, u32[]{:S(2)}, u32[]{:S(2)}) collective-permute-start(f32[512,128]{1,0:T(8,128)S(1)} %copy-done.43), channel_id=1, source_target_pairs={{0,4},{2,6},{4,0},{6,2},{1,5},{3,7},{5,1},{7,3},{8,12},{10,14},{12... | collective-permute-start | bytes 786440 | tf_op jit(solution)/shard_map/ppermute | solution.py:536
  154.6 14.3 %collective-permute-start.21 = (f32[1024,128]{1,0:T(8,128)S(1)}, f32[1024,128]{1,0:T(8,128)S(1)}, u32[]{:S(2)}, u32[]{:S(2)}) collective-permute-start(f32[1024,128]{1,0:T(8,128)S(1)} %spread_a.3), channel_id=1, source_target_pairs={{8,0},{16,8},{24,16},{32,24},{40,32},{48,40},{56,48},{64,56},{72,6... | collective-permute-start | bytes 1572872 | tf_op jit(solution)/shard_map/ppermute | solution.py:614
  156.1 12.7 %collective-permute-start.20 = (f32[1024,128]{1,0:T(8,128)S(1)}, f32[1024,128]{1,0:T(8,128)S(1)}, u32[]{:S(2)}, u32[]{:S(2)}) collective-permute-start(f32[1024,128]{1,0:T(8,128)S(1)} %spread_s.3), channel_id=1, source_target_pairs={{0,8},{8,16},{16,24},{24,32},{32,40},{40,48},{48,56},{56,64},{64,7... | collective-permute-start | bytes 1572872 | tf_op jit(solution)/shard_map/ppermute | solution.py:613
  169.9 12.9 %collective-permute-start.23 = (f32[128,256]{1,0:T(8,128)S(1)}, f32[128,256]{1,0:T(8,128)S(1)}, u32[]{:S(2)}, u32[]{:S(2)}) collective-permute-start(f32[128,256]{1,0:T(8,128)S(1)} %far.1.refs_0_), channel_id=1, source_target_pairs={{0,2},{2,4},{4,6},{6,0},{1,3},{3,5},{5,7},{7,1},{8,10},{10,12},{12... | collective-permute-start | bytes 393224 | tf_op jit(solution)/shard_map/ppermute | solution.py:635
  171.1 12.4 %collective-permute-start.25 = (f32[128,256]{1,0:T(8,128)S(1)}, f32[128,256]{1,0:T(8,128)S(1)}, u32[]{:S(2)}, u32[]{:S(2)}) collective-permute-start(f32[128,256]{1,0:T(8,128)S(1)} %far.1.refs_0_), channel_id=1, source_target_pairs={{0,4},{2,6},{4,0},{6,2},{1,5},{3,7},{5,1},{7,3},{8,12},{10,14},{12... | collective-permute-start | bytes 393224 | tf_op jit(solution)/shard_map/ppermute | solution.py:635
  173.7 12.0 %collective-permute-start.27 = (f32[128,256]{1,0:T(8,128)S(1)}, f32[128,256]{1,0:T(8,128)S(1)}, u32[]{:S(2)}, u32[]{:S(2)}) collective-permute-start(f32[128,256]{1,0:T(8,128)S(1)} %far.1.refs_0_), channel_id=1, source_target_pairs={{0,6},{2,0},{4,2},{6,4},{1,7},{3,1},{5,3},{7,5},{8,14},{10,8},{12,... | collective-permute-start | bytes 393224 | tf_op jit(solution)/shard_map/ppermute | solution.py:635
  174.8 16.5 %collective-permute-start.22 = (f32[128,256]{1,0:T(8,128)S(1)}, f32[128,256]{1,0:T(8,128)S(1)}, u32[]{:S(2)}, u32[]{:S(2)}) collective-permute-start(f32[128,256]{1,0:T(8,128)S(1)} %far.1.refs_0_), channel_id=1, source_target_pairs={{0,1},{1,0},{2,3},{3,2},{4,5},{5,4},{6,7},{7,6},{8,9},{9,8},{10,11... | collective-permute-start | bytes 393224 | tf_op jit(solution)/shard_map/ppermute | solution.py:636
  182.8 8.6 %collective-permute-start.24 = (f32[128,256]{1,0:T(8,128)S(1)}, f32[128,256]{1,0:T(8,128)S(1)}, u32[]{:S(2)}, u32[]{:S(2)}) collective-permute-start(f32[128,256]{1,0:T(8,128)S(1)} %collective-permute-done.23.refs_2_), channel_id=1, source_target_pairs={{0,1},{1,0},{2,3},{3,2},{4,5},{5,4},{6,7},{7,6},{8,9},{9,8},{10,11... | collective-permute-start | bytes 393224 | tf_op jit(solution)/shard_map/ppermute | solution.py:636
  183.5 7.8 %collective-permute-start.26 = (f32[128,256]{1,0:T(8,128)S(1)}, f32[128,256]{1,0:T(8,128)S(1)}, u32[]{:S(2)}, u32[]{:S(2)}) collective-permute-start(f32[128,256]{1,0:T(8,128)S(1)} %collective-permute-done.25.refs_4_), channel_id=1, source_target_pairs={{0,1},{1,0},{2,3},{3,2},{4,5},{5,4},{6,7},{7,6},{8,9},{9,8},{10,11... | collective-permute-start | bytes 393224 | tf_op jit(solution)/shard_map/ppermute | solution.py:636
  (52 other events, 359.0 us)
